TPU v7x, 32 devices: a whole 2x2x4 slice. The times are simulated.
32 devices in a mesh: dp: 8 (over y, x, core), tensor: 4 (over z).
Axes of the slice: x: 2, y: 2, z: 4, core: 2. Of those that a mesh axis runs over, the one named last changes fastest.
Arguments:
- tokens: bfloat16 [16, 1568, 1024], P('dp', 'tensor'), may hold values from -6 to 6
- cotangent: bfloat16 [16, 1568, 1024], P('dp', 'tensor'), may hold values from -6 to 6
- clip_live: int32 [16], P('dp'), may hold values from 0 to 1, as said below
- adapter_index: int32 [16], P('dp'), may hold values from 0 to 7
- gain_one: float32 [1024], replicated, may hold values from 0.25 to 1.75
- gain_two: float32 [1024], replicated, may hold values from 0.25 to 1.75
- weight_qkv: bfloat16 [3, 1024, 1024], P(None, 'dp', 'tensor'), may hold values from -0.1875 to 0.1875
- weight_out: bfloat16 [1024, 1024], P('tensor', 'dp'), may hold values from -6 to 6
- weight_fc1: bfloat16 [1024, 4096], P('dp', 'tensor'), may hold values from -0.1875 to 0.1875
- weight_fc2: bfloat16 [4096, 1024], P('tensor', 'dp'), may hold values from -0.09375 to 0.09375
- qkv_down: bfloat16 [8, 16, 1024], replicated, may hold values from -0.1875 to 0.1875
- qkv_up: bfloat16 [8, 3, 16, 1024], replicated, may hold values from -0.75 to 0.75
- out_down: bfloat16 [8, 16, 1024], replicated, may hold values from -6 to 6
- out_up: bfloat16 [8, 16, 1024], replicated, may hold values from -0.75 to 0.75
- fc1_down: bfloat16 [8, 16, 1024], replicated, may hold values from -0.1875 to 0.1875
- fc1_up: bfloat16 [8, 16, 4096], replicated, may hold values from -0.75 to 0.75
- fc2_down: bfloat16 [8, 16, 4096], replicated, may hold values from -0.09375 to 0.09375
- fc2_up: bfloat16 [8, 16, 1024], replicated, may hold values from -0.75 to 0.75
Outputs:
- layer_out: bfloat16 [16, 1568, 1024], P('dp', 'tensor')
- grad_tokens: bfloat16 [16, 1568, 1024], P('dp', 'tensor')
- grad_qkv_down: float32 [8, 16, 1024], replicated
- grad_qkv_up: float32 [8, 3, 16, 1024], replicated
- grad_out_down: float32 [8, 16, 1024], replicated
- grad_out_up: float32 [8, 16, 1024], replicated
- grad_fc1_down: float32 [8, 16, 1024], replicated
- grad_fc1_up: float32 [8, 16, 4096], replicated
- grad_fc2_down: float32 [8, 16, 4096], replicated
- grad_fc2_up: float32 [8, 16, 1024], replicated
Inputs may be any that keep to these rules, and one draw needn't show every extreme that they name: `clip_live`: 1 where the slot holds a clip; the first of the 2 slots of every index of dp always does, index 0 of dp holds 2 clips and index 1 holds one.
All inputs are finite; a program needn't handle non-finite values.
Results may differ from a plain program's by a relative error of at most 0.018.
Values may be sent and summed in bfloat16 or wider, within the bound.
A program may use at most 256 MiB of HBM per device.

v0:
```python
import jax
import jax.numpy as jnp
from jax import lax
from jax.sharding import PartitionSpec as P

HEAD_DIM = 64


highest_precision = lax.Precision.HIGHEST
eps_norm = 1e-06


def block_count(length):
    number = max(1, length // 512)
    while length % number:
        number -= 1
    return number


def normalize(field, gain_vec):
    average = jnp.mean(field, axis=-1, keepdims=True)
    centered = field - average
    variance = jnp.mean(centered * centered, axis=-1, keepdims=True)
    return centered * lax.rsqrt(variance + eps_norm) * gain_vec


def normalize_back(field, gain_vec, incoming):
    unused, pullback = jax.vjp(lambda inner: normalize(inner, gain_vec), field)
    return pullback(incoming)[0]


def widen(piece, start, full, axis_num):
    target = list(piece.shape)
    target[axis_num] = full
    return lax.dynamic_update_slice_in_dim(jnp.zeros(target, jnp.float32), piece, start, axis_num)


def per_device(
    tokens,
    cotangent,
    clip_live,
    adapter_index,
    gain_one,
    gain_two,
    weight_qkv,
    weight_out,
    weight_fc1,
    weight_fc2,
    qkv_down,
    qkv_up,
    out_down,
    out_up,
    fc1_down,
    fc1_up,
    fc2_down,
    fc2_up,
):
    single_float_32 = jnp.float32
    brain_float_16 = jnp.bfloat16
    groups = lax.axis_size("tensor")
    member = lax.axis_index("tensor")
    slot_count, local_rows, width = tokens.shape
    length = local_rows * groups
    head_cols = weight_qkv.shape[2]
    heads_here = head_cols // HEAD_DIM
    hidden_here = weight_fc1.shape[1]
    head_start = member * head_cols
    unit_start = member * hidden_here
    score_scale = HEAD_DIM ** (-0.5)
    blocks_count = block_count(length)
    block_rows = length // blocks_count
    live_mask = clip_live.astype(single_float_32)[:, None, None]
    picker = jax.nn.one_hot(adapter_index, qkv_down.shape[0], dtype=brain_float_16)

    def choose(source):
        return jnp.einsum("se,e...->s...", picker, source, preferred_element_type=single_float_32)

    def to_tables(piece):
        return jnp.einsum(
            "se,s...->e...", picker.astype(single_float_32), piece, precision=highest_precision
        )

    selected_query_key_value_down = choose(qkv_down)
    pick_up_qkv = choose(lax.dynamic_slice_in_dim(qkv_up, head_start, head_cols, 3))
    pick_down_out = choose(lax.dynamic_slice_in_dim(out_down, head_start, head_cols, 2))
    selected_output_up = choose(out_up)
    selected_first_linear_down = choose(fc1_down)
    pick_up_fc1 = choose(lax.dynamic_slice_in_dim(fc1_up, unit_start, hidden_here, 2))
    pick_down_fc2 = choose(lax.dynamic_slice_in_dim(fc2_down, unit_start, hidden_here, 2))
    selected_second_linear_up = choose(fc2_up)
    (
        complete_query_key_value,
        complete_output_projection,
        complete_first_linear,
        complete_second_linear,
    ) = (
        lax.all_gather(weight_qkv, "dp", axis=1, tiled=True),
        lax.all_gather(weight_out, "dp", axis=1, tiled=True),
        lax.all_gather(weight_fc1, "dp", axis=0, tiled=True),
        lax.all_gather(weight_fc2, "dp", axis=1, tiled=True),
    )
    tokens_wide = tokens.astype(single_float_32)
    normed_one = normalize(tokens_wide, gain_one).astype(brain_float_16)
    first_normed_rows = lax.all_gather(normed_one, "tensor", axis=1, tiled=True)
    low_qkv = jnp.einsum(
        "zkw,zmw->zkm",
        first_normed_rows,
        selected_query_key_value_down.astype(brain_float_16),
        preferred_element_type=single_float_32,
    )
    projected_rows = jnp.einsum(
        "woq,fqb->fwob",
        first_normed_rows,
        complete_query_key_value,
        preferred_element_type=single_float_32,
    )
    projected_rows = projected_rows + jnp.einsum(
        "slr,sjrc->jslc", low_qkv, pick_up_qkv, precision=highest_precision
    )
    shaped = projected_rows.astype(brain_float_16).reshape(
        3, slot_count, length, heads_here, HEAD_DIM
    )

    def attend_slot(inputs):
        queries, all_keys, all_values = inputs

        def forward_block(query_block):
            scores = (
                jnp.einsum(
                    "qhc,khc->hqk", query_block, all_keys, preferred_element_type=single_float_32
                )
                * score_scale
            )
            row_max = jnp.max(scores, axis=-1, keepdims=True)
            raised = jnp.exp(scores - row_max)
            row_total = jnp.sum(raised, axis=-1, keepdims=True)
            soft_weights = (raised / row_total).astype(brain_float_16)
            context_block = jnp.einsum(
                "hqk,khc->qhc", soft_weights, all_values, preferred_element_type=single_float_32
            )
            return (context_block, row_max + jnp.log(row_total))

        query_blocks = queries.reshape(blocks_count, block_rows, heads_here, HEAD_DIM)
        return lax.map(forward_block, query_blocks)

    context_blocks, log_totals = lax.map(attend_slot, (shaped[0], shaped[1], shaped[2]))
    attention_context = context_blocks.reshape(slot_count, length, head_cols).astype(brain_float_16)
    lowrank_output = jnp.einsum(
        "slc,src->slr",
        attention_context,
        pick_down_out.astype(brain_float_16),
        preferred_element_type=single_float_32,
    )
    first_partial_term = jnp.einsum(
        "akh,hu->aku",
        attention_context,
        complete_output_projection,
        preferred_element_type=single_float_32,
    )
    first_partial_term = first_partial_term + jnp.einsum(
        "zih,zhw->ziw", lowrank_output, selected_output_up, precision=highest_precision
    )
    attention = lax.psum_scatter(
        first_partial_term.astype(jnp.bfloat16), "tensor", scatter_dimension=1, tiled=True
    ).astype(jnp.float32)
    middle = tokens_wide + attention
    normed_two = normalize(middle, gain_two).astype(brain_float_16)
    second_normed_rows = lax.all_gather(normed_two, "tensor", axis=1, tiled=True)
    low_fc1 = jnp.einsum(
        "zkw,zmw->zkm",
        second_normed_rows,
        selected_first_linear_down.astype(brain_float_16),
        preferred_element_type=single_float_32,
    )
    preactivation = jnp.einsum(
        "wbe,eg->wbg",
        second_normed_rows,
        complete_first_linear,
        preferred_element_type=single_float_32,
    )
    preactivation = preactivation + jnp.einsum(
        "slr,srf->slf", low_fc1, pick_up_fc1, precision=highest_precision
    )
    hidden_state = jax.nn.gelu(preactivation, approximate=False).astype(brain_float_16)
    lowrank_second_linear = jnp.einsum(
        "slf,srf->slr",
        hidden_state,
        pick_down_fc2.astype(brain_float_16),
        preferred_element_type=single_float_32,
    )
    second_partial_term = jnp.einsum(
        "wmv,vo->wmo", hidden_state, complete_second_linear, preferred_element_type=single_float_32
    )
    second_partial_term = second_partial_term + jnp.einsum(
        "zih,zhw->ziw",
        lowrank_second_linear,
        selected_second_linear_up,
        precision=highest_precision,
    )
    feed = lax.psum_scatter(
        second_partial_term.astype(jnp.bfloat16), "tensor", scatter_dimension=1, tiled=True
    ).astype(jnp.float32)
    layer_out = (live_mask * (middle + feed)).astype(brain_float_16)
    (
        complete_query_key_value,
        complete_output_projection,
        complete_first_linear,
        complete_second_linear,
    ) = (
        lax.all_gather(weight_qkv, "dp", axis=1, tiled=True),
        lax.all_gather(weight_out, "dp", axis=1, tiled=True),
        lax.all_gather(weight_fc1, "dp", axis=0, tiled=True),
        lax.all_gather(weight_fc2, "dp", axis=1, tiled=True),
    )
    first_normed_rows, second_normed_rows = (
        lax.all_gather(normed_one, "tensor", axis=1, tiled=True),
        lax.all_gather(normed_two, "tensor", axis=1, tiled=True),
    )
    grad_layer = cotangent.astype(single_float_32) * live_mask
    feedforward_gradient = lax.all_gather(
        grad_layer.astype(brain_float_16), "tensor", axis=1, tiled=True
    )
    back_fc2 = jnp.einsum(
        "zkw,zmw->zkm",
        feedforward_gradient,
        selected_second_linear_up.astype(brain_float_16),
        preferred_element_type=single_float_32,
    )
    hidden_gradient = jnp.einsum(
        "rhg,zg->rhz",
        feedforward_gradient,
        complete_second_linear,
        preferred_element_type=single_float_32,
    )
    hidden_gradient = hidden_gradient + jnp.einsum(
        "slr,srf->slf", back_fc2, pick_down_fc2, precision=highest_precision
    )
    second_linear_up_gradient = jnp.einsum(
        "wfo,wfc->woc", lowrank_second_linear, feedforward_gradient, precision=highest_precision
    )
    grad_down_fc2 = jnp.einsum("slr,slf->srf", back_fc2, hidden_state, precision=highest_precision)
    unused, gelu_back = jax.vjp(lambda inner: jax.nn.gelu(inner, approximate=False), preactivation)
    preactivation_gradient = gelu_back(hidden_gradient)[0].astype(brain_float_16)
    backward_first_linear = jnp.einsum(
        "slf,srf->slr",
        preactivation_gradient,
        pick_up_fc1.astype(brain_float_16),
        preferred_element_type=single_float_32,
    )
    third_partial_term = jnp.einsum(
        "okh,rh->okr",
        preactivation_gradient,
        complete_first_linear,
        preferred_element_type=single_float_32,
    )
    third_partial_term = third_partial_term + jnp.einsum(
        "zih,zhw->ziw",
        backward_first_linear,
        selected_first_linear_down,
        precision=highest_precision,
    )
    grad_up_fc1 = jnp.einsum(
        "slr,slf->srf", low_fc1, preactivation_gradient, precision=highest_precision
    )
    first_linear_down_gradient = jnp.einsum(
        "wfo,wfc->woc", backward_first_linear, second_normed_rows, precision=highest_precision
    )
    grad_normtwo = lax.psum_scatter(
        third_partial_term.astype(jnp.bfloat16), "tensor", scatter_dimension=1, tiled=True
    ).astype(jnp.float32)
    grad_middle = grad_layer + normalize_back(middle, gain_two, grad_normtwo)
    attention_gradient = lax.all_gather(
        grad_middle.astype(brain_float_16), "tensor", axis=1, tiled=True
    )
    back_out = jnp.einsum(
        "zkw,zmw->zkm",
        attention_gradient,
        selected_output_up.astype(brain_float_16),
        preferred_element_type=single_float_32,
    )
    context_gradient = jnp.einsum(
        "urq,jq->urj",
        attention_gradient,
        complete_output_projection,
        preferred_element_type=single_float_32,
    )
    context_gradient = context_gradient + jnp.einsum(
        "slr,src->slc", back_out, pick_down_out, precision=highest_precision
    )
    output_up_gradient = jnp.einsum(
        "wfo,wfc->woc", lowrank_output, attention_gradient, precision=highest_precision
    )
    grad_down_out = jnp.einsum(
        "slr,slc->src", back_out, attention_context, precision=highest_precision
    )
    context_gradient = context_gradient.astype(brain_float_16).reshape(
        slot_count, length, heads_here, HEAD_DIM
    )

    def backward_slot(inputs):
        queries, all_keys, all_values, grad_ctx, log_total = inputs
        query_blocks = queries.reshape(blocks_count, block_rows, heads_here, HEAD_DIM)
        grad_blocks = grad_ctx.reshape(blocks_count, block_rows, heads_here, HEAD_DIM)

        def backward_block(running, block_in):
            grad_keys, grad_values = running
            query_block, grad_block, log_block = block_in
            scores = (
                jnp.einsum(
                    "qhc,khc->hqk", query_block, all_keys, preferred_element_type=single_float_32
                )
                * score_scale
            )
            soft_weights = jnp.exp(scores - log_block)
            grad_values = grad_values + jnp.einsum(
                "hqk,qhc->khc",
                soft_weights.astype(brain_float_16),
                grad_block,
                preferred_element_type=single_float_32,
            )
            grad_soft = jnp.einsum(
                "qhc,khc->hqk", grad_block, all_values, preferred_element_type=single_float_32
            )
            grad_scores = soft_weights * (
                grad_soft - jnp.sum(soft_weights * grad_soft, axis=-1, keepdims=True)
            )
            grad_scores = grad_scores.astype(brain_float_16)
            grad_query = (
                jnp.einsum(
                    "hqk,khc->qhc", grad_scores, all_keys, preferred_element_type=single_float_32
                )
                * score_scale
            )
            grad_keys = (
                grad_keys
                + jnp.einsum(
                    "hqk,qhc->khc", grad_scores, query_block, preferred_element_type=single_float_32
                )
                * score_scale
            )
            return ((grad_keys, grad_values), grad_query)

        zero_grads = jnp.zeros((length, heads_here, HEAD_DIM), single_float_32)
        (grad_keys, grad_values), query_grads = lax.scan(
            backward_block, (zero_grads, zero_grads), (query_blocks, grad_blocks, log_total)
        )
        return (query_grads.reshape(length, heads_here, HEAD_DIM), grad_keys, grad_values)

    grad_query_all, grad_keys_all, grad_values_all = lax.map(
        backward_slot, (shaped[0], shaped[1], shaped[2], context_gradient, log_totals)
    )
    query_key_value_gradient = (
        jnp.stack([grad_query_all, grad_keys_all, grad_values_all])
        .reshape(3, slot_count, length, head_cols)
        .astype(brain_float_16)
    )
    backward_query_key_value = jnp.einsum(
        "jslc,sjrc->slr",
        query_key_value_gradient,
        pick_up_qkv.astype(brain_float_16),
        preferred_element_type=single_float_32,
    )
    fourth_partial_term = jnp.einsum(
        "gvtf,gxf->vtx",
        query_key_value_gradient,
        complete_query_key_value,
        preferred_element_type=single_float_32,
    )
    fourth_partial_term = fourth_partial_term + jnp.einsum(
        "zih,zhw->ziw",
        backward_query_key_value,
        selected_query_key_value_down,
        precision=highest_precision,
    )
    grad_up_qkv = jnp.einsum(
        "slr,jslc->sjrc", low_qkv, query_key_value_gradient, precision=highest_precision
    )
    query_key_value_down_gradient = jnp.einsum(
        "wfo,wfc->woc", backward_query_key_value, first_normed_rows, precision=highest_precision
    )
    grad_normone = lax.psum_scatter(
        fourth_partial_term.astype(jnp.bfloat16), "tensor", scatter_dimension=1, tiled=True
    ).astype(jnp.float32)
    grad_tokens = (grad_middle + normalize_back(tokens_wide, gain_one, grad_normone)).astype(
        brain_float_16
    )
    full_ff = hidden_here * groups
    summed = lax.psum(
        (
            to_tables(query_key_value_down_gradient),
            to_tables(widen(grad_up_qkv, head_start, width, 3)),
            to_tables(widen(grad_down_out, head_start, width, 2)),
            to_tables(output_up_gradient),
            to_tables(first_linear_down_gradient),
            to_tables(widen(grad_up_fc1, unit_start, full_ff, 2)),
            to_tables(widen(grad_down_fc2, unit_start, full_ff, 2)),
            to_tables(second_linear_up_gradient),
        ),
        ("dp", "tensor"),
    )
    results = (
        summed[0],
        summed[1],
        summed[2],
        summed[3],
        summed[4],
        summed[5],
        summed[6],
        summed[7],
    )
    return (
        layer_out,
        grad_tokens,
        results[0],
        results[1],
        results[2],
        results[3],
        results[4],
        results[5],
        results[6],
        results[7],
    )


def solution(mesh):
    placed = (
        P("dp", "tensor", None),
        P("dp", "tensor", None),
        P("dp"),
        P("dp"),
        P(),
        P(),
        P(None, "dp", "tensor"),
        P("tensor", "dp"),
        P("dp", "tensor"),
        P("tensor", "dp"),
        P(),
        P(),
        P(),
        P(),
        P(),
        P(),
        P(),
        P(),
    )
    return jax.shard_map(
        per_device,
        mesh=mesh,
        in_specs=placed,
        out_specs=(
            P("dp", "tensor", None),
            P("dp", "tensor", None),
            P(),
            P(),
            P(),
            P(),
            P(),
            P(),
            P(),
            P(),
        ),
        check_vma=False,
    )
```

profile of v0, /device:TPU:1, one launch (start us, length us, event | category | flops | bytes accessed | tf_op | source)
XLA Modules:
  0.0 1779.6 jit_solution(17534920790291402126)
XLA Ops:
  31.9 102.2 %all-gather.8.cloned.1.call-done = bf16[2,1568,1024]{2,1,0:T(8,128)(2,1)} async-done(((bf16[2,392,1024]{2,1,0:T(8,128)(2,1)}), bf16[2,1568,1024]{2,1,0:T(8,128)(2,1)}) %all-gather.8.cloned.1.call-update) | async-done | bytes 6422544 | tf_op jit(solution)/shard_map/all_gather | solution.py:104
  138.7 21.4 %all-gather.10.cloned.1.call-done = bf16[3,1024,256]{2,1,0:T(8,128)(2,1)} async-done(((bf16[3,128,256]{2,1,0:T(8,128)(2,1)}), bf16[3,1024,256]{2,1,0:T(8,128)(2,1)}) %all-gather.10.cloned.1.call-update) | async-done | bytes 1572880 | tf_op jit(solution)/shard_map/all_gather | solution.py:97
  188.1 105.9 %while.54 = (s32[]{:T(128)}, bf16[2,2,784,4,64]{2,4,3,1,0:T(8,128)(2,1)}, f32[2,2,4,784,1]{3,2,1,4,0:T(4,128)}, bf16[2,1568,4,64]{1,3,2,0:T(8,128)(2,1)}, bf16[2...) while((s32[]{:T(128)}, ...), condition=%wide.region_7.8_spmd, body=%wide.region_2.7_spmd.sunk | while | flops 1303067648 | bytes 154176624 | solution.py:146
  193.0 47.1 %while.57 = (s32[]{:T(128)}, bf16[2,784,4,64]{1,3,2,0:T(8,128)(2,1)S(1)}, f32[2,4,784,1]{2,1,3,0:T(4,128)S(1)}, bf16[2,784,4,64]{1,3,2,0:T(8,128)(2,1)S(1)}, bf1...) while((s32[]{:T(128)}, bf16[2,784,4,64]{1,3,2,0:T(8,128)(2,1)S(1)}, ...), condition=%wide.region_6.6_spmd, body=%wide.region_3.5_spmd.sunk | while | flops 1303067648 | bytes 143969168 | solution.py:144
  245.8 47.1 %while.57 = (s32[]{:T(128)}, bf16[2,784,4,64]{1,3,2,0:T(8,128)(2,1)S(1)}, f32[2,4,784,1]{2,1,3,0:T(4,128)S(1)}, bf16[2,784,4,64]{1,3,2,0:T(8,128)(2,1)S(1)}, bf1...) while((s32[]{:T(128)}, bf16[2,784,4,64]{1,3,2,0:T(8,128)(2,1)S(1)}, ...), condition=%wide.region_6.6_spmd, body=%wide.region_3.5_spmd.sunk | while | flops 1303067648 | bytes 143969168 | solution.py:144
  318.6 39.4 %copy.184 = bf16[2,1568,1024]{2,0,1:T(2,128)(2,1)S(1)} copy(bf16[2,1568,1024]{2,1,0:T(8,128)(2,1)} %add_convert_fusion.3) | data formatting | bytes 12845056
  367.2 108.8 %reduce-scatter.13.cloned.1.call-done = bf16[392,2048]{1,0:T(8,128)(2,1)} async-done(((bf16[1568,2048]{1,0:T(8,128)(2,1)}), bf16[392,2048]{1,0:T(8,128)(2,1)}) %reduce-scatter.13.cloned.1.call-update) | async-done | bytes 1605648
  489.5 106.7 %all-gather.18.cloned.1.call-done = bf16[2,1568,1024]{2,1,0:T(8,128)(2,1)} async-done(((bf16[2,392,1024]{2,1,0:T(8,128)(2,1)}), bf16[2,1568,1024]{2,1,0:T(8,128)(2,1)}) %all-gather.18.cloned.1.call-update) | async-done | bytes 6422544 | tf_op jit(solution)/shard_map/all_gather | solution.py:220
  600.8 23.8 %all-gather.16.cloned.1.call-done = bf16[1024,1024]{1,0:T(8,128)(2,1)} async-done(((bf16[1024,128]{1,0:T(8,128)(2,1)}), bf16[1024,1024]{1,0:T(8,128)(2,1)}) %all-gather.16.cloned.1.call-update) | async-done | bytes 2097168 | tf_op jit(solution)/shard_map/all_gather | solution.py:100
  637.7 106.2 %all-gather.12.cloned.1.call-done = bf16[2,1568,1024]{2,1,0:T(8,128)(2,1)} async-done(((bf16[2,392,1024]{2,1,0:T(8,128)(2,1)}), bf16[2,1568,1024]{2,1,0:T(8,128)(2,1)}) %all-gather.12.cloned.1.call-update) | async-done | bytes 6422544 | tf_op jit(solution)/shard_map/all_gather | solution.py:168
  748.5 23.6 %all-gather.14.cloned.1.call-done = bf16[1024,1024]{1,0:T(8,128)(2,1)} async-done(((bf16[128,1024]{1,0:T(8,128)(2,1)}), bf16[1024,1024]{1,0:T(8,128)(2,1)}) %all-gather.14.cloned.1.call-update) | async-done | bytes 2097168 | tf_op jit(solution)/shard_map/all_gather | solution.py:99
  785.0 20.5 %fusion.54 = (u8[1568,1024]{1,0:T(8,128)(4,1)S(1)}, u8[1568,1024]{1,0:T(8,128)(4,1)S(1)}, f32[2,1568,1024]{2,1,0:T(8,128)}) fusion(f32[2,1568,1024]{2,1,0:T(8,128)} %fusion.64, f32[2,1568,16]{1,2,0:T(8,128)S(1)} %fusion.114, f32[2,16,1024]{2,0,1:T(2,128)S(1)} %get-tuple-element.397), kind=kOutput, calls=%fused_computation.110 | convolution fusion | flops 658309120 | bytes 29233152 | tf_op jit(solution)/shard_map/slr,srf->slf/dot_general | solution.py:181
  805.5 31.7 %multiply_convert_fusion.1 = (bf16[2,1568,1024]{2,1,0:T(8,128)(2,1)}, f32[2,1568,1024]{2,1,0:T(8,128)}) fusion(f32[2,1568,1024]{2,1,0:T(8,128)} %get-tuple-element.393, u8[1568,1024]{1,0:T(8,128)(4,1)S(1)} %get-tuple-element.303, u8[1568,1024]{1,0:T(8,128)(4,1)S(1)} %get-tuple-element.302), kind=kLoop, calls=%fused_computation.65 | loop fusion | flops 224788480 | bytes 35323904 | tf_op jit(solution)/shard_map/convert_element_type | solution.py:184
  837.3 22.0 %add_convert_fusion.1 = bf16[2,1568,1024]{2,1,0:T(8,128)(2,1)} fusion(f32[2,1568,1024]{2,1,0:T(8,128)} %get-tuple-element.373, f32[2,1568,1024]{2,1,0:T(8,128)} %fusion.58, f32[2,1568,1024]{2,1,0:T(8,128)} %get-tuple-element.393, f32[2,1568,16]{1,2,0:T(8,128)S(1)} %fusion.110, f32[2,16,1024]{2,0,1:T(2,128)S(1)} %get-tuple-element.403), kind=kOutput, calls=%fused_computation.63 | convolution fusion | flops 664731648 | bytes 45289472 | tf_op jit(solution)/shard_map/slr,srf->slf/dot_general | solution.py:235
  884.3 13.7 copy.188
  903.4 112.6 %reduce-scatter.17.cloned.1.call-done = bf16[392,2048]{1,0:T(8,128)(2,1)} async-done(((bf16[1568,2048]{1,0:T(8,128)(2,1)}), bf16[392,2048]{1,0:T(8,128)(2,1)}) %reduce-scatter.17.cloned.1.call-update) | async-done | bytes 1605648
  1055.3 46.1 %copy.186 = bf16[2,1568,1024]{2,0,1:T(2,128)(2,1)} copy(bf16[2,1568,1024]{2,1,0:T(8,128)(2,1)S(1)} %add_convert_fusion.2) | data formatting | bytes 12845056
  1129.9 18.0 %all-gather.20.cloned.1.call-done = bf16[2,1568,1024]{2,1,0:T(8,128)(2,1)} async-done(((bf16[2,392,1024]{2,1,0:T(8,128)(2,1)}), bf16[2,1568,1024]{2,1,0:T(8,128)(2,1)}) %all-gather.20.cloned.1.call-update) | async-done | bytes 6422544 | tf_op jit(solution)/shard_map/all_gather | solution.py:272
  1160.0 266.1 %while.56 = (s32[]{:T(128)}, bf16[2,1568,4,64]{3,2,1,0:T(4,128)(2,1)}, bf16[2,1568,4,64]{1,3,2,0:T(8,128)(2,1)}, bf16[2,1568,4,64]{1,3,2,0:T(8,128)(2,1)}, bf16[...) while((s32[]{:T(128)}, ...), condition=%wide.region_19.20_spmd, body=%wide.region_15.19_spmd.sunk | while | flops 3188581376 | bytes 211075568 | solution.py:349
  1168.7 113.8 %while.58 = (s32[]{:T(128)}, f32[1568,4,64]{0,2,1:T(8,128)}, f32[1568,4,64]{0,2,1:T(8,128)}, bf16[2,784,4,64]{1,3,2,0:T(8,128)(2,1)}, bf16[2,784,4,64]{1,3,2,0:T...) while((s32[]{:T(128)}, f32[1568,4,64]{0,2,1:T(8,128)}, ...), condition=%wide.region_18.18_spmd.clone, body=%wide.region_16.17_spmd.clone.sunk | while | flops 3188581376 | bytes 161053840 | solution.py:344
  1180.1 13.8 multiply_reduce_fusion.6
  1193.9 13.8 multiply_convert_fusion.5
  1236.0 13.7 multiply_reduce_fusion.6
  1249.7 13.9 multiply_convert_fusion.5
  1301.8 113.3 %while.58 = (s32[]{:T(128)}, f32[1568,4,64]{0,2,1:T(8,128)}, f32[1568,4,64]{0,2,1:T(8,128)}, bf16[2,784,4,64]{1,3,2,0:T(8,128)(2,1)}, bf16[2,784,4,64]{1,3,2,0:T...) while((s32[]{:T(128)}, f32[1568,4,64]{0,2,1:T(8,128)}, ...), condition=%wide.region_18.18_spmd.clone, body=%wide.region_16.17_spmd.clone.sunk | while | flops 3188581376 | bytes 161053840 | solution.py:344
  1313.1 13.7 multiply_reduce_fusion.6
  1326.8 13.7 multiply_convert_fusion.5
  1368.8 13.7 multiply_reduce_fusion.6
  1382.5 13.7 multiply_convert_fusion.5
  1480.6 13.7 copy.190
  1505.4 135.8 %all-reduce.3.cloned.1.call-done = (f32[8,16,1024]{2,0,1:T(8,128)}, f32[8,3,16,1024]{3,0,2,1:T(8,128)}, f32[8,16,1024]{2,0,1:T(8,128)}, f32[8,16,1024]{2,0,1:T(8...) async-done(((f32[8,16,1024]{2,0,1:T(8,128)}, f32[8,3,16,1024]{3,0,2,1:T(8,128)}, ...) | async-done | bytes 8388624 | tf_op jit(solution)/shard_map/psum | solution.py:388
  1657.2 99.1 %reduce-scatter.19.cloned.1.call-done = bf16[392,2048]{1,0:T(8,128)(2,1)} async-done(((bf16[1568,2048]{1,0:T(8,128)(2,1)}), bf16[392,2048]{1,0:T(8,128)(2,1)}) %reduce-scatter.19.cloned.1.call-update) | async-done | bytes 1605648
  (431 shorter events, 607.5 us)
Async XLA Ops:
  7.2 21.0 %copy-start = (bf16[8,3,16,1024]{3,2,1,0:T(8,128)(2,1)S(1)}, bf16[8,3,16,1024]{3,2,1,0:T(8,128)(2,1)}, u32[]{:S(2)}) copy-start(bf16[8,3,16,1024]{3,2,1,0:T(8,128)(2,1)} %param.37) | copy-start | bytes 2359300
  7.2 126.9 %all-gather.8.cloned.1.call-start = ((), (), s32[]{:S(2)}) async-start(), calls=%async_computation.4 | async-start | bytes 8028160 | tf_op jit(solution)/shard_map/all_gather | solution.py:104
  11.8 16.5 copy-start.55
  12.4 17.6 copy-start.46
  12.4 18.5 %copy-start.47 = (bf16[8,16,1024]{2,1,0:T(8,128)(2,1)S(1)}, bf16[8,16,1024]{2,1,0:T(8,128)(2,1)}, u32[]{:S(2)}) copy-start(bf16[8,16,1024]{2,1,0:T(8,128)(2,1)} %param.39) | copy-start | bytes 786436
  14.1 146.0 %all-gather.10.cloned.1.call-start = ((), (), s32[]{:S(2)}) async-start(), calls=%async_computation.5 | async-start | bytes 1769472 | tf_op jit(solution)/shard_map/all_gather | solution.py:97
  14.9 461.1 %reduce-scatter.13.cloned.1.call-start = ((), (), s32[]{:S(2)}) async-start(), calls=%async_computation.11 | async-start | bytes 8028160
  138.7 29.3 %copy-start.37 = (f32[2,1568,16,1]{1,2,3,0:T(8,128)}, f32[2,1568,16,1]{1,2,3,0:T(8,128)S(1)}, u32[]{:S(2)}) copy-start(f32[2,1568,16,1]{1,2,3,0:T(8,128)S(1)} %convolution_bitcast_fusion) | copy-start | bytes 602116
  192.9 47.1 %copy-start.43 = (f32[2,2,4,784,1]{3,2,1,4,0:T(4,128)S(1)}, f32[2,2,4,784,1]{3,2,1,4,0:T(4,128)}, u32[]{:S(2)}) copy-start(f32[2,2,4,784,1]{3,2,1,4,0:T(4,128)} %get-tuple-element.713) | copy-start | bytes 150532 | tf_op jit(solution)/shard_map/while
  245.8 47.1 %copy-start.43 = (f32[2,2,4,784,1]{3,2,1,4,0:T(4,128)S(1)}, f32[2,2,4,784,1]{3,2,1,4,0:T(4,128)}, u32[]{:S(2)}) copy-start(f32[2,2,4,784,1]{3,2,1,4,0:T(4,128)} %get-tuple-element.713) | copy-start | bytes 150532 | tf_op jit(solution)/shard_map/while
  363.4 232.9 %all-gather.18.cloned.1.call-start = ((), (), s32[]{:S(2)}) async-start(), calls=%async_computation.9 | async-start | bytes 8028160 | tf_op jit(solution)/shard_map/all_gather | solution.py:220
  364.8 661.9 %copy-start.75 = (f32[2]{0:T(128)}, f32[2]{0:T(128)S(1)}, u32[]{:S(2)}) copy-start(f32[2]{0:T(128)S(1)} %convert_element_type.113) | copy-start | bytes 28
  366.5 114.8 %copy-start.5 = (bf16[2,392,1024]{2,1,0:T(8,128)(2,1)S(1)}, bf16[2,392,1024]{2,1,0:T(8,128)(2,1)}, u32[]{:S(2)}) copy-start(bf16[2,392,1024]{2,1,0:T(8,128)(2,1)} %param.26) | copy-start | bytes 4816900
  366.6 258.0 %all-gather.16.cloned.1.call-start = ((), (), s32[]{:S(2)}) async-start(), calls=%async_computation.8 | async-start | bytes 2359296 | tf_op jit(solution)/shard_map/all_gather | solution.py:100
  367.1 376.8 %all-gather.12.cloned.1.call-start = ((), (), s32[]{:S(2)}) async-start(), calls=%async_computation.6 | async-start | bytes 8028160 | tf_op jit(solution)/shard_map/all_gather | solution.py:168
  483.5 543.2 %copy-start.50 = (f32[2,392]{1,0:T(2,128)}, f32[2,392]{1,0:T(2,128)S(1)}, u32[]{:S(2)}) copy-start(f32[2,392]{1,0:T(2,128)S(1)} %broadcast_multiply_fusion) | copy-start | bytes 9412
  484.3 542.4 %copy-start.58 = (f32[2,392]{1,0:T(2,128)}, f32[2,392]{1,0:T(2,128)S(1)}, u32[]{:S(2)}) copy-start(f32[2,392]{1,0:T(2,128)S(1)} %fusion.122) | copy-start | bytes 9412
  486.2 286.0 %all-gather.14.cloned.1.call-start = ((), (), s32[]{:S(2)}) async-start(), calls=%async_computation.7 | async-start | bytes 2359296 | tf_op jit(solution)/shard_map/all_gather | solution.py:99
  486.9 529.1 %reduce-scatter.17.cloned.1.call-start = ((), (), s32[]{:S(2)}) async-start(), calls=%async_computation.13 | async-start | bytes 8028160
  903.4 244.6 %all-gather.20.cloned.1.call-start = ((), (), s32[]{:S(2)}) async-start(), calls=%async_computation.10 | async-start | bytes 8028160 | tf_op jit(solution)/shard_map/all_gather | solution.py:272
  1029.6 470.3 %reduce-scatter.15.cloned.1.call-start = ((), (), s32[]{:S(2)}) async-start(), calls=%async_computation.12 | async-start | bytes 8028160
  1055.3 54.5 %slice-start = ((s8[6422528]{0:T(1024)(128)(4,1)}), s8[4194304]{0:T(1024)(128)(4,1)S(1)}, s32[]{:S(2)}) async-start(s8[6422528]{0:T(1024)(128)(4,1)} %bitcast.304), calls=%async_computation.16 | async-start | bytes 8388608
  1055.3 57.5 %slice-start.10 = ((s8[6422528]{0:T(1024)(128)(4,1)}), s8[4194304]{0:T(1024)(128)(4,1)S(1)}, s32[]{:S(2)}) async-start(s8[6422528]{0:T(1024)(128)(4,1)} %bitcast.319), calls=%async_computation.26 | async-start | bytes 8388608
  1129.8 18.1 %copy-start.27 = (bf16[256,1024]{1,0:T(8,128)(2,1)S(1)}, bf16[256,1024]{1,0:T(8,128)(2,1)}, u32[]{:S(2)}) copy-start(bf16[256,1024]{1,0:T(8,128)(2,1)} %all_gather.32) | copy-start | bytes 1572868
  1129.9 23.0 %copy-start.45 = (bf16[2,16,1024]{2,0,1:T(2,128)(2,1)S(1)}, bf16[2,16,1024]{2,0,1:T(2,128)(2,1)}, u32[]{:S(2)}) copy-start(bf16[2,16,1024]{2,0,1:T(2,128)(2,1)} %get-tuple-element.398) | copy-start | bytes 196612
  1129.9 511.2 %all-reduce.3.cloned.1.call-start = ((), (), s32[]{:S(2)}) async-start(), calls=%async_computation.15 | async-start | bytes 16777216 | tf_op jit(solution)/shard_map/psum | solution.py:388
  1461.3 295.0 %reduce-scatter.19.cloned.1.call-start = ((), (), s32[]{:S(2)}) async-start(), calls=%async_computation.14 | async-start | bytes 8028160
  1654.7 107.0 %copy-start.6 = (bf16[2,392,1024]{2,1,0:T(8,128)(2,1)S(1)}, bf16[2,392,1024]{2,1,0:T(8,128)(2,1)}, u32[]{:S(2)}) copy-start(bf16[2,392,1024]{2,1,0:T(8,128)(2,1)} %param.26) | copy-start | bytes 4816900
  1654.7 107.0 %copy-start.53 = (f32[2,392]{1,0:T(2,128)S(1)}, f32[2,392]{1,0:T(2,128)}, u32[]{:S(2)}) copy-start(f32[2,392]{1,0:T(2,128)} %copy-done.52) | copy-start | bytes 9412
  1654.7 107.0 %copy-start.63 = (f32[1024]{0:T(1024)S(1)}, f32[1024]{0:T(1024)}, u32[]{:S(2)}) copy-start(f32[1024]{0:T(1024)} %param.30) | copy-start | bytes 12292
  1657.2 107.0 %copy-start.74 = (f32[2,392]{1,0:T(2,128)S(1)}, f32[2,392]{1,0:T(2,128)}, u32[]{:S(2)}) copy-start(f32[2,392]{1,0:T(2,128)} %copy-done.73) | copy-start | bytes 9412
  1657.2 107.0 %copy-start.65 = (f32[2,392]{1,0:T(2,128)S(1)}, f32[2,392]{1,0:T(2,128)}, u32[]{:S(2)}) copy-start(f32[2,392]{1,0:T(2,128)} %copy-done.64) | copy-start | bytes 9412
  (83 other events, 401.2 us)
Sparse Core Ops, SparseCore 0:
  14.3 119.7 all-gather.7
  136.0 24.0 all-gather.9
  363.5 112.4 reduce-scatter.12
  478.0 118.1 all-gather.17
  598.0 26.5 all-gather.15
  626.6 117.2 all-gather.11
  745.8 26.2 all-gather.13
  903.5 112.4 reduce-scatter.16
  1029.7 118.1 all-gather.19
  1150.1 110.8 reduce-scatter.14
  1461.4 179.6 all-reduce.2
  1643.3 112.9 reduce-scatter.18
where the time goes:
time: 1790 us; the launch traced here: 1780 us
  waiting for transfers between devices  860 us (48%)
  matrix products  458 us (26%)
  local copies, waits for them, and re-layouts  298 us (17%)
  other arithmetic  134 us (7%)
    unnamed x16, waiting for transfers between devices  323 us
    unnamed x186, local copies, waits for them, and re-layouts  178 us
    psum x1, waiting for transfers between devices, per_device(): lax.psum((to_tables(query_key_value_down_gradient), to_tables(widen(grad_...  136 us
    all_gather x1, waiting for transfers between devices, per_device(): lax.all_gather(grad_layer.astype(brain_float_16), 'tensor', axis=1, tiled...  107 us
    all_gather x1, waiting for transfers between devices, per_device(): lax.all_gather(normed_two, 'tensor', axis=1, tiled=True)  106 us
    all_gather x1, waiting for transfers between devices, per_device(): first_normed_rows = lax.all_gather(normed_one, 'tensor', axis=1, tiled=True)  102 us
    convert_element_type x4, other arithmetic, backward_block(): grad_scores = grad_scores.astype(brain_float_16)  55.1 us
    dot_general x4, matrix products, backward_block(): jnp.einsum('qhc,khc->hqk', query_block, all_keys, preferred_element_type=...  54.9 us
  transfers between devices with their start and end apart: 12, of which 11 were waited for; matrix products, arithmetic and copies ran while one was open for 29% of the time, Pallas kernels for 0%

commit v1 on v0

v1 whole, which is shorter than its diff:
```python
import functools
import math

import jax
import jax.numpy as jnp
from jax import lax
from jax.experimental import pallas as pl
from jax.experimental.pallas import tpu as pltpu
from jax.sharding import PartitionSpec as P

HEAD_DIM = 64
EPS = 1e-06
F32 = jnp.float32
BF16 = jnp.bfloat16
NT = (((1,), (1,)), ((), ()))
TN = (((0,), (0,)), ((), ()))
VMEM_BYTES = 58 << 20
SAFE_SCORE = 60.0


def mm(a, b):
    return jnp.dot(a, b, preferred_element_type=F32)


def mm_nt(a, b):
    return lax.dot_general(a, b, NT, preferred_element_type=F32)


def mm_tn(a, b):
    return lax.dot_general(a, b, TN, preferred_element_type=F32)


def norm_parts(field):
    centered = field - jnp.mean(field, axis=-1, keepdims=True)
    scale = lax.rsqrt(jnp.mean(centered * centered, axis=-1, keepdims=True) + EPS)
    return centered * scale, scale


def norm_back(normed, scale, gain, incoming):
    weighted = incoming * gain
    return scale * (
        weighted
        - jnp.mean(weighted, axis=-1, keepdims=True)
        - normed * jnp.mean(weighted * normed, axis=-1, keepdims=True)
    )


def params(*semantics):
    return pltpu.CompilerParams(vmem_limit_bytes=VMEM_BYTES)


class Plan:
    def __init__(self, dps, tens):
        self.tens = tens
        bits = [1 << i for i in range(1, dps.bit_length() - 1)]
        self.orders = (bits + [1], bits[::-1] + [1])
        self.hops = dps - 1
        self.ways = []
        for order in self.orders:
            blocks = [0]
            for bit in order:
                blocks = blocks + [r | bit for r in blocks]
            tops = {r: max([j for j, bit in enumerate(order) if r & bit], default=-1) for r in blocks}
            sends = {r: range(tops[r] + 1, len(order)) for r in blocks}
            ids = {}
            for r in blocks:
                for j in sends[r]:
                    ids[(r, j)] = len(ids)
            blocks.sort(key=lambda r: bin(r).count("1"))
            self.ways.append((order, blocks, tops, sends, ids))

    def semaphores(self, items):
        dma = lambda *shape: pltpu.SemaphoreType.DMA(shape)
        near = self.tens - 1
        return [dma(items), dma(items, near), dma(items, near), dma(items, self.hops), dma(items, self.hops)]

    def greet(self):
        me, t = lax.axis_index("dp"), lax.axis_index("tensor")
        peers = [(me, lax.rem(t + k, self.tens)) for k in range(1, self.tens)]
        peers += [(me ^ bit, t) for bit in self.orders[0]]
        barrier = pltpu.get_barrier_semaphore()
        for peer in peers:
            pl.semaphore_signal(barrier, inc=1, device_id=peer, device_id_type=pl.DeviceIdType.MESH)
        pl.semaphore_wait(barrier, len(peers))


class Item:
    def __init__(self, plan, sems, number, src, spot, order):
        self.plan, self.src, self.spot = plan, src, spot
        self.local, self.zs, self.zr, self.ss, self.rs = [s.at[number] for s in sems]
        self.order, self.blocks, self.tops, self.sends, self.ids = plan.ways[order]
        self.me, self.t = lax.axis_index("dp"), lax.axis_index("tensor")
        self.stages = [r for r in self.blocks if len(self.sends[r])]

    def keep(self):
        return pltpu.make_async_copy(self.src, self.spot(self.me, self.t), self.local)

    def along(self, d, arriving=False):
        n = self.plan.tens
        return pltpu.make_async_remote_copy(
            src_ref=self.src,
            dst_ref=self.spot(self.me, lax.rem(self.t + n - d, n) if arriving else self.t),
            send_sem=self.zs.at[d - 1],
            recv_sem=self.zr.at[d - 1],
            device_id=(self.me, lax.rem(self.t + d, n)),
            device_id_type=pl.DeviceIdType.MESH,
        )

    def across(self, r, j, arriving=False):
        bit, n = self.order[j], self.ids[(r, j)]
        block = self.me ^ r
        return pltpu.make_async_remote_copy(
            src_ref=self.spot(block, None),
            dst_ref=self.spot(block ^ bit if arriving else block, None),
            send_sem=self.ss.at[n],
            recv_sem=self.rs.at[n],
            device_id=(self.me ^ bit, self.t),
            device_id_type=pl.DeviceIdType.MESH,
        )

    def start(self):
        self.keep().start()
        for d in range(1, self.plan.tens):
            self.along(d).start()

    def arrived(self, r):
        if r == 0:
            self.keep().wait()
            for d in range(1, self.plan.tens):
                self.along(d, True).wait_recv()
        else:
            j = self.tops[r]
            self.across(r ^ self.order[j], j, True).wait_recv()

    def advance(self, stage):
        r = self.stages[stage]
        self.arrived(r)
        for j in self.sends[r]:
            self.across(r, j).start()

    def finish(self):
        for r in self.blocks:
            if not len(self.sends[r]):
                self.arrived(r)
        for d in range(1, self.plan.tens):
            self.along(d).wait_send()
        for r in self.blocks:
            for j in self.sends[r]:
                self.across(r, j).wait_send()


def schedule(items):
    pairs = [items[k : k + 2] for k in range(0, len(items), 2)]
    stages = len(items[0].stages)
    steps = []
    for s in range(len(pairs) + stages):
        def step(s=s):
            for item in (pairs[:2] if s == 0 else pairs[s + 1 : s + 2]):
                for one in item:
                    one.start()
            for n, pair in enumerate(pairs):
                if 0 <= s - n < stages:
                    for one in pair:
                        one.advance(s - n)
        steps.append(step)
    def close():
        for item in items:
            item.finish()
    return steps + [close]


def at(ref, cut):
    return lambda a, t: ref.at[a, :, cut] if t is None else ref.at[a, t, cut]


def gather_kernel(plan, cuts, x_ref, o_ref, *sems):
    plan.greet()
    size = x_ref.shape[0] // cuts
    items = []
    for k in range(cuts):
        cut = pl.ds(k * size, size)
        items.append(Item(plan, sems, k, x_ref.at[cut], at(o_ref, cut), k % 2))
    for step in schedule(items):
        step()


def gather(plan, dps, x, cuts, number):
    return pl.pallas_call(
        functools.partial(gather_kernel, plan, cuts),
        in_specs=[pl.BlockSpec(memory_space=pl.ANY)],
        out_specs=pl.BlockSpec(memory_space=pl.ANY),
        out_shape=jax.ShapeDtypeStruct((dps, plan.tens) + x.shape, x.dtype),
        scratch_shapes=plan.semaphores(cuts),
        compiler_params=pltpu.CompilerParams(collective_id=number, has_side_effects=True),
        name="gather",
    )(x)


def share_kernel(plan, x_ref, o_ref, got, src, swap_send, swap_recv, *sems):
    plan.greet()
    me, t = lax.axis_index("dp"), lax.axis_index("tensor")
    mine = lax.rem(me, 2)
    swap = pltpu.make_async_remote_copy(
        src_ref=x_ref.at[1 - mine], dst_ref=got, send_sem=swap_send, recv_sem=swap_recv,
        device_id=(me ^ 1, t), device_id_type=pl.DeviceIdType.MESH,
    )
    swap.start()
    swap.wait()
    src[...] = (x_ref[mine].astype(F32) + got[...].astype(F32)).astype(BF16)
    cuts = src.shape[0]
    items = [Item(plan, sems, k, src.at[pl.ds(k, 1)], at(o_ref, pl.ds(k, 1)), k % 2) for k in range(cuts)]
    for step in schedule(items):
        step()


def share(plan, dps, pieces, cuts, number):
    flat = jnp.concatenate(pieces, axis=-1).astype(BF16)
    rank, cols = flat.shape
    cols = cols // (2 * cuts)
    flat = flat.reshape(rank, 2, cuts, cols).transpose(1, 2, 0, 3)
    return pl.pallas_call(
        functools.partial(share_kernel, plan),
        in_specs=[pl.BlockSpec(memory_space=pltpu.VMEM)],
        out_specs=pl.BlockSpec(memory_space=pl.ANY),
        out_shape=jax.ShapeDtypeStruct((dps, plan.tens, cuts, rank, cols), BF16),
        scratch_shapes=[pltpu.VMEM((cuts, rank, cols), BF16), pltpu.VMEM((cuts, rank, cols), BF16),
                        pltpu.SemaphoreType.DMA, pltpu.SemaphoreType.DMA] + plan.semaphores(cuts),
        compiler_params=pltpu.CompilerParams(collective_id=number, has_side_effects=True),
        name="share",
    )(flat)


def qkv_kernel(info, xa_ref, xb_ref, gain_ref, w_ref, down_ref, up_ref, q_ref, kv_ref, low_ref, n_s, low_s):
    half = xa_ref.shape[0]
    parts, width = w_ref.shape[1], w_ref.shape[4]
    depth = n_s.shape[1]
    step = pl.program_id(0)

    @pl.when(step == 0)
    def _():
        for part, ref in enumerate((xa_ref, xb_ref)):
            normed, _ = norm_parts(ref[...].astype(F32))
            n_s[part * half : (part + 1) * half, :] = normed * gain_ref[...]

    n = n_s[...].astype(BF16)

    @pl.when(step == 0)
    def _():
        low = mm_nt(n, down_ref[0])
        low_ref[...] = low
        low_s[...] = low

    low = low_s[...].astype(BF16)
    for part in range(parts):
        cols = slice(part * width, (part + 1) * width)
        res = mm(n, w_ref[:, part, 0].reshape(depth, width)) + mm(low, up_ref[0, 0, :, cols])
        res = res.astype(BF16)

        @pl.when(step == 0)
        def _():
            q_ref[:, cols] = res

        @pl.when(step > 0)
        def _():
            kv_ref[0, :, cols] = res


def project(info, xa, xb, gain, w, down, up):
    half, depth = xa.shape
    rows = 2 * half
    rank = down.shape[1]
    dp, tens, _, wr, wc = w.shape
    whole = lambda *shape: pl.BlockSpec(shape, lambda j, info: (0,) * len(shape))
    return pl.pallas_call(
        qkv_kernel,
        grid_spec=pltpu.PrefetchScalarGridSpec(
            num_scalar_prefetch=1,
            grid=(3,),
            in_specs=[
                whole(half, depth),
                whole(half, depth),
                whole(1, depth),
                pl.BlockSpec((dp, tens, 1, wr, wc), lambda j, info: (0, 0, j, 0, 0)),
                pl.BlockSpec((1, rank, depth), lambda j, info: (info[0], 0, 0)),
                pl.BlockSpec((1, 1, rank, depth), lambda j, info: (info[0], j, 0, 0)),
            ],
            out_specs=[
                whole(rows, depth),
                pl.BlockSpec((1, rows, depth), lambda j, info: (jnp.maximum(j - 1, 0), 0, 0)),
                whole(rows, rank),
            ],
            scratch_shapes=[pltpu.VMEM((rows, depth), F32), pltpu.VMEM((rows, rank), F32)],
        ),
        out_shape=[
            jax.ShapeDtypeStruct((rows, depth), BF16),
            jax.ShapeDtypeStruct((2, rows, depth), BF16),
            jax.ShapeDtypeStruct((rows, rank), F32),
        ],
        compiler_params=params(),
        name="project",
    )(info, xa, xb, gain, w, down, up)


def attend_pair(q2, ks, vs, shifted):
    lane = lax.broadcasted_iota(jnp.int32, (1, 128), 1)
    outs, lses = [], []
    for h in range(2):
        mine = (lane // HEAD_DIM) == h
        s = mm_nt(jnp.where(mine, q2, BF16(0)), ks[...])
        if shifted:
            m = jnp.max(s, axis=1, keepdims=True)
            p = jnp.exp(s - m).astype(BF16)
        else:
            p = jnp.exp(s).astype(BF16)
        o = mm(p, vs[h])
        total = pltpu.roll(o, HEAD_DIM, 1)
        outs.append(o / total)
        lse = jnp.log(jnp.where(mine, total, o))
        lses.append(lse + m if shifted else lse)
    return (
        jnp.where(lane < HEAD_DIM, outs[0], outs[1]).astype(BF16),
        jnp.where(lane < HEAD_DIM, lses[0], lses[1]),
    )


def stage_keys(k_ref, v_ref, k2_ref, v2_ref, ks, vs):
    rows = k_ref.shape[1]
    lane = lax.broadcasted_iota(jnp.int32, (1, 128), 1)
    ks[0:rows, :] = k_ref[0]
    ks[rows:, :] = k2_ref[0]
    for h in range(2):
        mine = (lane // HEAD_DIM) == h
        vs[h, 0:rows, :] = jnp.where(mine, v_ref[0], BF16(1))
        vs[h, rows:, :] = jnp.where(mine, v2_ref[0], BF16(1))


def attend_exact_kernel(q_ref, k_ref, v_ref, k2_ref, v2_ref, o_ref, lse_ref, ks, vs):
    stage_keys(k_ref, v_ref, k2_ref, v2_ref, ks, vs)
    o_ref[...], lse_ref[...] = attend_pair(q_ref[...] * BF16(HEAD_DIM ** -0.5), ks, vs, True)


def attend_specs(rows):
    flat = pl.BlockSpec((rows, 128), lambda i: (0, i))
    part = lambda j: pl.BlockSpec((1, rows, 128), lambda i: (j, 0, i))
    return flat, [flat, part(0), part(1), part(0), part(1)]


def attend_exact(q, kv, kv2):
    rows, depth = q.shape
    flat, blocks = attend_specs(rows)
    return pl.pallas_call(
        attend_exact_kernel,
        grid=(depth // 128,),
        in_specs=blocks,
        out_specs=[flat, flat],
        out_shape=[jax.ShapeDtypeStruct((rows, depth), BF16), jax.ShapeDtypeStruct((rows, depth), F32)],
        scratch_shapes=[pltpu.VMEM((2 * rows, 128), BF16), pltpu.VMEM((2, 2 * rows, 128), BF16)],
        compiler_params=params(),
        name="attend_exact",
    )(q, kv, kv, kv2, kv2)


def attend_gather_kernel(
    plan, cuts, heads_of, q_ref, k_ref, v_ref, k2_ref, v2_ref, wo_ref, w1_ref, w2_ref,
    o_ref, lse_ref, reach_ref, go_ref, g1_ref, g2_ref, ks, vs, *sems
):
    step, last = pl.program_id(0), pl.num_programs(0) - 1
    items = []
    for ref, out in ((wo_ref, go_ref), (w1_ref, g1_ref), (w2_ref, g2_ref)):
        n = 2 if ref is wo_ref else cuts
        size = ref.shape[0] // n
        for k in range(n):
            cut = pl.ds(k * size, size)
            items.append((ref.at[cut], at(out, cut)))
    items = items[:2] + [one for k in range(cuts) for one in (items[2 + k], items[2 + cuts + k])]
    items = [Item(plan, sems, n, src, spot, n % 2) for n, (src, spot) in enumerate(items)]
    steps = schedule(items)
    steps = [lambda first=steps[0]: (plan.greet(), first())] + steps[1:]
    heads = heads_of
    for n in range(heads):
        @pl.when(step == n)
        def _():
            if n < len(steps):
                steps[n]()

    stage_keys(k_ref, v_ref, k2_ref, v2_ref, ks, vs)
    q2 = q_ref[...] * BF16(HEAD_DIM ** -0.5)
    lane = lax.broadcasted_iota(jnp.int32, (1, 128), 1)
    reach = jnp.zeros((), F32)
    qf, kf = q2.astype(F32), ks[...].astype(F32)
    for h in range(2):
        mine = (lane // HEAD_DIM) == h
        far = lambda x: jnp.max(jnp.sum(jnp.where(mine, x * x, 0.0), axis=1, keepdims=True), axis=0, keepdims=True)
        reach = jnp.maximum(reach, far(qf) * far(kf))
    reach_ref[...] = jnp.broadcast_to(reach, reach_ref.shape)
    o_ref[...], lse_ref[...] = attend_pair(q2, ks, vs, False)

    @pl.when(step == last)
    def _():
        for one in steps[heads:]:
            one()


def attend_gather(plan, dps, q, kv, kv2, wo, w1, w2, cuts, number):
    rows, depth = q.shape
    flat, blocks = attend_specs(rows)
    hbm = pl.BlockSpec(memory_space=pl.ANY)
    big = lambda w: jax.ShapeDtypeStruct((dps, plan.tens) + w.shape, w.dtype)
    grid = depth // 128
    kernel = functools.partial(attend_gather_kernel, plan, cuts, grid)
    ctx, lse, reach, go, g1, g2 = pl.pallas_call(
        kernel,
        grid=(grid,),
        in_specs=blocks + [hbm] * 3,
        out_specs=[flat, flat, pl.BlockSpec((1, 8, 128), lambda i: (i, 0, 0)), hbm, hbm, hbm],
        out_shape=[jax.ShapeDtypeStruct((rows, depth), BF16), jax.ShapeDtypeStruct((rows, depth), F32),
                   jax.ShapeDtypeStruct((grid, 8, 128), F32), big(wo), big(w1), big(w2)],
        scratch_shapes=[pltpu.VMEM((2 * rows, 128), BF16), pltpu.VMEM((2, 2 * rows, 128), BF16)]
        + plan.semaphores(2 + 2 * cuts),
        compiler_params=pltpu.CompilerParams(
            vmem_limit_bytes=VMEM_BYTES, collective_id=number, has_side_effects=True
        ),
        name="attend_gather",
    )(q, kv, kv, kv2, kv2, wo, w1, w2)
    safe = jnp.max(reach) <= SAFE_SCORE * SAFE_SCORE
    ctx, lse = lax.cond(safe, lambda: (ctx, lse), lambda: tuple(attend_exact(q, kv, kv2)))
    return ctx, lse, go, g1, g2


def gelu_both(x):
    cdf = 0.5 * (1.0 + lax.erf(x * (2.0 ** -0.5)))
    pdf = jnp.exp(-0.5 * x * x) * ((2.0 * math.pi) ** -0.5)
    return x * cdf, cdf + x * pdf


def feed_kernel(
    info, xa_ref, xb_ref, ca_ref, cb_ref, ctx_ref, gain_ref, wo_ref, w1_ref, w2_ref,
    od_ref, ou_ref, d1_ref, u1_ref, d2_ref, u2_ref,
    la_ref, lb_ref, gm_ref, gctx_ref, g_od, g_ou, g_d1, g_u1, g_d2, g_u2,
    wo_s, w1_s, w2_s, mid_s, n_s, gf_s, feed_s, gn_s, lowo_s, low1_s, low2_s, b1_s, b2_s,
):
    half, depth = xa_ref.shape
    rows = 2 * half
    step, last = pl.program_id(0), pl.num_programs(0) - 1
    live = info[1].astype(F32)
    dp, tens, wop, wor, woc = wo_ref.shape
    fp, fr, fc = w1_ref.shape[2:]

    @pl.when(step == 0)
    def _():
        for a in range(dp):
            for t in range(tens):
                for k in range(wop):
                    row = (t * wop + k) * wor
                    wo_s[row : row + wor, a * woc : (a + 1) * woc] = wo_ref[a, t, k]
        ctx = ctx_ref[...]
        low = mm_nt(ctx, od_ref[0])
        lowo_s[...] = low
        attention = mm(ctx, wo_s[...]) + mm(low.astype(BF16), ou_ref[0])
        for part, ref in enumerate((xa_ref, xb_ref)):
            s = slice(part * half, (part + 1) * half)
            mid_s[s, :] = ref[...].astype(F32) + attention[s, :]
        for part, ref in enumerate((ca_ref, cb_ref)):
            s = slice(part * half, (part + 1) * half)
            gm_ref[s, :] = ref[...].astype(F32) * live
        gf_s[...] = gm_ref[...].astype(BF16)
        normed, _ = norm_parts(mid_s[...])
        n_s[...] = (normed * gain_ref[...]).astype(BF16)
        low1_s[...] = mm_nt(n_s[...], d1_ref[0])
        b2_s[...] = mm_nt(gf_s[...], u2_ref[0])
        feed_s[...] = jnp.zeros_like(feed_s)
        gn_s[...] = jnp.zeros_like(gn_s)
        low2_s[...] = jnp.zeros_like(low2_s)
        b1_s[...] = jnp.zeros_like(b1_s)

    for a in range(dp):
        for k in range(fp):
            w1_s[a * fr : (a + 1) * fr, k * fc : (k + 1) * fc] = w1_ref[a, 0, k]
        w2_s[:, a * woc : (a + 1) * woc] = w2_ref[a, 0].reshape(w2_s.shape[0], woc)
    w1, w2 = w1_s[...], w2_s[...]
    u1, d2 = u1_ref[0], d2_ref[0]
    n, gf = n_s[...], gf_s[...]
    low1, b2 = low1_s[...].astype(BF16), b2_s[...].astype(BF16)
    preact = mm(n, w1) + mm(low1, u1)
    ghid = mm_nt(gf, w2) + mm(b2, d2)
    hid, slope = gelu_both(preact)
    hid = hid.astype(BF16)
    gpre = (ghid * slope).astype(BF16)
    feed_s[...] += mm(hid, w2)
    gn_s[...] += mm_nt(gpre, w1)
    low2_s[...] += mm_nt(hid, d2)
    b1_s[...] += mm_nt(gpre, u1)
    g_d2[...] = mm_tn(b2, hid)
    g_u1[...] = mm_tn(low1, gpre)

    @pl.when(step == last)
    def _():
        low2, b1 = low2_s[...].astype(BF16), b1_s[...].astype(BF16)
        out = live * (mid_s[...] + feed_s[...] + mm(low2, u2_ref[0]))
        la_ref[...] = out[:half].astype(BF16)
        lb_ref[...] = out[half:].astype(BF16)
        g_u2[...] = mm_tn(low2, gf_s[...])
        gn = gn_s[...] + mm(b1, d1_ref[0])
        normed, scale = norm_parts(mid_s[...])
        g_d1[...] = mm_tn(b1, n_s[...])
        gm = gm_ref[...] + norm_back(normed, scale, gain_ref[...], gn)
        gm_ref[...] = gm
        ga = gm.astype(BF16)
        back = mm_nt(ga, ou_ref[0]).astype(BF16)
        gctx_ref[...] = (mm_nt(ga, wo_s[...]) + mm(back, od_ref[0])).astype(BF16)
        g_od[...] = mm_tn(back, ctx_ref[...])
        g_ou[...] = mm_tn(lowo_s[...].astype(BF16), ga)


def feed_forward(info, xa, xb, ca, cb, ctx, gain, wo, w1, w2, od, ou, d1, u1, d2, u2, cuts):
    half, depth = xa.shape
    rows = 2 * half
    rank = od.shape[1]
    dp, tens, wop, wor, woc = wo.shape
    fp, fr, fc = w1.shape[2:]
    rp, rr = w2.shape[2:4]
    hidden = fp * fc
    wide = hidden // cuts
    ff = hidden * tens
    once = lambda *shape: pl.BlockSpec(shape, lambda f, info: (0,) * len(shape), pipeline_mode=pl.Buffered(1))
    whole = lambda *shape: pl.BlockSpec(shape, lambda f, info: (0,) * len(shape))
    picked = pl.BlockSpec((1, rank, depth), lambda f, info: (info[0], 0, 0))
    picked_f = pl.BlockSpec((1, rank, wide), lambda f, info: (info[0], 0, f))
    unit = jax.ShapeDtypeStruct((rank, depth), F32)
    unit_f = jax.ShapeDtypeStruct((rank, ff), F32)
    block_f = pl.BlockSpec((rank, wide), lambda f, info: (0, f))
    return pl.pallas_call(
        feed_kernel,
        grid_spec=pltpu.PrefetchScalarGridSpec(
            num_scalar_prefetch=1,
            grid=(tens * cuts,),
            in_specs=[
                once(half, depth), once(half, depth), once(half, depth), once(half, depth),
                once(rows, depth),
                whole(1, depth),
                once(dp, tens, wop, wor, woc),
                pl.BlockSpec((dp, 1, fp // cuts, fr, fc), lambda f, info: (0, f // cuts, f % cuts, 0, 0)),
                pl.BlockSpec((dp, 1, rp // cuts, rr, woc), lambda f, info: (0, f // cuts, f % cuts, 0, 0)),
                picked, picked, picked, picked_f, picked_f, picked,
            ],
            out_specs=[
                whole(half, depth), whole(half, depth), whole(rows, depth), whole(rows, depth),
                whole(rank, depth), whole(rank, depth), whole(rank, depth), block_f, block_f, whole(rank, depth),
            ],
            scratch_shapes=[
                pltpu.VMEM((depth, depth), BF16),
                pltpu.VMEM((depth, wide), BF16),
                pltpu.VMEM((wide, depth), BF16),
                pltpu.VMEM((rows, depth), F32),
                pltpu.VMEM((rows, depth), BF16),
                pltpu.VMEM((rows, depth), BF16),
                pltpu.VMEM((rows, depth), F32),
                pltpu.VMEM((rows, depth), F32),
            ]
            + [pltpu.VMEM((rows, rank), F32)] * 5,
        ),
        out_shape=[
            jax.ShapeDtypeStruct((half, depth), BF16),
            jax.ShapeDtypeStruct((half, depth), BF16),
            jax.ShapeDtypeStruct((rows, depth), F32),
            jax.ShapeDtypeStruct((rows, depth), BF16),
            unit, unit, unit, unit_f, unit_f, unit,
        ],
        compiler_params=params(),
        name="feed_forward",
    )(info, xa, xb, ca, cb, ctx, gain, wo, w1, w2, od, ou, d1, u1, d2, u2)


def split3(x):
    hi = x.astype(BF16)
    rest = x - hi.astype(F32)
    mid = rest.astype(BF16)
    return hi, mid, (rest - mid.astype(F32)).astype(BF16)


def attend_back_kernel(
    q_ref, k_ref, v_ref, k2_ref, v2_ref, g_ref, o_ref, lse_ref, dq_ref, dk_ref, dv_ref, dk2_ref, dv2_ref, ks, vs, kd, acc
):
    rows = q_ref.shape[0]
    zero = BF16(0)
    lane = lax.broadcasted_iota(jnp.int32, (1, 128), 1)
    scale = BF16(HEAD_DIM ** -0.5)
    q2 = q_ref[...] * scale
    g2 = g_ref[...]
    hi, mid, lo = split3(pltpu.roll(lse_ref[...], HEAD_DIM, 1))
    prod = g2.astype(F32) * o_ref[...].astype(F32)
    qa, ga, qm, gm = [], [], [], []
    for h in range(2):
        mine, b = (lane // HEAD_DIM) == h, HEAD_DIM * (1 - h)
        qa.append(
            jnp.where(mine, q2, jnp.where(lane == b, -hi, jnp.where(lane == b + 1, -mid, jnp.where(lane == b + 2, -lo, zero))))
        )
        dh, dm, dl = split3(jnp.sum(jnp.where(mine, prod, 0.0), axis=1, keepdims=True))
        ga.append(
            jnp.where(mine, g2, jnp.where(lane == b, -dh, jnp.where(lane == b + 1, -dm, jnp.where(lane == b + 2, -dl, zero))))
        )
        qm.append(jnp.where(mine, q2, zero))
        gm.append(jnp.where(mine, g2, zero))
        ones = ((lane >= b) & (lane < b + 3)).astype(BF16)
        for i, (kr, vr) in enumerate(((k_ref, v_ref), (k2_ref, v2_ref))):
            s = slice(i * rows, (i + 1) * rows)
            ks[h, s, :] = jnp.where(mine, kr[0], ones)
            vs[h, s, :] = jnp.where(mine, vr[0], ones)
            kd[h, s, :] = jnp.where(mine, kr[0] * scale, zero)
    for i, (dk_out, dv_out) in enumerate(((dk_ref, dv_ref), (dk2_ref, dv2_ref))):
        s = slice(i * rows, (i + 1) * rows)
        dk = jnp.zeros((rows, 128), F32)
        dv = jnp.zeros((rows, 128), F32)
        dq = jnp.zeros((rows, 128), F32)
        for h in range(2):
            p = jnp.exp(mm_nt(ks[h, s, :], qa[h]))
            ds = (p * mm_nt(vs[h, s, :], ga[h])).astype(BF16)
            dv = dv + mm(p.astype(BF16), gm[h])
            dk = dk + mm(ds, qm[h])
            dq = dq + mm_tn(ds, kd[h, s, :])
        dk_out[0] = dk.astype(BF16)
        dv_out[0] = dv.astype(BF16)
        if i == 0:
            acc[...] = dq
        else:
            dq_ref[...] = (acc[...] + dq).astype(BF16)


def attend_back_body(*refs):
    *rest, dkv_ref, dkv2_ref, ks, vs, kd, acc = refs
    attend_back_kernel(
        *rest, dkv_ref.at[0:1], dkv_ref.at[1:2], dkv2_ref.at[0:1], dkv2_ref.at[1:2], ks, vs, kd, acc
    )


def attend_back(q, kv, kv2, g, ctx, lse):
    rows, depth = q.shape
    flat = pl.BlockSpec((rows, 128), lambda i: (0, i))
    part = lambda j: pl.BlockSpec((1, rows, 128), lambda i: (j, 0, i))
    both = pl.BlockSpec((2, rows, 128), lambda i: (0, 0, i))
    return pl.pallas_call(
        attend_back_body,
        grid=(depth // 128,),
        in_specs=[flat, part(0), part(1), part(0), part(1), flat, flat, flat],
        out_specs=[flat, both, both],
        out_shape=[jax.ShapeDtypeStruct((rows, depth), BF16)] + [jax.ShapeDtypeStruct((2, rows, depth), BF16)] * 2,
        scratch_shapes=[pltpu.VMEM((2, 2 * rows, 128), BF16)] * 3 + [pltpu.VMEM((rows, 128), F32)],
        compiler_params=params(),
        name="attend_back",
    )(q, kv, kv, kv2, kv2, g, ctx, lse)


def qkv_back_kernel(
    info, xa_ref, xb_ref, gain_ref, dq_ref, dkv_ref, dkv2_ref, gm_ref, low_ref, w_ref, down_ref, up_ref,
    ya_ref, yb_ref, g_down, g_up, gn_s, back_s,
):
    half, depth = xa_ref.shape
    parts, width = w_ref.shape[1], w_ref.shape[4]
    step, last = pl.program_id(0), pl.num_programs(0) - 1

    def go(g, first):
        back = mm_nt(g, up_ref[0, 0])
        total = back if first else back_s[...] + back
        back_s[...] = total
        acc = None if first else gn_s[...]
        for part in range(parts):
            cols = slice(part * width, (part + 1) * width)
            term = mm_nt(g[:, cols], w_ref[:, part, 0].reshape(depth, width))
            acc = term if acc is None else acc + term
        gn_s[...] = acc
        g_up[0] = mm_tn(low_ref[...].astype(BF16), g)

    @pl.when(step == 0)
    def _():
        go(dq_ref[...], True)

    @pl.when(step > 0)
    def _():
        go((dkv_ref[0].astype(F32) + dkv2_ref[0].astype(F32)).astype(BF16), False)

    @pl.when(step == last)
    def _():
        back = back_s[...].astype(BF16)
        gn_s[...] += mm(back, down_ref[0])
        total = jnp.zeros(g_down.shape, F32)
        for part, (x_ref, y_ref) in enumerate(((xa_ref, ya_ref), (xb_ref, yb_ref))):
            s = slice(part * half, (part + 1) * half)
            normed, scale = norm_parts(x_ref[...].astype(F32))
            total = total + mm_tn(back_s[s, :].astype(BF16), (normed * gain_ref[...]).astype(BF16))
            y_ref[...] = (gm_ref[s, :] + norm_back(normed, scale, gain_ref[...], gn_s[s, :])).astype(BF16)
        g_down[...] = total


def project_back(info, xa, xb, gain, dq, dkv, dkv2, gm, low, w, down, up):
    half, depth = xa.shape
    rows = 2 * half
    rank = down.shape[1]
    dp, tens, _, wr, wc = w.shape
    whole = lambda *shape: pl.BlockSpec(shape, lambda j, info: (0,) * len(shape))
    once = lambda *shape: pl.BlockSpec(shape, lambda j, info: (0,) * len(shape), pipeline_mode=pl.Buffered(1))
    pair = pl.BlockSpec((1, rows, depth), lambda j, info: (jnp.maximum(j - 1, 0), 0, 0))
    return pl.pallas_call(
        qkv_back_kernel,
        grid_spec=pltpu.PrefetchScalarGridSpec(
            num_scalar_prefetch=1,
            grid=(3,),
            in_specs=[
                once(half, depth), once(half, depth), whole(1, depth),
                once(rows, depth), pair, pair,
                once(rows, depth), once(rows, rank),
                pl.BlockSpec((dp, tens, 1, wr, wc), lambda j, info: (0, 0, j, 0, 0)),
                pl.BlockSpec((1, rank, depth), lambda j, info: (info[0], 0, 0)),
                pl.BlockSpec((1, 1, rank, depth), lambda j, info: (info[0], j, 0, 0)),
            ],
            out_specs=[
                whole(half, depth), whole(half, depth), whole(rank, depth),
                pl.BlockSpec((1, rank, depth), lambda j, info: (j, 0, 0)),
            ],
            scratch_shapes=[pltpu.VMEM((rows, depth), F32), pltpu.VMEM((rows, rank), F32)],
        ),
        out_shape=[
            jax.ShapeDtypeStruct((half, depth), BF16),
            jax.ShapeDtypeStruct((half, depth), BF16),
            jax.ShapeDtypeStruct((rank, depth), F32),
            jax.ShapeDtypeStruct((3, rank, depth), F32),
        ],
        compiler_params=params(),
        name="project_back",
    )(info, xa, xb, gain, dq, dkv, dkv2, gm, low, w, down, up)


def table_kernel(places, owner, g_ref, *outs):
    _, halves, tens, cuts, _, width = g_ref.shape
    pair = pl.program_id(0)

    @pl.when(pair == 0)
    def _():
        for out in outs:
            out[...] = jnp.zeros_like(out)

    for t in range(tens):
        e = owner[pair * tens + t]
        for out, (sub, start) in zip([outs[n] for n, _, _ in places], [(sub, start) for _, sub, start in places]):
            cols = out.shape[-1]
            step = min(cols, width)
            for c in range(0, cols, step):
                where = start + c
                half, where = where // (cuts * width), where % (cuts * width)
                cut, where = where // width, where % width
                piece = g_ref[0, half, t, cut, :, where : where + step].astype(F32)
                if sub is None:
                    out[e, :, c : c + step] += piece
                else:
                    out[e, sub, :, c : c + step] += piece


def tables(owner, gathered, outs, places):
    dps, tens = gathered.shape[:2]
    gathered = gathered.reshape((dps // 2, 2) + gathered.shape[1:])
    spots, start = [], 0
    for n, sub in places:
        spots.append((n, sub, start))
        start += outs[n][-1]
    block = (1,) + gathered.shape[1:]
    return pl.pallas_call(
        functools.partial(table_kernel, tuple(spots)),
        grid_spec=pltpu.PrefetchScalarGridSpec(
            num_scalar_prefetch=1,
            grid=(dps // 2,),
            in_specs=[pl.BlockSpec(block, lambda p, owner: (p, 0, 0, 0, 0, 0))],
            out_specs=[pl.BlockSpec(shape, lambda p, owner, n=len(shape): (0,) * n) for shape in outs],
        ),
        out_shape=[jax.ShapeDtypeStruct(shape, F32) for shape in outs],
        compiler_params=params(),
        name="tables",
    )(owner, gathered)


def per_device(
    tokens, cotangent, clip_live, adapter_index, gain_one, gain_two, weight_qkv, weight_out, weight_fc1, weight_fc2,
    qkv_down, qkv_up, out_down, out_up, fc1_down, fc1_up, fc2_down, fc2_up,
):
    dps, tens = lax.axis_size("dp"), lax.axis_size("tensor")
    slots = tokens.shape[0]
    axes = ("dp", "tensor")
    dp, t = lax.axis_index("dp"), lax.axis_index("tensor")
    assert slots == 2 and tens == 4 and dps % 2 == 0

    def route(flip):
        perm = []
        for a in range(dps):
            for b in range(tens):
                slot = (b % 2) ^ flip
                perm.append((a * tens + b, (a - a % 2 + b // 2) * tens + 2 * (a % 2) + slot))
        return perm

    routes = [route(0), route(1)]
    swap = [(a * tens + b, (a ^ 1) * tens + b) for a in range(dps) for b in range(tens)]
    back_routes = [[(d, s) for s, d in r] for r in routes]

    def spread(field):
        parts = []
        for flip in range(2):
            slot = (t % 2) ^ flip
            parts.append(lax.ppermute(lax.dynamic_index_in_dim(field, slot, 0, False), axes, routes[flip]))
        return parts

    def unspread(parts):
        got = [lax.ppermute(part, axes, r) for part, r in zip(parts, back_routes)]
        return jnp.where(t % 2 == 0, jnp.stack(got), jnp.stack(got[::-1]))

    codes = lax.all_gather(jnp.stack([adapter_index, clip_live]), "dp")
    owner, alive = codes[:, 0].reshape(-1), codes[:, 1].reshape(-1)
    clip = (dp // 2) * tens + t
    info = jnp.stack([owner[clip], alive[clip]])

    def fold(w, dim):
        k = max(1, 128 // w.shape[dim])
        if k == 1:
            return w
        w = jnp.moveaxis(w.reshape((dps // k, k) + w.shape[1:]), 1, dim)
        return w.reshape(w.shape[:dim] + (-1,) + w.shape[dim + 2 :])

    plan = Plan(dps, tens)
    fine = 8 if dps <= 8 else 2
    w_qkv = weight_qkv.reshape(-1, 16, weight_qkv.shape[2])
    w_qkv = gather(plan, dps, w_qkv, fine, 0).reshape((dps, tens) + weight_qkv.shape)
    w_qkv = fold(w_qkv, 3)
    xa, xb = spread(tokens)
    g1, g2 = gain_one.reshape(1, -1), gain_two.reshape(1, -1)
    q, kv, low = project(info, xa, xb, g1, w_qkv, qkv_down, qkv_up)
    kv2 = lax.ppermute(kv, axes, swap)
    ca, cb = spread(cotangent)
    in_rows = weight_fc1.shape[0]
    parts_1 = weight_fc1.reshape(in_rows, -1, 128).transpose(1, 0, 2)
    parts_2 = weight_fc2.reshape(parts_1.shape[0], -1, weight_fc2.shape[1])
    parts_o = weight_out.reshape(2, -1, weight_out.shape[1])
    ctx, lse, w_out, w_fc1, w_fc2 = attend_gather(plan, dps, q, kv, kv2, parts_o, parts_1, parts_2, fine, 1)
    w_out, w_fc1, w_fc2 = fold(w_out, 4), fold(w_fc1, 3), fold(w_fc2, 4)
    cuts = 2
    la, lb, gm, gctx, g_od, g_ou, g_d1, g_u1, g_d2, g_u2 = feed_forward(
        info, xa, xb, ca, cb, ctx, g2, w_out, w_fc1, w_fc2, out_down, out_up, fc1_down, fc1_up, fc2_down, fc2_up, cuts
    )
    layer_out = unspread([la, lb])

    def pool(pieces):
        flat = jnp.concatenate(pieces, axis=-1).astype(BF16)
        cols = flat.shape[-1] // 2
        mine = lax.dynamic_slice_in_dim(flat, dp % 2 * cols, cols, 1)
        other = lax.dynamic_slice_in_dim(flat, (1 - dp % 2) * cols, cols, 1)
        total = mine.astype(F32) + lax.ppermute(other, axes, swap).astype(F32)
        got = lax.all_gather(total.astype(BF16), axes)
        return got.reshape(dps, tens, 1, flat.shape[0], cols)

    early = pool([g_od, g_ou, g_u1, g_d1, g_u2, g_d2])
    dq, dkv, dkv_far = attend_back(q, kv, kv2, gctx, ctx, lse)
    dkv2 = lax.ppermute(dkv_far, axes, swap)
    dq, dkv2, early, layer_out = lax.optimization_barrier((dq, dkv2, early, layer_out))
    ya, yb, g_qd, g_qu = project_back(info, xa, xb, g1, dq, dkv, dkv2, gm, low, w_qkv, qkv_down, qkv_up)
    late = share(plan, dps, [g_qd, g_qu[0], g_qu[1], g_qu[2]], 2, 2)
    grad_tokens = unspread([ya, yb])
    t_od, t_ou, t_d1, t_u1, t_d2, t_u2 = tables(
        owner, early, [a.shape for a in (out_down, out_up, fc1_down, fc1_up, fc2_down, fc2_up)],
        [(0, None), (1, None), (3, None), (2, None), (5, None), (4, None)],
    )
    t_qd, t_qu = tables(owner, late, [qkv_down.shape, qkv_up.shape], [(0, None), (1, 0), (1, 1), (1, 2)])
    return layer_out, grad_tokens, t_qd, t_qu, t_od, t_ou, t_d1, t_u1, t_d2, t_u2


def solution(mesh):
    rows, whole = P("dp", "tensor", None), P()
    return jax.shard_map(
        per_device,
        mesh=mesh,
        in_specs=(rows, rows, P("dp"), P("dp"), whole, whole, P(None, "dp", "tensor"), P("tensor", "dp"),
                  P("dp", "tensor"), P("tensor", "dp")) + (whole,) * 8,
        out_specs=(rows, rows) + (whole,) * 8,
        check_vma=False,
    )
```

time: 1790 us -> 546 us (0.31)
  waiting for transfers between devices: 860 us -> 28.9 us
  matrix products: 458 us -> 0 us
  Pallas kernels: 0 us -> 429 us
  local copies, waits for them, and re-layouts: 298 us -> 10.5 us
  other arithmetic: 134 us -> 16.8 us
  starting transfers between devices: 0.83 us -> 29.5 us
    dot_general x76 -> x0, matrix products: 458 us -> none  [the longest x4 54.9 us: backward_block(): jnp.einsum('qhc,khc->hqk', query_block, all_keys, preferred_element_type=...]
    pallas_call x0 -> x9, Pallas kernels: none -> 429 us  [the longest x1 127 us: attend_gather(): pl.pallas_call(kernel, grid=(grid,), in_specs=blocks + [hbm] * 3, out_spe...]
    all_gather x7 -> x1, waiting for transfers between devices: 402 us -> 0.01 us  [pool(): got = lax.all_gather(total.astype(BF16), axes)]
    unnamed x16 -> x1, waiting for transfers between devices: 323 us -> 0.02 us
    unnamed x186 -> x17, local copies, waits for them, and re-layouts: 178 us -> 4.72 us
    psum x1 -> x0, waiting for transfers between devices: 136 us -> none  [per_device(): lax.psum((to_tables(query_key_value_down_gradient), to_tables(widen(grad_...]
    convert_element_type x11 -> x1, other arithmetic: 102 us -> 1.74 us  [pool(): got = lax.all_gather(total.astype(BF16), axes)]
    while x48 -> x0, local copies, waits for them, and re-layouts: 41.8 us -> none
  transfers between devices with their start and end apart: 12 -> 12, of which waited for: 11 -> 3; matrix products, arithmetic and copies ran while one was open for 29% -> 3% of each run, Pallas kernels for 0% -> 62%
where the time goes in v1:
time: 546 us; the launch traced here: 539 us
  Pallas kernels  429 us (79%)
  starting transfers between devices  29.5 us (5%)
  waiting for transfers between devices  28.9 us (5%)
  other arithmetic  16.8 us (3%)
  between operations  15.4 us (3%)
  local copies, waits for them, and re-layouts  10.5 us (2%)
  blocking collectives  8.66 us (2%)
    pallas_call x1, Pallas kernels, attend_gather(): pl.pallas_call(kernel, grid=(grid,), in_specs=blocks + [hbm] * 3, out_spe...  127 us
    pallas_call x1, Pallas kernels, attend_back(): pl.pallas_call(attend_back_body, grid=(depth // 128,), in_specs=[flat, pa...  80.6 us
    pallas_call x1, Pallas kernels, gather(): pl.pallas_call(functools.partial(gather_kernel, plan, cuts), in_specs=[pl...  64.1 us
    pallas_call x1, Pallas kernels, feed_forward(): pl.pallas_call(feed_kernel, grid_spec=pltpu.PrefetchScalarGridSpec(num_sc...  59.6 us
    pallas_call x1, Pallas kernels, share(): pl.pallas_call(functools.partial(share_kernel, plan), in_specs=[pl.BlockS...  48.4 us
    ppermute x4, waiting for transfers between devices, unspread(): got = [lax.ppermute(part, axes, r) for part, r in zip(parts, back_routes)]  27.4 us
    pallas_call x1, Pallas kernels, project(): pl.pallas_call(qkv_kernel, grid_spec=pltpu.PrefetchScalarGridSpec(num_sca...  20.8 us
    ppermute x4, starting transfers between devices, unspread(): got = [lax.ppermute(part, axes, r) for part, r in zip(parts, back_routes)]  17.7 us
  transfers between devices with their start and end apart: 12, of which 3 were waited for; matrix products, arithmetic and copies ran while one was open for 3% of the time, Pallas kernels for 62%

profile of v1, /device:TPU:1, one launch (start us, length us, event | category | flops | bytes accessed | tf_op | source)
XLA Modules:
  0.0 539.0 jit_solution(428530842632082478)
XLA Ops:
  7.3 1.5 dynamic-slice_bitcast_fusion.2
  8.8 4.8 collective-permute-start.1
  13.6 1.9 collective-permute-start
  15.5 8.7 %all-gather.2 = s32[8,2,2]{2,1,0:T(2,128)S(1)} all-gather(s32[1,2,2]{2,1,0:T(2,128)S(1)} %add_bitcast_fusion), channel_id=2, replica_groups=mesh['dp'=8,'tensor'=4] {'dp'}, dimensions={0}, use_global_device_ids=true | all-gather | bytes 144 | tf_op jit(solution)/shard_map/all_gather | solution.py:812
  25.5 64.1 %gather.1 = bf16[8,4,24,16,256]{4,3,2,1,0:T(8,128)(2,1)} custom-call(bf16[24,16,256]{2,1,0:T(8,128)(2,1)} %bitcast.46), custom_call_target="tpu_custom_call" | custom-call | tf_op jit(solution)/shard_map/gather/pallas_call | solution.py:188
  89.6 1.9 pad_add_fusion.info
  92.6 20.8 %project.1 = (bf16[784,1024]{1,0:T(8,128)(2,1)}, bf16[2,784,1024]{2,1,0:T(8,128)(2,1)S(1)}, f32[784,16]{1,0:T(8,128)}) custom-call(s32[2]{0:T(128)} %pad_add_fusion.info, bf16[392,1024]{1,0:T(8,128)(2,1)} %copy-done.1, bf16[392,1024]{1,0:T(8,128)(2,1)} %copy-done, f32[1,1024]{1,0:T(1,128)} %bitcast.48, bf16[8,4,3,128,256]{4,3,2,1,0:T(8,128)(2,1)} %bitcast.36, ...), custom_call_target="tpu_custom_call" | custom-call | tf_op jit(solution)/shard_map/project/pallas_call | solution.py:274
  113.5 1.3 dynamic-slice_bitcast_fusion
  115.0 4.4 collective-permute-start.3
  119.4 1.1 copy.31
  121.4 126.9 %attend_gather.1 = (bf16[784,1024]{1,0:T(8,128)(2,1)}, f32[784,1024]{1,0:T(8,128)}, f32[8,8,128]{2,1,0:T(8,128)}, bf16[8,4,2,128,128]{4,3,2,1,0:T(8,128)(2,1)}, ...) custom-call(bf16[784,1024]{1,0:T(8,128)(2,1)} %get-tuple-element.63.q_ref.refs_0_, ...), custom_call_target="tpu_custom_call" | custom-call | tf_op jit(solution)/shard_map/attend_gather/pallas_call | solution.py:411
  248.2 1.4 reduce_max.9
  250.3 59.6 %feed_forward.1 = (bf16[392,1024]{1,0:T(8,128)(2,1)}, bf16[392,1024]{1,0:T(8,128)(2,1)}, f32[784,1024]{1,0:T(8,128)}, bf16[784,1024]{1,0:T(8,128)(2,1)}, f32[16,...) custom-call(s32[2]{0:T(128)} %pad_add_fusion.info, ...), custom_call_target="tpu_custom_call" | custom-call | tf_op jit(solution)/shard_map/feed_forward/pallas_call | solution.py:532
  311.6 1.0 convert_dynamic-update-slice_fusion.1
  314.3 1.0 convert_dynamic-update-slice_fusion
  316.2 1.5 collective-permute-done.6
  317.6 1.7 add_convert_fusion
  319.4 80.6 %attend_back.1 = (bf16[784,1024]{1,0:T(8,128)(2,1)}, bf16[2,784,1024]{2,1,0:T(8,128)(2,1)}, bf16[2,784,1024]{2,1,0:T(8,128)(2,1)}) custom-call(bf16[784,1024]{1,0:T(8,128)(2,1)} %get-tuple-element.63.q_ref.refs_0_, bf16[2,784,1024]{2,1,0:T(8,128)(2,1)S(1)} %get-tuple-element.64.k_ref.v_ref.refs_1_.refs_2_, ...), custom_call_target="tpu_custom_call" | custom-call | tf_op jit(solution)/shard_map/attend_back/pallas_call | solution.py:641
  400.3 1.9 collective-permute-start.7
  402.2 3.2 collective-permute-start.8
  405.3 21.8 %collective-permute-done.7 = bf16[392,1024]{1,0:T(8,128)(2,1)} collective-permute-done((bf16[392,1024]{1,0:T(8,128)(2,1)}, bf16[392,1024]{1,0:T(8,128)(2,1)}, u32[]{:S(2)}, u32[]{:S(2)}) %collective-permute-start.7) | collective-permute-done | bytes 802848 | tf_op jit(solution)/shard_map/ppermute | solution.py:809
  427.1 5.7 %collective-permute-done.8 = bf16[392,1024]{1,0:T(8,128)(2,1)} collective-permute-done((bf16[392,1024]{1,0:T(8,128)(2,1)}, bf16[392,1024]{1,0:T(8,128)(2,1)}, u32[]{:S(2)}, u32[]{:S(2)}) %collective-permute-start.8) | collective-permute-done | bytes 802848 | tf_op jit(solution)/shard_map/ppermute | solution.py:809
  432.8 3.3 maximum_select_fusion
  436.1 1.7 copy-done.2
  437.8 16.8 %project_back.1 = (bf16[392,1024]{1,0:T(8,128)(2,1)}, bf16[392,1024]{1,0:T(8,128)(2,1)}, f32[16,1024]{1,0:T(8,128)}, f32[3,16,1024]{2,1,0:T(8,128)}) custom-call(s32[2]{0:T(128)} %pad_add_fusion.info, bf16[392,1024]{1,0:T(8,128)(2,1)} %copy-done.1, bf16[392,1024]{1,0:T(8,128)(2,1)} %copy-done, f32[1,1024]{1,0:T(1,128)} %bitcast.49, ...), custom_call_target="tpu_custom_call" | custom-call | tf_op jit(solution)/shard_map/project_back/pallas_call | solution.py:702
  454.6 9.9 %collective-permute-start.9 = (bf16[392,1024]{1,0:T(8,128)(2,1)}, bf16[392,1024]{1,0:T(8,128)(2,1)S(1)}, u32[]{:S(2)}, u32[]{:S(2)}) collective-permute-start(bf16[392,1024]{1,0:T(8,128)(2,1)} %get-tuple-element.90), channel_id=1, source_target_pairs={{0,0},{1,1},{4,2},{5,3},{2,4},{3,5},{6,6},{7,7},{8,8},{9,9},{12,10... | collective-permute-start | bytes 2408456 | tf_op jit(solution)/shard_map/ppermute | solution.py:809
  464.5 2.7 collective-permute-start.10
  468.1 0.9 convert.39
  469.8 48.4 %share.1 = bf16[8,4,2,16,1024]{4,3,2,1,0:T(8,128)(2,1)} custom-call(bf16[2,2,16,1024]{3,2,1,0:T(8,128)(2,1)} %bitcast.44), custom_call_target="tpu_custom_call" | custom-call | tf_op jit(solution)/shard_map/share/pallas_call | solution.py:221
  518.2 4.6 tables.2
  522.8 7.5 %tables.3 = (f32[8,16,1024]{2,1,0:T(8,128)}, f32[8,16,1024]{2,1,0:T(8,128)}, f32[8,16,1024]{2,1,0:T(8,128)}, f32[8,16,4096]{2,1,0:T(8,128)}, f32[8,16,4096]{2,1,0:T(8,128)}, /*index=5*/f32[8,16,1024]{2,1,0:T(8,128)}) custom-call(s32[16]{0:T(128)} %copy-done.5, bf16[4,2,4,1,16,6144]{5,4,3,2,1,0:T(8,128)(2,1)} %bitcast.39), custom_call_target="tpu_custom_call" | custom-call | tf_op jit(solution)/shard_map/tables/pallas_call | solution.py:765
  530.3 1.4 maximum_select_fusion.1
  (48 shorter events, 9.9 us)
Async XLA Ops:
  7.2 428.9 %all-gather.5.cloned.1.call-start = ((), (), s32[]{:S(2)}) async-start(), calls=%async_computation | async-start | bytes 6488064 | tf_op jit(solution)/shard_map/all_gather | solution.py:852
  7.2 8.2 %copy-start.6 = (s32[2]{0:T(128)S(1)}, s32[2]{0:T(128)}, u32[]{:S(2)}) copy-start(s32[2]{0:T(128)} %param.22) | copy-start | bytes 28
  7.3 8.2 %copy-start.7 = (s32[2]{0:T(128)S(1)}, s32[2]{0:T(128)}, u32[]{:S(2)}) copy-start(s32[2]{0:T(128)} %param.23) | copy-start | bytes 28
  8.8 82.7 %collective-permute-start.1 = (bf16[392,1024]{1,0:T(8,128)(2,1)S(1)}, bf16[392,1024]{1,0:T(8,128)(2,1)S(1)}, u32[]{:S(2)}, u32[]{:S(2)}) collective-permute-start(bf16[392,1024]{1,0:T(8,128)(2,1)S(1)} %get-tuple-element.107), channel_id=1, source_target_pairs={{0,1},{1,0},{2,5},{3,4},{4,3},{5,2},{6,7},{7,6},{8,9},{9,8},{10,13... | collective-permute-start | bytes 2408456 | tf_op jit(solution)/shard_map/ppermute | solution.py:805
  13.6 77.9 %collective-permute-start = (bf16[392,1024]{1,0:T(8,128)(2,1)S(1)}, bf16[392,1024]{1,0:T(8,128)(2,1)S(1)}, u32[]{:S(2)}, u32[]{:S(2)}) collective-permute-start(bf16[392,1024]{1,0:T(8,128)(2,1)S(1)} %get-tuple-element.108), channel_id=1, source_target_pairs={{0,0},{1,1},{2,4},{3,5},{4,2},{5,3},{6,6},{7,7},{8,8},{9,9},{10,12... | collective-permute-start | bytes 2408456 | tf_op jit(solution)/shard_map/ppermute | solution.py:805
  24.3 65.3 %copy-start.5 = (s32[16]{0:T(128)}, s32[16]{0:T(128)S(1)}, u32[]{:S(2)}) copy-start(s32[16]{0:T(128)S(1)} %reshape_squeeze.6.owner) | copy-start | bytes 196
  91.5 0.9 copy-start
  91.5 1.1 copy-start.1
  92.6 20.9 %copy-start.3 = (bf16[2,392,1024]{2,1,0:T(8,128)(2,1)S(1)}, bf16[2,392,1024]{2,1,0:T(8,128)(2,1)}, u32[]{:S(2)}) copy-start(bf16[2,392,1024]{2,1,0:T(8,128)(2,1)} %param.21) | copy-start | bytes 4816900
  113.4 8.0 %collective-permute-start.2 = (bf16[2,784,1024]{2,1,0:T(8,128)(2,1)S(1)}, bf16[2,784,1024]{2,1,0:T(8,128)(2,1)}, u32[]{:S(2)}, u32[]{:S(2)}) collective-permute-start(bf16[2,784,1024]{2,1,0:T(8,128)(2,1)S(1)} %get-tuple-element.64.k_ref.v_ref.refs_1_.refs_2_), channel_id=1, source_target_pairs={{0,4},{1,5},{2,6},{3,7},{4,0},{5,1},{6,2},{7,3},{8,12},{9,13},{10,... | collective-permute-start | bytes 9633800 | tf_op jit(solution)/shard_map/ppermute | solution.py:832
  114.8 135.5 %collective-permute-start.4 = (bf16[392,1024]{1,0:T(8,128)(2,1)}, bf16[392,1024]{1,0:T(8,128)(2,1)}, u32[]{:S(2)}, u32[]{:S(2)}) collective-permute-start(bf16[392,1024]{1,0:T(8,128)(2,1)} %get-tuple-element.105), channel_id=1, source_target_pairs={{0,1},{1,0},{2,5},{3,4},{4,3},{5,2},{6,7},{7,6},{8,9},{9,8},{10,13... | collective-permute-start | bytes 2408456 | tf_op jit(solution)/shard_map/ppermute | solution.py:805
  115.0 135.4 %collective-permute-start.3 = (bf16[392,1024]{1,0:T(8,128)(2,1)}, bf16[392,1024]{1,0:T(8,128)(2,1)}, u32[]{:S(2)}, u32[]{:S(2)}) collective-permute-start(bf16[392,1024]{1,0:T(8,128)(2,1)} %get-tuple-element.106), channel_id=1, source_target_pairs={{0,0},{1,1},{2,4},{3,5},{4,2},{5,3},{6,6},{7,7},{8,8},{9,9},{10,12... | collective-permute-start | bytes 2408456 | tf_op jit(solution)/shard_map/ppermute | solution.py:805
  315.2 0.7 copy-start.4
  316.0 1.6 collective-permute-start.6
  400.1 36.0 %collective-permute-start.5 = (bf16[2,784,1024]{2,1,0:T(8,128)(2,1)}, bf16[2,784,1024]{2,1,0:T(8,128)(2,1)S(1)}, u32[]{:S(2)}, u32[]{:S(2)}) collective-permute-start(bf16[2,784,1024]{2,1,0:T(8,128)(2,1)} %get-tuple-element.75), channel_id=1, source_target_pairs={{0,4},{1,5},{2,6},{3,7},{4,0},{5,1},{6,2},{7,3},{8,12},{9,13},{10,... | collective-permute-start | bytes 9633800 | tf_op jit(solution)/shard_map/ppermute | solution.py:857
  400.3 26.9 %collective-permute-start.7 = (bf16[392,1024]{1,0:T(8,128)(2,1)}, bf16[392,1024]{1,0:T(8,128)(2,1)}, u32[]{:S(2)}, u32[]{:S(2)}) collective-permute-start(bf16[392,1024]{1,0:T(8,128)(2,1)} %get-tuple-element.82), channel_id=1, source_target_pairs={{0,0},{1,1},{4,2},{5,3},{2,4},{3,5},{6,6},{7,7},{8,8},{9,9},{12,10... | collective-permute-start | bytes 2408456 | tf_op jit(solution)/shard_map/ppermute | solution.py:809
  402.2 30.6 %collective-permute-start.8 = (bf16[392,1024]{1,0:T(8,128)(2,1)}, bf16[392,1024]{1,0:T(8,128)(2,1)}, u32[]{:S(2)}, u32[]{:S(2)}) collective-permute-start(bf16[392,1024]{1,0:T(8,128)(2,1)} %get-tuple-element.83), channel_id=1, source_target_pairs={{1,0},{0,1},{5,2},{4,3},{3,4},{2,5},{7,6},{6,7},{9,8},{8,9},{13,10... | collective-permute-start | bytes 2408456 | tf_op jit(solution)/shard_map/ppermute | solution.py:809
  436.1 1.7 copy-start.2
  454.6 75.7 %collective-permute-start.9 = (bf16[392,1024]{1,0:T(8,128)(2,1)}, bf16[392,1024]{1,0:T(8,128)(2,1)S(1)}, u32[]{:S(2)}, u32[]{:S(2)}) collective-permute-start(bf16[392,1024]{1,0:T(8,128)(2,1)} %get-tuple-element.90), channel_id=1, source_target_pairs={{0,0},{1,1},{4,2},{5,3},{2,4},{3,5},{6,6},{7,7},{8,8},{9,9},{12,10... | collective-permute-start | bytes 2408456 | tf_op jit(solution)/shard_map/ppermute | solution.py:809
  464.5 65.7 %collective-permute-start.10 = (bf16[392,1024]{1,0:T(8,128)(2,1)}, bf16[392,1024]{1,0:T(8,128)(2,1)S(1)}, u32[]{:S(2)}, u32[]{:S(2)}) collective-permute-start(bf16[392,1024]{1,0:T(8,128)(2,1)} %get-tuple-element.91), channel_id=1, source_target_pairs={{1,0},{0,1},{5,2},{4,3},{3,4},{2,5},{7,6},{6,7},{9,8},{8,9},{13,10... | collective-permute-start | bytes 2408456 | tf_op jit(solution)/shard_map/ppermute | solution.py:809
Sparse Core Ops, SparseCore 0:
  319.5 68.7 all-gather.4

commit v2 on v1

v2 whole, which is shorter than its diff:
```python
import functools
import math

import jax
import jax.numpy as jnp
from jax import lax
from jax.experimental import pallas as pl
from jax.experimental.pallas import tpu as pltpu
from jax.sharding import PartitionSpec as P

HEAD_DIM = 64
EPS = 1e-06
F32 = jnp.float32
BF16 = jnp.bfloat16
NT = (((1,), (1,)), ((), ()))
TN = (((0,), (0,)), ((), ()))
VMEM_BYTES = 61 << 20
SAFE_SCORE = 60.0


def mm(a, b):
    return jnp.dot(a, b, preferred_element_type=F32)


def mm_nt(a, b):
    return lax.dot_general(a, b, NT, preferred_element_type=F32)


def mm_tn(a, b):
    return lax.dot_general(a, b, TN, preferred_element_type=F32)


def norm_parts(field):
    centered = field - jnp.mean(field, axis=-1, keepdims=True)
    scale = lax.rsqrt(jnp.mean(centered * centered, axis=-1, keepdims=True) + EPS)
    return centered * scale, scale


def norm_back(normed, scale, gain, incoming):
    weighted = incoming * gain
    return scale * (
        weighted
        - jnp.mean(weighted, axis=-1, keepdims=True)
        - normed * jnp.mean(weighted * normed, axis=-1, keepdims=True)
    )


def params(*semantics):
    return pltpu.CompilerParams(vmem_limit_bytes=VMEM_BYTES)


class Plan:
    def __init__(self, dps, tens):
        self.tens = tens
        bits = [1 << i for i in range(1, dps.bit_length() - 1)]
        self.orders = (bits + [1], bits[::-1] + [1])
        self.hops = dps - 1
        self.ways = []
        for order in self.orders:
            blocks = [0]
            for bit in order:
                blocks = blocks + [r | bit for r in blocks]
            tops = {r: max([j for j, bit in enumerate(order) if r & bit], default=-1) for r in blocks}
            sends = {r: range(tops[r] + 1, len(order)) for r in blocks}
            ids = {}
            for r in blocks:
                for j in sends[r]:
                    ids[(r, j)] = len(ids)
            blocks.sort(key=lambda r: bin(r).count("1"))
            self.ways.append((order, blocks, tops, sends, ids))

    def semaphores(self, items):
        dma = lambda *shape: pltpu.SemaphoreType.DMA(shape)
        near = self.tens - 1
        return [dma(items), dma(items, near), dma(items, near), dma(items, self.hops), dma(items, self.hops)]

    def greet(self, extra=()):
        me, t = lax.axis_index("dp"), lax.axis_index("tensor")
        peers = [(me, lax.rem(t + k, self.tens)) for k in range(1, self.tens)]
        peers += [(me ^ bit, t) for bit in self.orders[0]]
        peers += list(extra)
        barrier = pltpu.get_barrier_semaphore()
        for peer in peers:
            pl.semaphore_signal(barrier, inc=1, device_id=peer, device_id_type=pl.DeviceIdType.MESH)
        pl.semaphore_wait(barrier, len(peers))


class Item:
    def __init__(self, plan, sems, number, src, spot, order):
        self.plan, self.src, self.spot = plan, src, spot
        self.local, self.zs, self.zr, self.ss, self.rs = [s.at[number] for s in sems]
        self.order, self.blocks, self.tops, self.sends, self.ids = plan.ways[order]
        self.me, self.t = lax.axis_index("dp"), lax.axis_index("tensor")
        self.stages = [r for r in self.blocks if len(self.sends[r])]

    def keep(self):
        return pltpu.make_async_copy(self.src, self.spot(self.me, self.t), self.local)

    def along(self, d, arriving=False):
        n = self.plan.tens
        return pltpu.make_async_remote_copy(
            src_ref=self.src,
            dst_ref=self.spot(self.me, lax.rem(self.t + n - d, n) if arriving else self.t),
            send_sem=self.zs.at[d - 1],
            recv_sem=self.zr.at[d - 1],
            device_id=(self.me, lax.rem(self.t + d, n)),
            device_id_type=pl.DeviceIdType.MESH,
        )

    def across(self, r, j, arriving=False):
        bit, n = self.order[j], self.ids[(r, j)]
        block = self.me ^ r
        return pltpu.make_async_remote_copy(
            src_ref=self.spot(block, None),
            dst_ref=self.spot(block ^ bit if arriving else block, None),
            send_sem=self.ss.at[n],
            recv_sem=self.rs.at[n],
            device_id=(self.me ^ bit, self.t),
            device_id_type=pl.DeviceIdType.MESH,
        )

    def start(self):
        self.keep().start()
        for d in range(1, self.plan.tens):
            self.along(d).start()

    def arrived(self, r):
        if r == 0:
            self.keep().wait()
            for d in range(1, self.plan.tens):
                self.along(d, True).wait_recv()
        else:
            j = self.tops[r]
            self.across(r ^ self.order[j], j, True).wait_recv()

    def advance(self, stage):
        r = self.stages[stage]
        self.arrived(r)
        for j in self.sends[r]:
            self.across(r, j).start()

    def finish(self):
        for r in self.blocks:
            if not len(self.sends[r]):
                self.arrived(r)
        for d in range(1, self.plan.tens):
            self.along(d).wait_send()
        for r in self.blocks:
            for j in self.sends[r]:
                self.across(r, j).wait_send()


def schedule(items):
    pairs = [items[k : k + 2] for k in range(0, len(items), 2)]
    stages = len(items[0].stages)

    def step(s):
        for item in pairs[s : s + 1]:
            for one in item:
                one.start()
        for n, pair in enumerate(pairs):
            if 0 <= s - 1 - n < stages:
                for one in pair:
                    one.advance(s - 1 - n)

    def close():
        for item in items:
            item.finish()

    return [functools.partial(step, s) for s in range(len(pairs) + stages)] + [close]


class Route:
    def __init__(self, out, local, send, recv):
        self.out, self.local, self.send, self.recv = out, local, send, recv
        me, t = lax.axis_index("dp"), lax.axis_index("tensor")
        self.me, self.t = me, t
        core, high, low = lax.rem(me, 2), t // 2, lax.rem(t, 2)
        self.stays = core == high
        base = me - core
        self.peers = [(me ^ 1, t ^ 2), (base + high, 2 * core + 1 - low)]
        self.low = low

    def copy(self, f, src, out, arriving=False):
        if self.out:
            src, slot = src.at[self.low ^ f], f
        else:
            src, slot = src[f], self.low ^ f if arriving else self.low
        return pltpu.make_async_remote_copy(
            src_ref=src, dst_ref=out.at[slot], send_sem=self.send.at[f], recv_sem=self.recv.at[f],
            device_id=self.peers[f], device_id_type=pl.DeviceIdType.MESH,
        )

    def stay(self, blocks, out):
        if self.out:
            return pltpu.make_async_copy(blocks.at[self.low], out.at[0], self.local)
        return pltpu.make_async_copy(blocks[0], out.at[self.low], self.local)

    def start(self, blocks, out):
        self.copy(1, blocks, out).start()

        @pl.when(self.stays)
        def _():
            self.stay(blocks, out).start()

        @pl.when(jnp.logical_not(self.stays))
        def _():
            self.copy(0, blocks, out).start()

    def wait(self, blocks, out):
        @pl.when(self.stays)
        def _():
            self.stay(blocks, out).wait()

        @pl.when(jnp.logical_not(self.stays))
        def _():
            self.copy(0, blocks, out, True).wait_recv()
            self.copy(0, blocks, out).wait_send()

        self.copy(1, blocks, out, True).wait_recv()
        self.copy(1, blocks, out).wait_send()

    @staticmethod
    def semaphores():
        return [pltpu.SemaphoreType.DMA, pltpu.SemaphoreType.DMA((2,)), pltpu.SemaphoreType.DMA((2,))]


def at(ref, cut):
    return lambda a, t: ref.at[a, :, cut] if t is None else ref.at[a, t, cut]


class Pool:
    def __init__(self, plan, x_ref, o_ref, got, src, swap_send, swap_recv, *sems):
        me, t = lax.axis_index("dp"), lax.axis_index("tensor")
        self.mine = lax.rem(me, 2)
        self.x_ref, self.got, self.src = x_ref, got, src
        self.swap = pltpu.make_async_remote_copy(
            src_ref=x_ref.at[1 - self.mine], dst_ref=got, send_sem=swap_send, recv_sem=swap_recv,
            device_id=(me ^ 1, t), device_id_type=pl.DeviceIdType.MESH,
        )
        cuts = src.shape[0]
        self.items = [Item(plan, sems, k, src.at[pl.ds(k, 1)], at(o_ref, pl.ds(k, 1)), k % 2) for k in range(cuts)]
        steps = schedule(self.items)
        self.steps = [self.swap.start, functools.partial(self.add, steps[0])] + steps[1:]

    def add(self, then):
        self.swap.wait()
        self.src[...] = (self.x_ref[self.mine].astype(F32) + self.got[...].astype(F32)).astype(BF16)
        then()

    @staticmethod
    def scratch(plan, shape):
        return [pltpu.VMEM(shape, BF16), pltpu.VMEM(shape, BF16), pltpu.SemaphoreType.DMA, pltpu.SemaphoreType.DMA
                ] + plan.semaphores(shape[0])


def share_kernel(plan, x_ref, o_ref, *scratch):
    plan.greet()
    for step in Pool(plan, x_ref, o_ref, *scratch).steps:
        step()


def share(plan, dps, x, number):
    return pl.pallas_call(
        functools.partial(share_kernel, plan),
        in_specs=[pl.BlockSpec(memory_space=pltpu.VMEM)],
        out_specs=pl.BlockSpec(memory_space=pl.ANY),
        out_shape=jax.ShapeDtypeStruct((dps, plan.tens) + x.shape[1:], BF16),
        scratch_shapes=Pool.scratch(plan, x.shape[1:]),
        compiler_params=pltpu.CompilerParams(collective_id=number, has_side_effects=True),
        name="share",
    )(x)


def intro_kernel(
    plan, info, tok_ref, codes_ref, gain_ref, w_ref, wo_ref, w1_ref, w2_ref, down_ref, up_ref,
    x_ref, q_ref, kv_ref, kv2_ref, low_ref, codes_out, w_out, wo_out, w1_out, w2_out,
    x_s, w_s, n_s, kv_s, keep_sem, kv_send, kv_recv, r_local, r_send, r_recv, *sems,
):
    half, depth = x_ref.shape[1:]
    tens, width = plan.tens, w_ref.shape[2]
    me, t = lax.axis_index("dp"), lax.axis_index("tensor")
    sems_w, sems = sems[:5], sems[5:]
    cuts = sems_w[0].shape[0]
    size = w_ref.shape[0] // cuts
    first = [Item(plan, sems_w, k, w_ref.at[pl.ds(k * size, size)], at(w_s, pl.ds(k * size, size)), k % 2) for k in range(cuts)]
    rest = []
    for pairs in (((codes_ref, codes_out),), ((wo_ref, wo_out),), ((w1_ref, w1_out), (w2_ref, w2_out))):
        for k in range(pairs[0][0].shape[0]):
            for src, out in pairs:
                rest.append((src.at[pl.ds(k, 1)], at(out, pl.ds(k, 1))))
    rest = rest[1:] + rest[:1]
    rest = [Item(plan, sems, n, src, spot, n % 2) for n, (src, spot) in enumerate(rest)]
    later = schedule(rest)
    route = Route(True, r_local, r_send, r_recv)
    e = info[0]

    plan.greet(route.peers)
    for item in first:
        item.start()
    route.start(tok_ref, x_s)
    stages = len(first[0].stages)
    for s in range(cuts // 2 + stages - 1):
        for n in range(cuts // 2):
            if 0 <= s - n < stages:
                first[2 * n].advance(s - n)
                first[2 * n + 1].advance(s - n)
    route.wait(tok_ref, x_s)
    later[0]()
    x_ref[...] = x_s[...]
    for part in range(2):
        normed, _ = norm_parts(x_s[part].astype(F32))
        n_s[part * half : (part + 1) * half, :] = normed * gain_ref[...]
    n = n_s[...].astype(BF16)
    low = mm_nt(n, down_ref[e])
    low_ref[...] = low
    low = low.astype(BF16)
    for item in first:
        item.finish()
    keep = pltpu.make_async_copy(w_s, w_out, keep_sem)
    keep.start()
    swap = pltpu.make_async_remote_copy(
        src_ref=kv_s, dst_ref=kv2_ref, send_sem=kv_send, recv_sem=kv_recv,
        device_id=(me ^ 1, t), device_id_type=pl.DeviceIdType.MESH,
    )
    blocks = w_ref.shape[0] // 3
    for turn, j in enumerate((1, 2, 0)):
        later[turn + 1]()
        for c in range(tens):
            cols = slice(c * width, (c + 1) * width)
            w = w_s[:, c, j * blocks : (j + 1) * blocks].reshape(depth, width)
            res = (mm(n, w) + mm(low, up_ref[e, j, :, cols])).astype(BF16)
            if j == 0:
                q_ref[:, cols] = res
            else:
                kv_s[j - 1, :, cols] = res
        if j == 2:
            swap.start()
            kv_ref[...] = kv_s[...]
    for one in later[4:]:
        one()
    swap.wait()
    keep.wait()


def intro(plan, dps, info, tokens, codes, gain, w, wo, w1, w2, down, up, cuts, number):
    _, half, depth = tokens.shape
    rows, rank = 2 * half, down.shape[1]
    hbm, vm = pl.BlockSpec(memory_space=pl.ANY), pl.BlockSpec(memory_space=pltpu.VMEM)
    big = lambda x: jax.ShapeDtypeStruct((dps, plan.tens) + x.shape, x.dtype)
    items = codes.shape[0] + wo.shape[0] + 2 * w1.shape[0]
    return pl.pallas_call(
        functools.partial(intro_kernel, plan),
        in_specs=[pl.BlockSpec(memory_space=pltpu.SMEM), hbm, hbm, vm, hbm, hbm, hbm, hbm, vm, vm],
        out_specs=[vm, vm, vm, hbm, vm] + [hbm] * 5,
        out_shape=[
            jax.ShapeDtypeStruct(tokens.shape, BF16),
            jax.ShapeDtypeStruct((rows, depth), BF16),
            jax.ShapeDtypeStruct((2, rows, depth), BF16),
            jax.ShapeDtypeStruct((2, rows, depth), BF16),
            jax.ShapeDtypeStruct((rows, rank), F32),
            big(codes), big(w), big(wo), big(w1), big(w2),
        ],
        scratch_shapes=[
            pltpu.VMEM(tokens.shape, BF16), pltpu.VMEM((dps, plan.tens) + w.shape, BF16), pltpu.VMEM((rows, depth), F32),
            pltpu.VMEM((2, rows, depth), BF16),
        ]
        + [pltpu.SemaphoreType.DMA] * 3
        + Route.semaphores() + plan.semaphores(cuts) + plan.semaphores(items),
        compiler_params=pltpu.CompilerParams(
            vmem_limit_bytes=VMEM_BYTES, collective_id=number, has_side_effects=True
        ),
        name="intro",
    )(info, tokens, codes, gain, w, wo, w1, w2, down, up)


def attend_pair(q2, ks, vs, shifted):
    lane = lax.broadcasted_iota(jnp.int32, (1, 128), 1)
    outs, lses = [], []
    for h in range(2):
        mine = (lane // HEAD_DIM) == h
        s = mm_nt(jnp.where(mine, q2, BF16(0)), ks[...])
        if shifted:
            m = jnp.max(s, axis=1, keepdims=True)
            p = jnp.exp(s - m).astype(BF16)
        else:
            p = jnp.exp(s).astype(BF16)
        o = mm(p, vs[h])
        total = pltpu.roll(o, HEAD_DIM, 1)
        outs.append(o / total)
        lse = jnp.log(jnp.where(mine, total, o))
        lses.append(lse + m if shifted else lse)
    return (
        jnp.where(lane < HEAD_DIM, outs[0], outs[1]).astype(BF16),
        jnp.where(lane < HEAD_DIM, lses[0], lses[1]),
    )


def stage_keys(k_ref, v_ref, k2_ref, v2_ref, ks, vs):
    rows = k_ref.shape[1]
    lane = lax.broadcasted_iota(jnp.int32, (1, 128), 1)
    ks[0:rows, :] = k_ref[0]
    ks[rows:, :] = k2_ref[0]
    for h in range(2):
        mine = (lane // HEAD_DIM) == h
        vs[h, 0:rows, :] = jnp.where(mine, v_ref[0], BF16(1))
        vs[h, rows:, :] = jnp.where(mine, v2_ref[0], BF16(1))


def attend_kernel(q_ref, k_ref, v_ref, k2_ref, v2_ref, o_ref, lse_ref, ks, vs):
    stage_keys(k_ref, v_ref, k2_ref, v2_ref, ks, vs)
    q2 = q_ref[...] * BF16(HEAD_DIM ** -0.5)
    lane = lax.broadcasted_iota(jnp.int32, (1, 128), 1)
    qf, kf = q2.astype(F32), ks[...].astype(F32)
    safe = True
    for h in range(2):
        mine = (lane // HEAD_DIM) == h
        far = lambda x: jnp.max(jnp.sum(jnp.where(mine, x * x, 0.0), axis=1, keepdims=True))
        safe = jnp.logical_and(safe, far(qf) * far(kf) <= SAFE_SCORE * SAFE_SCORE)

    @pl.when(safe)
    def _():
        o_ref[...], lse_ref[...] = attend_pair(q2, ks, vs, False)

    @pl.when(jnp.logical_not(safe))
    def _():
        o_ref[...], lse_ref[...] = attend_pair(q2, ks, vs, True)


def attend(q, kv, kv2):
    rows, depth = q.shape
    flat = pl.BlockSpec((rows, 128), lambda i: (0, i))
    part = lambda j: pl.BlockSpec((1, rows, 128), lambda i: (j, 0, i))
    return pl.pallas_call(
        attend_kernel,
        grid=(depth // 128,),
        in_specs=[flat, part(0), part(1), part(0), part(1)],
        out_specs=[flat, flat],
        out_shape=[jax.ShapeDtypeStruct((rows, depth), BF16), jax.ShapeDtypeStruct((rows, depth), F32)],
        scratch_shapes=[pltpu.VMEM((2 * rows, 128), BF16), pltpu.VMEM((2, 2 * rows, 128), BF16)],
        compiler_params=params(),
        name="attend",
    )(q, kv, kv, kv2, kv2)


def gelu_both(x):
    cdf = 0.5 * (1.0 + lax.erf(x * (2.0 ** -0.5)))
    pdf = jnp.exp(-0.5 * x * x) * ((2.0 * math.pi) ** -0.5)
    return x * cdf, cdf + x * pdf


def feed_kernel(
    plan, info, xa_ref, xb_ref, ca_ref, cb_ref, ctx_ref, gain_ref, wo_ref, w1_ref, w2_ref, w1_src, w2_src,
    od_ref, ou_ref, d1_ref, u1_ref, d2_ref, u2_ref,
    la_ref, lb_ref, gm_ref, gctx_ref, grads_ref,
    wo_s, w1_s, w2_s, mid_s, n_s, gf_s, feed_s, gn_s, lowo_s, low1_s, low2_s, b1_s, b2_s, *late,
):
    half, depth = xa_ref.shape
    rows = 2 * half
    step, last = pl.program_id(0), pl.num_programs(0) - 1
    e, live = info[0], info[1].astype(F32)
    dp, tens, wop, wor, woc = wo_ref.shape
    fp, fr, fc = w1_ref.shape[2:]
    wide = fp * fc
    if late:
        w1_late, w2_late, *sems = late
        items = []
        for k in range(w1_src.shape[0]):
            for src, out in ((w1_src, w1_late), (w2_src, w2_late)):
                cut = pl.ds(k, 1)
                items.append(Item(plan, sems, len(items), src.at[cut], at(out, cut), len(items) % 2))
        steps = schedule(items)
        before = {0: 0, 2: 1, 3: 2, 4: 3, 5: 4, 6: 5, 7: 6}

    def put(unit, cols, value):
        per = grads_ref.shape[3] // depth
        cuts = grads_ref.shape[1]
        spot = (unit % per) * depth + cols
        if not isinstance(spot, int):
            spot = pl.multiple_of(spot, 128)
        grads_ref[unit // (per * cuts), unit // per % cuts, :, pl.ds(spot, value.shape[1])] = value.astype(BF16)

    if late:
        pl.when(step == 0)(plan.greet)
        for n, when in before.items():
            pl.when(step == when)(steps[n])
        for n in range(len(items) // 2):
            @pl.when(step == tens + n)
            def _():
                items[2 * n].finish()
                items[2 * n + 1].finish()

    @pl.when(step == 0)
    def _():
        for a in range(dp):
            for t in range(tens):
                for k in range(wop):
                    row = (t * wop + k) * wor
                    wo_s[row : row + wor, a * woc : (a + 1) * woc] = wo_ref[a, t, k]
        ctx = ctx_ref[...]
        low = mm_nt(ctx, od_ref[e])
        lowo_s[...] = low
        attention = mm(ctx, wo_s[...]) + mm(low.astype(BF16), ou_ref[e])
        for part, ref in enumerate((xa_ref, xb_ref)):
            s = slice(part * half, (part + 1) * half)
            mid_s[s, :] = ref[...].astype(F32) + attention[s, :]
        for part, ref in enumerate((ca_ref, cb_ref)):
            s = slice(part * half, (part + 1) * half)
            gm_ref[s, :] = ref[...].astype(F32) * live
        gf_s[...] = gm_ref[...].astype(BF16)
        normed, _ = norm_parts(mid_s[...])
        n_s[...] = (normed * gain_ref[...]).astype(BF16)
        low1_s[...] = mm_nt(n_s[...], d1_ref[e])
        b2_s[...] = mm_nt(gf_s[...], u2_ref[e])
        feed_s[...] = jnp.zeros_like(feed_s)
        gn_s[...] = jnp.zeros_like(gn_s)
        low2_s[...] = jnp.zeros_like(low2_s)
        b1_s[...] = jnp.zeros_like(b1_s)

    def stage(take_1, take_2):
        for a in range(dp):
            for k in range(fp):
                w1_s[a * fr : (a + 1) * fr, k * fc : (k + 1) * fc] = take_1(a, k)
                w2_s[k * fr : (k + 1) * fr, a * woc : (a + 1) * woc] = take_2(a, k)

    if late:
        @pl.when(step < tens)
        def _():
            stage(lambda a, k: w1_ref[a, 0, k], lambda a, k: w2_ref[a, 0, k])

        @pl.when(step >= tens)
        def _():
            part = step - tens
            stage(lambda a, k: w1_late[a, k, part], lambda a, k: w2_late[a, k, part])
    else:
        stage(lambda a, k: w1_ref[a, 0, k], lambda a, k: w2_ref[a, 0, k])

    w1, w2 = w1_s[...], w2_s[...]
    if late:
        early_step = step < tens
        runs = [
            pl.multiple_of(jnp.where(early_step, step * 2 * wide + k * fc, (2 * k + 1) * wide + (step - tens) * fc), fc)
            for k in range(fp)
        ]
        u1 = jnp.concatenate([u1_ref[e, :, pl.ds(run, fc)] for run in runs], axis=1)
        d2 = jnp.concatenate([d2_ref[e, :, pl.ds(run, fc)] for run in runs], axis=1)
    else:
        u1, d2 = u1_ref[e], d2_ref[e]
    n, gf = n_s[...], gf_s[...]
    low1, b2 = low1_s[...].astype(BF16), b2_s[...].astype(BF16)
    preact = mm(n, w1) + mm(low1, u1)
    ghid = mm_nt(gf, w2) + mm(b2, d2)
    if late:
        pl.when(step == 0)(steps[1])
    hid, slope = gelu_both(preact)
    hid = hid.astype(BF16)
    gpre = (ghid * slope).astype(BF16)
    feed_s[...] += mm(hid, w2)
    gn_s[...] += mm_nt(gpre, w1)
    low2_s[...] += mm_nt(hid, d2)
    b1_s[...] += mm_nt(gpre, u1)
    gu1, gd2 = mm_tn(low1, gpre), mm_tn(b2, hid)
    if late:
        for k, run in enumerate(runs):
            cols = slice(k * fc, (k + 1) * fc)
            put(4 + run // depth, lax.rem(run, depth), gu1[:, cols])
            put(4 + tens + run // depth, lax.rem(run, depth), gd2[:, cols])
    else:
        t, part = lax.rem(step, tens), step // tens
        put(4 + t, part * wide, gu1)
        put(4 + tens + t, part * wide, gd2)

    @pl.when(step == last)
    def _():
        low2, b1 = low2_s[...].astype(BF16), b1_s[...].astype(BF16)
        out = live * (mid_s[...] + feed_s[...] + mm(low2, u2_ref[e]))
        la_ref[...] = out[:half].astype(BF16)
        lb_ref[...] = out[half:].astype(BF16)
        put(3, 0, mm_tn(low2, gf_s[...]))
        gn = gn_s[...] + mm(b1, d1_ref[e])
        normed, scale = norm_parts(mid_s[...])
        put(2, 0, mm_tn(b1, n_s[...]))
        gm = gm_ref[...] + norm_back(normed, scale, gain_ref[...], gn)
        gm_ref[...] = gm
        ga = gm.astype(BF16)
        back = mm_nt(ga, ou_ref[e]).astype(BF16)
        gctx_ref[...] = (mm_nt(ga, wo_s[...]) + mm(back, od_ref[e])).astype(BF16)
        put(0, 0, mm_tn(back, ctx_ref[...]))
        put(1, 0, mm_tn(lowo_s[...].astype(BF16), ga))


def feed_forward(plan, info, xa, xb, ca, cb, ctx, gain, wo, w1, w2, late, od, ou, d1, u1, d2, u2, number):
    half, depth = xa.shape
    rows = 2 * half
    adapters, rank = od.shape[:2]
    dp, tens, wop, wor, woc = wo.shape
    fp, fr, fc = w1.shape[2:]
    fp = fp if late else fp // 2
    wide = fp * fc
    ff = 2 * wide * tens
    once = lambda *shape: pl.BlockSpec(shape, lambda f: (0,) * len(shape), pipeline_mode=pl.Buffered(1))
    whole = lambda *shape: pl.BlockSpec(shape, lambda f: (0,) * len(shape))
    table = once(adapters, rank, depth)
    if late:
        assert late[0].shape[0] == tens == fp
        table_f = once(adapters, rank, ff)
    else:
        table_f = pl.BlockSpec((adapters, rank, wide), lambda f: (0, 0, f % tens * 2 + f // tens))
    if late:
        place = lambda f: (0, jnp.minimum(f, tens - 1), 0, 0, 0)
    else:
        place = lambda f: (0, f % tens, f // tens, 0, 0)
    units = 4 + 2 * ff // depth
    cuts = 2
    hbm = pl.BlockSpec(memory_space=pl.ANY)
    scratch = [
        pltpu.VMEM((depth, depth), BF16),
        pltpu.VMEM((depth, wide), BF16),
        pltpu.VMEM((wide, depth), BF16),
        pltpu.VMEM((rows, depth), F32),
        pltpu.VMEM((rows, depth), BF16),
        pltpu.VMEM((rows, depth), BF16),
        pltpu.VMEM((rows, depth), F32),
        pltpu.VMEM((rows, depth), F32),
    ] + [pltpu.VMEM((rows, rank), F32)] * 5
    extra = {}
    if late:
        scratch += [pltpu.VMEM((dp, tens) + part.shape, BF16) for part in late]
        scratch += plan.semaphores(2 * late[0].shape[0])
        extra = dict(collective_id=number, has_side_effects=True)
    else:
        late = [jnp.zeros((16, 128), BF16)] * 2
    return pl.pallas_call(
        functools.partial(feed_kernel, plan),
        grid=(2 * tens,),
        in_specs=[
            pl.BlockSpec(memory_space=pltpu.SMEM),
            once(half, depth), once(half, depth), once(half, depth), once(half, depth),
            once(rows, depth),
            whole(1, depth),
            once(dp, tens, wop, wor, woc),
            pl.BlockSpec((dp, 1, fp, fr, fc), place),
            pl.BlockSpec((dp, 1, fp, fr, woc), place),
            hbm, hbm,
            table, table, table, table_f, table_f, table,
        ],
        out_specs=[
            whole(half, depth), whole(half, depth), whole(rows, depth), whole(rows, depth),
            whole(2, cuts, rank, units * depth // (2 * cuts)),
        ],
        scratch_shapes=scratch,
        out_shape=[
            jax.ShapeDtypeStruct((half, depth), BF16),
            jax.ShapeDtypeStruct((half, depth), BF16),
            jax.ShapeDtypeStruct((rows, depth), F32),
            jax.ShapeDtypeStruct((rows, depth), BF16),
            jax.ShapeDtypeStruct((2, cuts, rank, units * depth // (2 * cuts)), BF16),
        ],
        compiler_params=pltpu.CompilerParams(vmem_limit_bytes=VMEM_BYTES, **extra),
        name="feed_forward",
    )(info, xa, xb, ca, cb, ctx, gain, wo, w1, w2, late[0], late[1], od, ou, d1, u1, d2, u2)


def split3(x):
    hi = x.astype(BF16)
    rest = x - hi.astype(F32)
    mid = rest.astype(BF16)
    return hi, mid, (rest - mid.astype(F32)).astype(BF16)


def attend_back_kernel(
    plan, q_ref, k_ref, v_ref, k2_ref, v2_ref, g_ref, o_ref, lse_ref, la_ref, lb_ref, grads_ref,
    dq_ref, dkv_ref, far_ref, lo_ref, early_ref,
    ks, vs, kd, acc, far_s, far_send, far_recv, lo_local, lo_send, lo_recv, *pool,
):
    rows = q_ref.shape[0]
    step, steps = pl.program_id(0), pl.num_programs(0)
    me, t = lax.axis_index("dp"), lax.axis_index("tensor")
    route = Route(False, lo_local, lo_send, lo_recv)
    early = Pool(plan, grads_ref, early_ref, *pool).steps
    blocks = (la_ref, lb_ref)

    @pl.when(step == 0)
    def _():
        plan.greet(route.peers)

    for n, one in zip((0, 1, 3, 5, 6, 7), early[:-1]):
        @pl.when(step == n)
        def _():
            one()

    @pl.when(step == 3)
    def _():
        route.start(blocks, lo_ref)

    def far(n):
        return pltpu.make_async_remote_copy(
            src_ref=far_s.at[lax.rem(n, 2)],
            dst_ref=far_ref.at[:, :, pl.ds(pl.multiple_of(n * 128, 128), 128)],
            send_sem=far_send.at[n], recv_sem=far_recv.at[n],
            device_id=(me ^ 1, t), device_id_type=pl.DeviceIdType.MESH,
        )

    zero = BF16(0)
    lane = lax.broadcasted_iota(jnp.int32, (1, 128), 1)
    scale = BF16(HEAD_DIM ** -0.5)
    q2 = q_ref[...] * scale
    g2 = g_ref[...]
    hi, mid, lo = split3(pltpu.roll(lse_ref[...], HEAD_DIM, 1))
    prod = g2.astype(F32) * o_ref[...].astype(F32)
    qa, ga, qm, gm = [], [], [], []
    for h in range(2):
        mine, b = (lane // HEAD_DIM) == h, HEAD_DIM * (1 - h)
        qa.append(
            jnp.where(mine, q2, jnp.where(lane == b, -hi, jnp.where(lane == b + 1, -mid, jnp.where(lane == b + 2, -lo, zero))))
        )
        dh, dm, dl = split3(jnp.sum(jnp.where(mine, prod, 0.0), axis=1, keepdims=True))
        ga.append(
            jnp.where(mine, g2, jnp.where(lane == b, -dh, jnp.where(lane == b + 1, -dm, jnp.where(lane == b + 2, -dl, zero))))
        )
        qm.append(jnp.where(mine, q2, zero))
        gm.append(jnp.where(mine, g2, zero))
        ones = ((lane >= b) & (lane < b + 3)).astype(BF16)
        for i, (kr, vr) in enumerate(((k_ref, v_ref), (k2_ref, v2_ref))):
            s = slice(i * rows, (i + 1) * rows)
            ks[h, s, :] = jnp.where(mine, kr[0], ones)
            vs[h, s, :] = jnp.where(mine, vr[0], ones)
            kd[h, s, :] = jnp.where(mine, kr[0] * scale, zero)
    @pl.when(step >= 2)
    def _():
        far(step - 2).wait_send()

    slot = lax.rem(step, 2)
    for i in range(2):
        s = slice((1 - i) * rows, (2 - i) * rows)
        dk = jnp.zeros((rows, 128), F32)
        dv = jnp.zeros((rows, 128), F32)
        dq = jnp.zeros((rows, 128), F32)
        for h in range(2):
            p = jnp.exp(mm_nt(ks[h, s, :], qa[h]))
            ds = (p * mm_nt(vs[h, s, :], ga[h])).astype(BF16)
            dv = dv + mm(p.astype(BF16), gm[h])
            dk = dk + mm(ds, qm[h])
            dq = dq + mm_tn(ds, kd[h, s, :])
        if i == 0:
            far_s[slot, 0] = dk.astype(BF16)
            far_s[slot, 1] = dv.astype(BF16)
            far(step).start()
            acc[...] = dq
        else:
            dkv_ref[0] = dk.astype(BF16)
            dkv_ref[1] = dv.astype(BF16)
            dq_ref[...] = (acc[...] + dq).astype(BF16)

    @pl.when(step == steps - 1)
    def _():
        early[-1]()
        route.wait(blocks, lo_ref)
        far(step - 1).wait_send()
        far(step).wait_send()
        lax.fori_loop(0, steps, lambda n, c: (far(n).wait_recv(), c)[1], 0)


def attend_back(plan, dps, q, kv, kv2, g, ctx, lse, la, lb, grads, number):
    rows, depth = q.shape
    flat = pl.BlockSpec((rows, 128), lambda i: (0, i))
    part = lambda j: pl.BlockSpec((1, rows, 128), lambda i: (j, 0, i))
    both = pl.BlockSpec((2, rows, 128), lambda i: (0, 0, i))
    hbm = pl.BlockSpec(memory_space=pl.ANY)
    heads = depth // 128
    dma = lambda *shape: pltpu.SemaphoreType.DMA(shape)
    return pl.pallas_call(
        functools.partial(attend_back_kernel, plan),
        grid=(heads,),
        in_specs=[flat, part(0), part(1), part(0), part(1), flat, flat, flat, hbm, hbm,
                  pl.BlockSpec(grads.shape, lambda i: (0, 0, 0, 0), pipeline_mode=pl.Buffered(1))],
        out_specs=[flat, both, hbm, hbm, hbm],
        out_shape=[
            jax.ShapeDtypeStruct((rows, depth), BF16),
            jax.ShapeDtypeStruct((2, rows, depth), BF16),
            jax.ShapeDtypeStruct((2, rows, depth), BF16),
            jax.ShapeDtypeStruct((2,) + la.shape, BF16),
            jax.ShapeDtypeStruct((dps, plan.tens) + grads.shape[1:], BF16),
        ],
        scratch_shapes=[pltpu.VMEM((2, 2 * rows, 128), BF16)] * 3
        + [pltpu.VMEM((rows, 128), F32), pltpu.VMEM((2, 2, rows, 128), BF16), dma(heads), dma(heads),
           *Route.semaphores()]
        + Pool.scratch(plan, grads.shape[1:]),
        compiler_params=pltpu.CompilerParams(
            vmem_limit_bytes=VMEM_BYTES, collective_id=number, has_side_effects=True
        ),
        name="attend_back",
    )(q, kv, kv, kv2, kv2, g, ctx, lse, la, lb, grads)


def qkv_back_kernel(
    info, xa_ref, xb_ref, gain_ref, dq_ref, dkv_ref, dkv2_ref, gm_ref, low_ref, w_ref, down_ref, up_ref,
    ya_ref, yb_ref, g_down, g_up, gn_s, back_s,
):
    half, depth = xa_ref.shape
    parts, width = w_ref.shape[1], w_ref.shape[4]
    step, last = pl.program_id(0), pl.num_programs(0) - 1

    def go(g, first):
        back = mm_nt(g, up_ref[0, 0])
        total = back if first else back_s[...] + back
        back_s[...] = total
        acc = None if first else gn_s[...]
        for part in range(parts):
            cols = slice(part * width, (part + 1) * width)
            term = mm_nt(g[:, cols], w_ref[:, part, 0].reshape(depth, width))
            acc = term if acc is None else acc + term
        gn_s[...] = acc
        g_up[0] = mm_tn(low_ref[...].astype(BF16), g)

    @pl.when(step == 0)
    def _():
        go(dq_ref[...], True)

    @pl.when(step > 0)
    def _():
        go((dkv_ref[0].astype(F32) + dkv2_ref[0].astype(F32)).astype(BF16), False)

    @pl.when(step == last)
    def _():
        back = back_s[...].astype(BF16)
        gn_s[...] += mm(back, down_ref[0])
        total = jnp.zeros(g_down.shape, F32)
        for part, (x_ref, y_ref) in enumerate(((xa_ref, ya_ref), (xb_ref, yb_ref))):
            s = slice(part * half, (part + 1) * half)
            normed, scale = norm_parts(x_ref[...].astype(F32))
            total = total + mm_tn(back_s[s, :].astype(BF16), (normed * gain_ref[...]).astype(BF16))
            y_ref[...] = (gm_ref[s, :] + norm_back(normed, scale, gain_ref[...], gn_s[s, :])).astype(BF16)
        g_down[...] = total


def project_back(info, xa, xb, gain, dq, dkv, dkv2, gm, low, w, down, up):
    half, depth = xa.shape
    rows = 2 * half
    rank = down.shape[1]
    dp, tens, _, wr, wc = w.shape
    whole = lambda *shape: pl.BlockSpec(shape, lambda j, info: (0,) * len(shape))
    once = lambda *shape: pl.BlockSpec(shape, lambda j, info: (0,) * len(shape), pipeline_mode=pl.Buffered(1))
    pair = pl.BlockSpec((1, rows, depth), lambda j, info: (jnp.maximum(j - 1, 0), 0, 0))
    return pl.pallas_call(
        qkv_back_kernel,
        grid_spec=pltpu.PrefetchScalarGridSpec(
            num_scalar_prefetch=1,
            grid=(3,),
            in_specs=[
                once(half, depth), once(half, depth), whole(1, depth),
                once(rows, depth), pair, pair,
                once(rows, depth), once(rows, rank),
                pl.BlockSpec((dp, tens, 1, wr, wc), lambda j, info: (0, 0, j, 0, 0)),
                pl.BlockSpec((1, rank, depth), lambda j, info: (info[0], 0, 0)),
                pl.BlockSpec((1, 1, rank, depth), lambda j, info: (info[0], j, 0, 0)),
            ],
            out_specs=[
                whole(half, depth), whole(half, depth), whole(rank, depth),
                pl.BlockSpec((1, rank, depth), lambda j, info: (j, 0, 0)),
            ],
            scratch_shapes=[pltpu.VMEM((rows, depth), F32), pltpu.VMEM((rows, rank), F32)],
        ),
        out_shape=[
            jax.ShapeDtypeStruct((half, depth), BF16),
            jax.ShapeDtypeStruct((half, depth), BF16),
            jax.ShapeDtypeStruct((rank, depth), F32),
            jax.ShapeDtypeStruct((3, rank, depth), F32),
        ],
        compiler_params=params(),
        name="project_back",
    )(info, xa, xb, gain, dq, dkv, dkv2, gm, low, w, down, up)


def table_kernel(places, unit, owner, g_ref, *outs):
    _, _, tens, cuts, _, width = g_ref.shape
    pair, per = pl.program_id(0), width // unit

    @pl.when(pair == 0)
    def _():
        for out in outs:
            out[...] = jnp.zeros_like(out)

    for t in range(tens):
        e = owner[pair * tens + t]
        for n, (out, sub, start) in enumerate(places):
            col = n % per * unit
            piece = g_ref[0, n // (per * cuts), t, n // per % cuts, :, col : col + unit].astype(F32)
            if sub is None:
                outs[out][e, :, start : start + unit] += piece
            else:
                outs[out][e, sub, :, start : start + unit] += piece


def tables(owner, gathered, outs, places, unit):
    dps = gathered.shape[0]
    gathered = gathered.reshape((dps // 2, 2) + gathered.shape[1:])
    block = (1,) + gathered.shape[1:]
    return pl.pallas_call(
        functools.partial(table_kernel, places, unit),
        grid_spec=pltpu.PrefetchScalarGridSpec(
            num_scalar_prefetch=1,
            grid=(dps // 2,),
            in_specs=[pl.BlockSpec(block, lambda p, owner: (p, 0, 0, 0, 0, 0))],
            out_specs=[pl.BlockSpec(shape, lambda p, owner, n=len(shape): (0,) * n) for shape in outs],
        ),
        out_shape=[jax.ShapeDtypeStruct(shape, F32) for shape in outs],
        compiler_params=params(),
        name="tables",
    )(owner, gathered)


def per_device(
    tokens, cotangent, clip_live, adapter_index, gain_one, gain_two, weight_qkv, weight_out, weight_fc1, weight_fc2,
    qkv_down, qkv_up, out_down, out_up, fc1_down, fc1_up, fc2_down, fc2_up,
):
    dps, tens = lax.axis_size("dp"), lax.axis_size("tensor")
    slots = tokens.shape[0]
    axes = ("dp", "tensor")
    dp, t = lax.axis_index("dp"), lax.axis_index("tensor")
    assert slots == 2 and tens == 4 and dps % 2 == 0

    def route(flip):
        perm = []
        for a in range(dps):
            for b in range(tens):
                slot = (b % 2) ^ flip
                perm.append((a * tens + b, (a - a % 2 + b // 2) * tens + 2 * (a % 2) + slot))
        return perm

    routes = [route(0), route(1)]
    swap = [(a * tens + b, (a ^ 1) * tens + b) for a in range(dps) for b in range(tens)]
    back_routes = [[(d, s) for s, d in r] for r in routes]

    def spread(field):
        parts = []
        for flip in range(2):
            slot = (t % 2) ^ flip
            parts.append(lax.ppermute(lax.dynamic_index_in_dim(field, slot, 0, False), axes, routes[flip]))
        return parts

    def unspread(parts):
        got = [lax.ppermute(part, axes, r) for part, r in zip(parts, back_routes)]
        return jnp.where(t % 2 == 0, jnp.stack(got), jnp.stack(got[::-1]))

    both = jnp.stack([adapter_index, clip_live], axis=1)
    other = lax.ppermute(both, axes, swap)
    info = jnp.where(t // 2 == dp % 2, both, other)
    info = lax.dynamic_index_in_dim(info, t % 2, 0, False)
    codes = jnp.broadcast_to(adapter_index.reshape(1, 1, 2, 1), (1, 4, 2, 128)).reshape(1, 8, 128)

    def fold(w, dim):
        k = max(1, 128 // w.shape[dim])
        if k == 1:
            return w
        w = jnp.moveaxis(w.reshape((dps // k, k) + w.shape[1:]), 1, dim)
        return w.reshape(w.shape[:dim] + (-1,) + w.shape[dim + 2 :])

    plan = Plan(dps, tens)
    g1, g2 = gain_one.reshape(1, -1), gain_two.reshape(1, -1)
    parts_q = weight_qkv.reshape(-1, 16, weight_qkv.shape[2])
    in_rows = weight_fc1.shape[0]
    parts_1 = weight_fc1.reshape(in_rows, -1, 128).transpose(1, 0, 2)
    parts_2 = weight_fc2.reshape(parts_1.shape[0], -1, weight_fc2.shape[1])
    parts_o = weight_out.reshape(2, -1, weight_out.shape[1])
    late, fine = [], 2
    if dps <= 8:
        fine, n = 8, parts_1.shape[0] // 2
        late = [parts_1[n:], parts_2[n:]]
        parts_1, parts_2 = parts_1[:n], parts_2[:n]
    x, q, kv, kv2, low, codes, w_qkv, w_out, w_fc1, w_fc2 = intro(
        plan, dps, info, tokens, codes, g1, parts_q, parts_o, parts_1, parts_2, qkv_down, qkv_up, fine, 0
    )
    owner = codes[:, 0, 0, :2, 0].reshape(-1)
    xa, xb = x[0], x[1]
    w_qkv = fold(w_qkv.reshape((dps, tens) + weight_qkv.shape), 3)
    cotangent, q = lax.optimization_barrier((cotangent, q))
    ca, cb = spread(cotangent)
    ctx, lse = attend(q, kv, kv2)
    w_out, w_fc1, w_fc2 = fold(w_out, 4), fold(w_fc1, 3), fold(w_fc2, 4)
    la, lb, gm, gctx, grads = feed_forward(
        plan, info, xa, xb, ca, cb, ctx, g2, w_out, w_fc1, w_fc2, late,
        out_down, out_up, fc1_down, fc1_up, fc2_down, fc2_up, 2,
    )
    dq, dkv, dkv2, layer_out, early = attend_back(plan, dps, q, kv, kv2, gctx, ctx, lse, la, lb, grads, 3)
    depth, ff = out_down.shape[2], fc1_up.shape[2]
    t_od, t_ou, t_d1, t_u2, t_u1, t_d2 = tables(
        owner, early, [a.shape for a in (out_down, out_up, fc1_down, fc2_up, fc1_up, fc2_down)],
        [(n, None, 0) for n in range(4)] + [(n, None, c) for n in (4, 5) for c in range(0, ff, depth)], depth,
    )
    ya, yb, g_qd, g_qu = project_back(info, xa, xb, g1, dq, dkv, dkv2, gm, low, w_qkv, qkv_down, qkv_up)
    grads = jnp.concatenate([g_qd[None], g_qu]).astype(BF16)
    late_grads = share(plan, dps, grads.reshape((2, 2) + grads.shape[1:]), 4)
    grad_tokens = unspread([ya, yb])
    t_qd, t_qu = tables(
        owner, late_grads, [qkv_down.shape, qkv_up.shape], [(0, None, 0)] + [(1, j, 0) for j in range(3)], depth
    )
    return layer_out, grad_tokens, t_qd, t_qu, t_od, t_ou, t_d1, t_u1, t_d2, t_u2


def solution(mesh):
    rows, whole = P("dp", "tensor", None), P()
    return jax.shard_map(
        per_device,
        mesh=mesh,
        in_specs=(rows, rows, P("dp"), P("dp"), whole, whole, P(None, "dp", "tensor"), P("tensor", "dp"),
                  P("dp", "tensor"), P("tensor", "dp")) + (whole,) * 8,
        out_specs=(rows, rows) + (whole,) * 8,
        check_vma=False,
    )
```

time: 546 us -> 450 us (0.82)
  waiting for transfers between devices: 28.9 us -> 0.01 us
  starting transfers between devices: 29.5 us -> 11.7 us
  between operations: 15.4 us -> 1.23 us
  Pallas kernels: 429 us -> 415 us
  other arithmetic: 16.8 us -> 4.59 us
  blocking collectives: 8.66 us -> 0 us
    ppermute x4 -> x2, waiting for transfers between devices: 27.4 us -> 0.01 us  [unspread(): got = [lax.ppermute(part, axes, r) for part, r in zip(parts, back_routes)]]
    pallas_call x7 -> x6, Pallas kernels: 364 us -> 350 us  [the longest x1 127 us: intro(): pl.pallas_call(functools.partial(intro_kernel, plan), in_specs=[pl.BlockS...]
    ppermute x4 -> x2, starting transfers between devices: 17.7 us -> 4.61 us  [unspread(): got = [lax.ppermute(part, axes, r) for part, r in zip(parts, back_routes)]]
    all_gather x1 -> x0, blocking collectives: 8.66 us -> none  [per_device(): codes = lax.all_gather(jnp.stack([adapter_index, clip_live]), 'dp')]
    ppermute x4 -> x2, starting transfers between devices: 11.2 us -> 7.02 us  [spread(): lax.ppermute(lax.dynamic_index_in_dim(field, slot, 0, False), axes, route...]
  transfers between devices with their start and end apart: 12 -> 5, of which waited for: 3 -> 0; matrix products, arithmetic and copies ran while one was open for 3% -> 2% of each run, Pallas kernels for 62% -> 22%
where the time goes in v2:
time: 450 us; the launch traced here: 443 us
  Pallas kernels  415 us (92%)
  starting transfers between devices  11.7 us (3%)
  local copies, waits for them, and re-layouts  10.4 us (2%)
  other arithmetic  4.59 us (1%)
    pallas_call x1, Pallas kernels, intro(): pl.pallas_call(functools.partial(intro_kernel, plan), in_specs=[pl.BlockS...  127 us
    pallas_call x1, Pallas kernels, attend_back(): pl.pallas_call(functools.partial(attend_back_kernel, plan), grid=(heads,)...  96.8 us
    pallas_call x1, Pallas kernels, feed_forward(): pl.pallas_call(functools.partial(feed_kernel, plan), grid=(2 * tens,), in...  78.3 us
    pallas_call x1, Pallas kernels, share(): pl.pallas_call(functools.partial(share_kernel, plan), in_specs=[pl.BlockS...  47.8 us
    pallas_call x1, Pallas kernels, attend(): pl.pallas_call(attend_kernel, grid=(depth // 128,), in_specs=[flat, part(...  36.6 us
    pallas_call x1, Pallas kernels, project_back(): pl.pallas_call(qkv_back_kernel, grid_spec=pltpu.PrefetchScalarGridSpec(nu...  16.8 us
    pallas_call x2, Pallas kernels, tables(): pl.pallas_call(functools.partial(table_kernel, places, unit), grid_spec=p...  12 us
  transfers between devices with their start and end apart: 5, of which 0 were waited for; matrix products, arithmetic and copies ran while one was open for 2% of the time, Pallas kernels for 22%

profile of v2, /device:TPU:1, one launch (start us, length us, event | category | flops | bytes accessed | tf_op | source)
XLA Modules:
  0.0 443.0 jit_solution(13062528052596848241)
XLA Ops:
  0.7 0.7 pad_add_fusion
  1.4 0.1 collective-permute-start
  1.5 0.7 broadcast_in_dim.13
  2.1 0.1 broadcast_in_dim.14
  2.2 1.1 copy.28
  3.3 0.2 copy.29
  3.5 0.7 fusion.1
  4.2 0.7 fusion
  5.0 0.7 dynamic-slice_reduce_fusion.info
  5.7 0.7 broadcast_in_dim.15.codes_ref
  6.3 126.7 %intro.1 = (bf16[2,392,1024]{2,1,0:T(8,128)(2,1)}, bf16[784,1024]{1,0:T(8,128)(2,1)}, bf16[2,784,1024]{2,1,0:T(8,128)(2,1)}, bf16[2,784,1024]{2,1,0:T(8,128)(2,1...) custom-call(s32[2]{0:T(128)} %dynamic-slice_reduce_fusion.info, ...), custom_call_target="tpu_custom_call" | custom-call | tf_op jit(solution)/shard_map/intro/pallas_call | solution.py:352
  133.0 1.0 dynamic-slice_bitcast_fusion
  134.1 4.6 %collective-permute-start.2 = (bf16[392,1024]{1,0:T(8,128)(2,1)}, bf16[392,1024]{1,0:T(8,128)(2,1)}, u32[]{:S(2)}, u32[]{:S(2)}) collective-permute-start(bf16[392,1024]{1,0:T(8,128)(2,1)} %get-tuple-element.82), channel_id=1, source_target_pairs={{0,1},{1,0},{2,5},{3,4},{4,3},{5,2},{6,7},{7,6},{8,9},{9,8},{10,13... | collective-permute-start | bytes 2408456 | tf_op jit(solution)/shard_map/ppermute | solution.py:939
  138.7 2.4 collective-permute-start.1
  141.1 36.6 %attend.1 = (bf16[784,1024]{1,0:T(8,128)(2,1)}, f32[784,1024]{1,0:T(8,128)}) custom-call(bf16[784,1024]{1,0:T(8,128)(2,1)} %get-tuple-element.47.q_ref, bf16[2,784,1024]{2,1,0:T(8,128)(2,1)} %get-tuple-element.48.k_ref.v_ref, bf16[2,784,1024]{2,1,0:T(8,128)(2,1)} %get-tuple-element.48.k_ref.v_ref, bf16[2,784,1024]{2,1,0:T(8,128)(2,1)} %get-tuple-element.49.k2_ref.v2_ref, ...), custom_call_target="tpu_custom_call" | custom-call | tf_op jit(solution)/shard_map/attend/pallas_call | solution.py:434
  177.7 1.3 slice_bitcast_fusion
  179.0 78.3 %feed_forward.1 = (bf16[392,1024]{1,0:T(8,128)(2,1)}, bf16[392,1024]{1,0:T(8,128)(2,1)}, f32[784,1024]{1,0:T(8,128)}, bf16[784,1024]{1,0:T(8,128)(2,1)}, bf16[2,2,16,3072]{3,2,1,0:T(8,128)(2,1)}) custom-call(s32[2]{0:T(128)} %dynamic-slice_reduce_fusion.info, bf16[392,1024]{1,0:T(8,128)(2,1)} %get-tuple-element.85.xa_ref, ...), custom_call_target="tpu_custom_call" | custom-call | tf_op jit(solution)/shard_map/feed_forward/pallas_call | solution.py:633
  257.3 96.8 %attend_back.1 = (bf16[784,1024]{1,0:T(8,128)(2,1)}, bf16[2,784,1024]{2,1,0:T(8,128)(2,1)}, bf16[2,784,1024]{2,1,0:T(8,128)(2,1)}, bf16[2,392,1024]{2,1,0:T(8,128)(2,1)}, bf16[8,4,2,16,3072]{4,3,2,1,0:T(8,128)(2,1)}) custom-call(bf16[784,1024]{1,0:T(8,128)(2,1)} %get-tuple-element.47.q_ref, bf16[2,784,1024]{2,1,0:T(8,128)(2,1)} %get-tuple-element.48.k_ref.v_ref, ...), custom_call_target="tpu_custom_call" | custom-call | tf_op jit(solution)/shard_map/attend_back/pallas_call | solution.py:772
  354.2 16.8 %project_back.1 = (bf16[392,1024]{1,0:T(8,128)(2,1)}, bf16[392,1024]{1,0:T(8,128)(2,1)}, f32[16,1024]{1,0:T(8,128)}, f32[3,16,1024]{2,1,0:T(8,128)}) custom-call(s32[2]{0:T(128)} %dynamic-slice_reduce_fusion.info, bf16[392,1024]{1,0:T(8,128)(2,1)} %get-tuple-element.85.xa_ref, bf16[392,1024]{1,0:T(8,128)(2,1)} %get-tuple-element.84.xb_ref, ...), custom_call_target="tpu_custom_call" | custom-call | tf_op jit(solution)/shard_map/project_back/pallas_call | solution.py:845
  371.0 2.4 collective-permute-start.3
  373.4 2.2 collective-permute-start.4
  375.6 1.0 slice_reduce_fusion
  376.6 0.6 reshape_squeeze.3.owner
  377.2 0.9 convert.8
  378.1 0.8 convert_bitcast_fusion
  378.9 0.7 pad_maximum_fusion
  379.6 47.8 %share.1 = bf16[8,4,2,16,1024]{4,3,2,1,0:T(8,128)(2,1)} custom-call(bf16[2,2,16,1024]{3,2,1,0:T(8,128)(2,1)} %bitcast.34), custom_call_target="tpu_custom_call" | custom-call | tf_op jit(solution)/shard_map/share/pallas_call | solution.py:264
  427.5 4.6 %tables.2 = (f32[8,16,1024]{2,1,0:T(8,128)}, f32[8,3,16,1024]{3,2,1,0:T(8,128)}) custom-call(s32[16]{0:T(128)} %reshape_squeeze.3.owner, bf16[4,2,4,2,16,1024]{5,4,3,2,1,0:T(8,128)(2,1)} %bitcast.26), custom_call_target="tpu_custom_call" | custom-call | tf_op jit(solution)/shard_map/tables/pallas_call | solution.py:899
  432.0 7.5 %tables.3 = (f32[8,16,1024]{2,1,0:T(8,128)}, f32[8,16,1024]{2,1,0:T(8,128)}, f32[8,16,1024]{2,1,0:T(8,128)}, f32[8,16,1024]{2,1,0:T(8,128)}, f32[8,16,4096]{2,1,0:T(8,128)}, /*index=5*/f32[8,16,4096]{2,1,0:T(8,128)}) custom-call(s32[16]{0:T(128)} %reshape_squeeze.3.owner, bf16[4,2,4,2,16,3072]{5,4,3,2,1,0:T(8,128)(2,1)} %bitcast.27), custom_call_target="tpu_custom_call" | custom-call | tf_op jit(solution)/shard_map/tables/pallas_call | solution.py:899
  439.5 1.4 maximum_select_fusion
  440.9 0.5 copy-done.1
  441.4 1.2 copy.31
  (17 shorter events, 0.0 us)
Async XLA Ops:
  0.6 4.3 copy-start.4
  0.7 4.3 copy-start.5
  0.7 3.6 copy-start.3
  1.4 3.6 collective-permute-start
  5.0 128.1 %copy-start = (bf16[2,392,1024]{2,1,0:T(8,128)(2,1)S(1)}, bf16[2,392,1024]{2,1,0:T(8,128)(2,1)}, u32[]{:S(2)}) copy-start(bf16[2,392,1024]{2,1,0:T(8,128)(2,1)} %param.19) | copy-start | bytes 4816900
  134.1 44.9 %collective-permute-start.2 = (bf16[392,1024]{1,0:T(8,128)(2,1)}, bf16[392,1024]{1,0:T(8,128)(2,1)}, u32[]{:S(2)}, u32[]{:S(2)}) collective-permute-start(bf16[392,1024]{1,0:T(8,128)(2,1)} %get-tuple-element.82), channel_id=1, source_target_pairs={{0,1},{1,0},{2,5},{3,4},{4,3},{5,2},{6,7},{7,6},{8,9},{9,8},{10,13... | collective-permute-start | bytes 2408456 | tf_op jit(solution)/shard_map/ppermute | solution.py:939
  138.7 40.3 %collective-permute-start.1 = (bf16[392,1024]{1,0:T(8,128)(2,1)S(1)}, bf16[392,1024]{1,0:T(8,128)(2,1)}, u32[]{:S(2)}, u32[]{:S(2)}) collective-permute-start(bf16[392,1024]{1,0:T(8,128)(2,1)S(1)} %get-tuple-element.83), channel_id=1, source_target_pairs={{0,0},{1,1},{2,4},{3,5},{4,2},{5,3},{6,6},{7,7},{8,8},{9,9},{10,12... | collective-permute-start | bytes 2408456 | tf_op jit(solution)/shard_map/ppermute | solution.py:939
  141.1 36.6 %copy-start.2 = (bf16[2,392,1024]{2,1,0:T(8,128)(2,1)S(1)}, bf16[2,392,1024]{2,1,0:T(8,128)(2,1)}, u32[]{:S(2)}) copy-start(bf16[2,392,1024]{2,1,0:T(8,128)(2,1)} %get-tuple-element.50) | copy-start | bytes 4816900
  371.0 68.5 %collective-permute-start.3 = (bf16[392,1024]{1,0:T(8,128)(2,1)}, bf16[392,1024]{1,0:T(8,128)(2,1)S(1)}, u32[]{:S(2)}, u32[]{:S(2)}) collective-permute-start(bf16[392,1024]{1,0:T(8,128)(2,1)} %get-tuple-element.68), channel_id=1, source_target_pairs={{0,0},{1,1},{4,2},{5,3},{2,4},{3,5},{6,6},{7,7},{8,8},{9,9},{12,10... | collective-permute-start | bytes 2408456 | tf_op jit(solution)/shard_map/ppermute | solution.py:943
  373.4 66.1 %collective-permute-start.4 = (bf16[392,1024]{1,0:T(8,128)(2,1)}, bf16[392,1024]{1,0:T(8,128)(2,1)S(1)}, u32[]{:S(2)}, u32[]{:S(2)}) collective-permute-start(bf16[392,1024]{1,0:T(8,128)(2,1)} %get-tuple-element.69), channel_id=1, source_target_pairs={{1,0},{0,1},{5,2},{4,3},{3,4},{2,5},{7,6},{6,7},{9,8},{8,9},{13,10... | collective-permute-start | bytes 2408456 | tf_op jit(solution)/shard_map/ppermute | solution.py:943
  439.5 1.9 copy-start.1

commit v3 on v2

--- a/solution.py
+++ b/solution.py
@@ -16,6 +16,7 @@
 TN = (((0,), (0,)), ((), ()))
 VMEM_BYTES = 61 << 20
 SAFE_SCORE = 60.0
+EARLY = 4
 
 
 def mm(a, b):
@@ -155,7 +156,7 @@
     stages = len(items[0].stages)
 
     def step(s):
-        for item in pairs[s : s + 1]:
+        for item in pairs[0:2] if s == 0 else pairs[s + 1 : s + 2]:
             for one in item:
                 one.start()
         for n, pair in enumerate(pairs):
@@ -254,28 +255,10 @@
                 ] + plan.semaphores(shape[0])
 
 
-def share_kernel(plan, x_ref, o_ref, *scratch):
-    plan.greet()
-    for step in Pool(plan, x_ref, o_ref, *scratch).steps:
-        step()
-
-
-def share(plan, dps, x, number):
-    return pl.pallas_call(
-        functools.partial(share_kernel, plan),
-        in_specs=[pl.BlockSpec(memory_space=pltpu.VMEM)],
-        out_specs=pl.BlockSpec(memory_space=pl.ANY),
-        out_shape=jax.ShapeDtypeStruct((dps, plan.tens) + x.shape[1:], BF16),
-        scratch_shapes=Pool.scratch(plan, x.shape[1:]),
-        compiler_params=pltpu.CompilerParams(collective_id=number, has_side_effects=True),
-        name="share",
-    )(x)
-
-
 def intro_kernel(
     plan, info, tok_ref, codes_ref, gain_ref, w_ref, wo_ref, w1_ref, w2_ref, down_ref, up_ref,
-    x_ref, q_ref, kv_ref, kv2_ref, low_ref, codes_out, w_out, wo_out, w1_out, w2_out,
-    x_s, w_s, n_s, kv_s, keep_sem, kv_send, kv_recv, r_local, r_send, r_recv, *sems,
+    x_ref, q_ref, kv_ref, kv2_ref, low_ref, reach_ref, codes_out, w_out, wo_out, w1_out, w2_out,
+    x_s, w_s, n_s, kv_s, far_s, far_got, keep_sem, kv_send, kv_recv, far_send, far_recv, r_local, r_send, r_recv, *sems,
 ):
     half, depth = x_ref.shape[1:]
     tens, width = plan.tens, w_ref.shape[2]
@@ -298,15 +281,18 @@
     plan.greet(route.peers)
     for item in first:
         item.start()
-    route.start(tok_ref, x_s)
     stages = len(first[0].stages)
     for s in range(cuts // 2 + stages - 1):
         for n in range(cuts // 2):
             if 0 <= s - n < stages:
                 first[2 * n].advance(s - n)
                 first[2 * n + 1].advance(s - n)
+        if s == cuts // 2 - 1:
+            later[0]()
+            route.start(tok_ref, x_s)
+    later[1]()
+    later[2]()
     route.wait(tok_ref, x_s)
-    later[0]()
     x_ref[...] = x_s[...]
     for part in range(2):
         normed, _ = norm_parts(x_s[part].astype(F32))
@@ -323,9 +309,13 @@
         src_ref=kv_s, dst_ref=kv2_ref, send_sem=kv_send, recv_sem=kv_recv,
         device_id=(me ^ 1, t), device_id_type=pl.DeviceIdType.MESH,
     )
+    far_swap = pltpu.make_async_remote_copy(
+        src_ref=far_s, dst_ref=far_got, send_sem=far_send, recv_sem=far_recv,
+        device_id=(me ^ 1, t), device_id_type=pl.DeviceIdType.MESH,
+    )
     blocks = w_ref.shape[0] // 3
     for turn, j in enumerate((1, 2, 0)):
-        later[turn + 1]()
+        later[turn + 3]()
         for c in range(tens):
             cols = slice(c * width, (c + 1) * width)
             w = w_s[:, c, j * blocks : (j + 1) * blocks].reshape(depth, width)
@@ -334,10 +324,23 @@
                 q_ref[:, cols] = res
             else:
                 kv_s[j - 1, :, cols] = res
+            if j != 2:
+                spread = lax.broadcasted_iota(jnp.int32, (width, 128), 0) // HEAD_DIM + c * (width // HEAD_DIM)
+                spread = (spread == lax.broadcasted_iota(jnp.int32, (width, 128), 1)).astype(BF16)
+                norms = mm(res * res, spread)
+                reach = norms if c == 0 else reach + norms
+        if j != 2:
+            reach = 1.02 * jnp.max(reach, axis=0, keepdims=True)
+        if j == 1:
+            far_s[...] = jnp.broadcast_to(reach, far_s.shape)
+            far_swap.start()
+        if j == 0:
+            far_swap.wait()
+            reach_ref[...] = reach * jnp.maximum(far_s[...], far_got[...]) * (1.0 / HEAD_DIM)
         if j == 2:
             swap.start()
             kv_ref[...] = kv_s[...]
-    for one in later[4:]:
+    for one in later[6:]:
         one()
     swap.wait()
     keep.wait()
@@ -352,20 +355,21 @@
     return pl.pallas_call(
         functools.partial(intro_kernel, plan),
         in_specs=[pl.BlockSpec(memory_space=pltpu.SMEM), hbm, hbm, vm, hbm, hbm, hbm, hbm, vm, vm],
-        out_specs=[vm, vm, vm, hbm, vm] + [hbm] * 5,
+        out_specs=[vm, vm, vm, hbm, vm, vm] + [hbm] * 5,
         out_shape=[
             jax.ShapeDtypeStruct(tokens.shape, BF16),
             jax.ShapeDtypeStruct((rows, depth), BF16),
             jax.ShapeDtypeStruct((2, rows, depth), BF16),
             jax.ShapeDtypeStruct((2, rows, depth), BF16),
             jax.ShapeDtypeStruct((rows, rank), F32),
+            jax.ShapeDtypeStruct((8, 128), F32),
             big(codes), big(w), big(wo), big(w1), big(w2),
         ],
         scratch_shapes=[
             pltpu.VMEM(tokens.shape, BF16), pltpu.VMEM((dps, plan.tens) + w.shape, BF16), pltpu.VMEM((rows, depth), F32),
-            pltpu.VMEM((2, rows, depth), BF16),
+            pltpu.VMEM((2, rows, depth), BF16), pltpu.VMEM((8, 128), F32), pltpu.VMEM((8, 128), F32),
         ]
-        + [pltpu.SemaphoreType.DMA] * 3
+        + [pltpu.SemaphoreType.DMA] * 5
         + Route.semaphores() + plan.semaphores(cuts) + plan.semaphores(items),
         compiler_params=pltpu.CompilerParams(
             vmem_limit_bytes=VMEM_BYTES, collective_id=number, has_side_effects=True
@@ -407,40 +411,39 @@
         vs[h, rows:, :] = jnp.where(mine, v2_ref[0], BF16(1))
 
 
-def attend_kernel(q_ref, k_ref, v_ref, k2_ref, v2_ref, o_ref, lse_ref, ks, vs):
+def attend_kernel(safe, q_ref, k_ref, v_ref, k2_ref, v2_ref, o_ref, lse_ref, ks, vs):
     stage_keys(k_ref, v_ref, k2_ref, v2_ref, ks, vs)
     q2 = q_ref[...] * BF16(HEAD_DIM ** -0.5)
-    lane = lax.broadcasted_iota(jnp.int32, (1, 128), 1)
-    qf, kf = q2.astype(F32), ks[...].astype(F32)
-    safe = True
-    for h in range(2):
-        mine = (lane // HEAD_DIM) == h
-        far = lambda x: jnp.max(jnp.sum(jnp.where(mine, x * x, 0.0), axis=1, keepdims=True))
-        safe = jnp.logical_and(safe, far(qf) * far(kf) <= SAFE_SCORE * SAFE_SCORE)
-
-    @pl.when(safe)
+    pair = safe[pl.program_id(0)]
+
+    @pl.when(pair == 1)
     def _():
         o_ref[...], lse_ref[...] = attend_pair(q2, ks, vs, False)
 
-    @pl.when(jnp.logical_not(safe))
+    @pl.when(pair != 1)
     def _():
         o_ref[...], lse_ref[...] = attend_pair(q2, ks, vs, True)
 
 
-def attend(q, kv, kv2):
+def attend(reach, q, kv, kv2):
     rows, depth = q.shape
-    flat = pl.BlockSpec((rows, 128), lambda i: (0, i))
-    part = lambda j: pl.BlockSpec((1, rows, 128), lambda i: (j, 0, i))
+    heads = depth // 128
+    safe = (jnp.max(reach[0, : 2 * heads].reshape(heads, 2), axis=1) <= SAFE_SCORE * SAFE_SCORE).astype(jnp.int32)
+    flat = pl.BlockSpec((rows, 128), lambda i, safe: (0, i))
+    part = lambda j: pl.BlockSpec((1, rows, 128), lambda i, safe: (j, 0, i))
     return pl.pallas_call(
         attend_kernel,
-        grid=(depth // 128,),
-        in_specs=[flat, part(0), part(1), part(0), part(1)],
-        out_specs=[flat, flat],
+        grid_spec=pltpu.PrefetchScalarGridSpec(
+            num_scalar_prefetch=1,
+            grid=(heads,),
+            in_specs=[flat, part(0), part(1), part(0), part(1)],
+            out_specs=[flat, flat],
+            scratch_shapes=[pltpu.VMEM((2 * rows, 128), BF16), pltpu.VMEM((2, 2 * rows, 128), BF16)],
+        ),
         out_shape=[jax.ShapeDtypeStruct((rows, depth), BF16), jax.ShapeDtypeStruct((rows, depth), F32)],
-        scratch_shapes=[pltpu.VMEM((2 * rows, 128), BF16), pltpu.VMEM((2, 2 * rows, 128), BF16)],
         compiler_params=params(),
         name="attend",
-    )(q, kv, kv, kv2, kv2)
+    )(safe, q, kv, kv, kv2, kv2)
 
 
 def gelu_both(x):
@@ -460,8 +463,10 @@
     step, last = pl.program_id(0), pl.num_programs(0) - 1
     e, live = info[0], info[1].astype(F32)
     dp, tens, wop, wor, woc = wo_ref.shape
-    fp, fr, fc = w1_ref.shape[2:]
-    wide = fp * fc
+    fr, fc = w1_ref.shape[3:]
+    wide = tens * fc
+    ff = u1_ref.shape[2]
+    parts = ff // wide
     if late:
         w1_late, w2_late, *sems = late
         items = []
@@ -470,7 +475,9 @@
                 cut = pl.ds(k, 1)
                 items.append(Item(plan, sems, len(items), src.at[cut], at(out, cut), len(items) % 2))
         steps = schedule(items)
-        before = {0: 0, 2: 1, 3: 2, 4: 3, 5: 4, 6: 5, 7: 6}
+        known = parts - len(items) // 2
+    else:
+        known = parts
 
     def put(unit, cols, value):
         per = grads_ref.shape[3] // depth
@@ -482,10 +489,11 @@
 
     if late:
         pl.when(step == 0)(plan.greet)
-        for n, when in before.items():
-            pl.when(step == when)(steps[n])
-        for n in range(len(items) // 2):
-            @pl.when(step == tens + n)
+        pl.when(step == 0)(steps[0])
+        for n in range(3, len(steps) - 1):
+            pl.when(step == n - 2)(steps[n])
+        for n in range(parts - known):
+            @pl.when(step == known + n)
             def _():
                 items[2 * n].finish()
                 items[2 * n + 1].finish()
@@ -504,6 +512,8 @@
         for part, ref in enumerate((xa_ref, xb_ref)):
             s = slice(part * half, (part + 1) * half)
             mid_s[s, :] = ref[...].astype(F32) + attention[s, :]
+        if late:
+            steps[1]()
         for part, ref in enumerate((ca_ref, cb_ref)):
             s = slice(part * half, (part + 1) * half)
             gm_ref[s, :] = ref[...].astype(F32) * live
@@ -517,41 +527,33 @@
         low2_s[...] = jnp.zeros_like(low2_s)
         b1_s[...] = jnp.zeros_like(b1_s)
 
-    def stage(take_1, take_2):
+    def stage(ref_1, ref_2, part):
         for a in range(dp):
-            for k in range(fp):
-                w1_s[a * fr : (a + 1) * fr, k * fc : (k + 1) * fc] = take_1(a, k)
-                w2_s[k * fr : (k + 1) * fr, a * woc : (a + 1) * woc] = take_2(a, k)
+            for t in range(tens):
+                w1_s[a * fr : (a + 1) * fr, t * fc : (t + 1) * fc] = ref_1[a, t, part]
+                w2_s[t * fr : (t + 1) * fr, a * woc : (a + 1) * woc] = ref_2[a, t, part]
 
     if late:
-        @pl.when(step < tens)
+        @pl.when(step < known)
         def _():
-            stage(lambda a, k: w1_ref[a, 0, k], lambda a, k: w2_ref[a, 0, k])
-
-        @pl.when(step >= tens)
+            stage(w1_ref, w2_ref, 0)
+
+        @pl.when(step >= known)
         def _():
-            part = step - tens
-            stage(lambda a, k: w1_late[a, k, part], lambda a, k: w2_late[a, k, part])
+            stage(w1_late, w2_late, step - known)
     else:
-        stage(lambda a, k: w1_ref[a, 0, k], lambda a, k: w2_ref[a, 0, k])
+        stage(w1_ref, w2_ref, 0)
 
     w1, w2 = w1_s[...], w2_s[...]
-    if late:
-        early_step = step < tens
-        runs = [
-            pl.multiple_of(jnp.where(early_step, step * 2 * wide + k * fc, (2 * k + 1) * wide + (step - tens) * fc), fc)
-            for k in range(fp)
-        ]
-        u1 = jnp.concatenate([u1_ref[e, :, pl.ds(run, fc)] for run in runs], axis=1)
-        d2 = jnp.concatenate([d2_ref[e, :, pl.ds(run, fc)] for run in runs], axis=1)
-    else:
-        u1, d2 = u1_ref[e], d2_ref[e]
+    runs = [pl.multiple_of((t * parts + step) * fc, fc) for t in range(tens)]
+    u1 = jnp.concatenate([u1_ref[e, :, pl.ds(run, fc)] for run in runs], axis=1)
+    d2 = jnp.concatenate([d2_ref[e, :, pl.ds(run, fc)] for run in runs], axis=1)
     n, gf = n_s[...], gf_s[...]
     low1, b2 = low1_s[...].astype(BF16), b2_s[...].astype(BF16)
     preact = mm(n, w1) + mm(low1, u1)
     ghid = mm_nt(gf, w2) + mm(b2, d2)
     if late:
-        pl.when(step == 0)(steps[1])
+        pl.when(step == 0)(steps[2])
     hid, slope = gelu_both(preact)
     hid = hid.astype(BF16)
     gpre = (ghid * slope).astype(BF16)
@@ -560,15 +562,10 @@
     low2_s[...] += mm_nt(hid, d2)
     b1_s[...] += mm_nt(gpre, u1)
     gu1, gd2 = mm_tn(low1, gpre), mm_tn(b2, hid)
-    if late:
-        for k, run in enumerate(runs):
-            cols = slice(k * fc, (k + 1) * fc)
-            put(4 + run // depth, lax.rem(run, depth), gu1[:, cols])
-            put(4 + tens + run // depth, lax.rem(run, depth), gd2[:, cols])
-    else:
-        t, part = lax.rem(step, tens), step // tens
-        put(4 + t, part * wide, gu1)
-        put(4 + tens + t, part * wide, gd2)
+    for t, run in enumerate(runs):
+        cols = slice(t * fc, (t + 1) * fc)
+        put(4 + run // depth, lax.rem(run, depth), gu1[:, cols])
+        put(4 + ff // depth + run // depth, lax.rem(run, depth), gd2[:, cols])
 
     @pl.when(step == last)
     def _():
@@ -594,22 +591,14 @@
     rows = 2 * half
     adapters, rank = od.shape[:2]
     dp, tens, wop, wor, woc = wo.shape
-    fp, fr, fc = w1.shape[2:]
-    fp = fp if late else fp // 2
-    wide = fp * fc
-    ff = 2 * wide * tens
+    fr, fc = w1.shape[3:]
+    wide = tens * fc
+    ff = u1.shape[2]
+    known = w1.shape[2]
     once = lambda *shape: pl.BlockSpec(shape, lambda f: (0,) * len(shape), pipeline_mode=pl.Buffered(1))
     whole = lambda *shape: pl.BlockSpec(shape, lambda f: (0,) * len(shape))
-    table = once(adapters, rank, depth)
-    if late:
-        assert late[0].shape[0] == tens == fp
-        table_f = once(adapters, rank, ff)
-    else:
-        table_f = pl.BlockSpec((adapters, rank, wide), lambda f: (0, 0, f % tens * 2 + f // tens))
-    if late:
-        place = lambda f: (0, jnp.minimum(f, tens - 1), 0, 0, 0)
-    else:
-        place = lambda f: (0, f % tens, f // tens, 0, 0)
+    table, table_f = once(adapters, rank, depth), once(adapters, rank, ff)
+    place = lambda f: (0, 0, jnp.minimum(f, known - 1), 0, 0)
     units = 4 + 2 * ff // depth
     cuts = 2
     hbm = pl.BlockSpec(memory_space=pl.ANY)
@@ -632,15 +621,15 @@
         late = [jnp.zeros((16, 128), BF16)] * 2
     return pl.pallas_call(
         functools.partial(feed_kernel, plan),
-        grid=(2 * tens,),
+        grid=(ff // wide,),
         in_specs=[
             pl.BlockSpec(memory_space=pltpu.SMEM),
             once(half, depth), once(half, depth), once(half, depth), once(half, depth),
             once(rows, depth),
             whole(1, depth),
             once(dp, tens, wop, wor, woc),
-            pl.BlockSpec((dp, 1, fp, fr, fc), place),
-            pl.BlockSpec((dp, 1, fp, fr, woc), place),
+            pl.BlockSpec((dp, tens, 1, fr, fc), place),
+            pl.BlockSpec((dp, tens, 1, fr, woc), place),
             hbm, hbm,
             table, table, table, table_f, table_f, table,
         ],
@@ -671,7 +660,7 @@
 def attend_back_kernel(
     plan, q_ref, k_ref, v_ref, k2_ref, v2_ref, g_ref, o_ref, lse_ref, la_ref, lb_ref, grads_ref,
     dq_ref, dkv_ref, far_ref, lo_ref, early_ref,
-    ks, vs, kd, acc, far_s, far_send, far_recv, lo_local, lo_send, lo_recv, *pool,
+    ks, vs, qs, gs, acc, far_s, far_send, far_recv, lo_local, lo_send, lo_recv, *pool,
 ):
     rows = q_ref.shape[0]
     step, steps = pl.program_id(0), pl.num_programs(0)
@@ -704,53 +693,48 @@
     zero = BF16(0)
     lane = lax.broadcasted_iota(jnp.int32, (1, 128), 1)
     scale = BF16(HEAD_DIM ** -0.5)
-    q2 = q_ref[...] * scale
-    g2 = g_ref[...]
-    hi, mid, lo = split3(pltpu.roll(lse_ref[...], HEAD_DIM, 1))
+    q2, g2 = q_ref[...] * scale, g_ref[...]
     prod = g2.astype(F32) * o_ref[...].astype(F32)
-    qa, ga, qm, gm = [], [], [], []
+
+    def less(parts, b):
+        return jnp.where(lane == b, -parts[0], jnp.where(lane == b + 1, -parts[1], jnp.where(lane == b + 2, -parts[2], zero)))
+
+    totals = split3(lse_ref[...])
     for h in range(2):
-        mine, b = (lane // HEAD_DIM) == h, HEAD_DIM * (1 - h)
-        qa.append(
-            jnp.where(mine, q2, jnp.where(lane == b, -hi, jnp.where(lane == b + 1, -mid, jnp.where(lane == b + 2, -lo, zero))))
-        )
-        dh, dm, dl = split3(jnp.sum(jnp.where(mine, prod, 0.0), axis=1, keepdims=True))
-        ga.append(
-            jnp.where(mine, g2, jnp.where(lane == b, -dh, jnp.where(lane == b + 1, -dm, jnp.where(lane == b + 2, -dl, zero))))
-        )
-        qm.append(jnp.where(mine, q2, zero))
-        gm.append(jnp.where(mine, g2, zero))
-        ones = ((lane >= b) & (lane < b + 3)).astype(BF16)
-        for i, (kr, vr) in enumerate(((k_ref, v_ref), (k2_ref, v2_ref))):
-            s = slice(i * rows, (i + 1) * rows)
-            ks[h, s, :] = jnp.where(mine, kr[0], ones)
-            vs[h, s, :] = jnp.where(mine, vr[0], ones)
-            kd[h, s, :] = jnp.where(mine, kr[0] * scale, zero)
+        mine, b = (lane // HEAD_DIM) == h, HEAD_DIM * h
+        s = slice(h * rows, (h + 1) * rows)
+        qs[s, 0:128] = jnp.where(mine, q2, zero)
+        qs[s, 128:256] = less(totals, b)
+        gs[s, 0:128] = jnp.where(mine, g2, zero)
+        gs[s, 128:256] = less(split3(jnp.sum(jnp.where(mine, prod, 0.0), axis=1, keepdims=True)), b)
+    ones = jnp.broadcast_to((lax.rem(lane, HEAD_DIM) < 3).astype(BF16), (rows, 128))
+
     @pl.when(step >= 2)
     def _():
         far(step - 2).wait_send()
 
     slot = lax.rem(step, 2)
-    for i in range(2):
-        s = slice((1 - i) * rows, (2 - i) * rows)
-        dk = jnp.zeros((rows, 128), F32)
-        dv = jnp.zeros((rows, 128), F32)
-        dq = jnp.zeros((rows, 128), F32)
-        for h in range(2):
-            p = jnp.exp(mm_nt(ks[h, s, :], qa[h]))
-            ds = (p * mm_nt(vs[h, s, :], ga[h])).astype(BF16)
-            dv = dv + mm(p.astype(BF16), gm[h])
-            dk = dk + mm(ds, qm[h])
-            dq = dq + mm_tn(ds, kd[h, s, :])
+    for i, (kr, vr) in enumerate(((k2_ref, v2_ref), (k_ref, v_ref))):
+        s = slice(i * rows, (i + 1) * rows)
+        ks[s, 0:128] = kr[0]
+        vs[s, 0:128] = vr[0]
+        ks[s, 128:256] = ones
+        vs[s, 128:256] = ones
+        p = jnp.exp(mm_nt(ks[s, :], qs[...]))
+        ds = (p * mm_nt(vs[s, :], gs[...])).astype(BF16)
+        dv = mm(p.astype(BF16), gs[:, 0:128]).astype(BF16)
+        dk = mm(ds, qs[:, 0:128]).astype(BF16)
+        dq = mm_tn(ds, ks[s, 0:128])
+        dq = jnp.where(lane < HEAD_DIM, dq[:rows], dq[rows:])
         if i == 0:
-            far_s[slot, 0] = dk.astype(BF16)
-            far_s[slot, 1] = dv.astype(BF16)
+            far_s[slot, 0] = dk
+            far_s[slot, 1] = dv
             far(step).start()
             acc[...] = dq
         else:
-            dkv_ref[0] = dk.astype(BF16)
-            dkv_ref[1] = dv.astype(BF16)
-            dq_ref[...] = (acc[...] + dq).astype(BF16)
+            dkv_ref[0] = dk
+            dkv_ref[1] = dv
+            dq_ref[...] = ((acc[...] + dq) * (HEAD_DIM ** -0.5)).astype(BF16)
 
     @pl.when(step == steps - 1)
     def _():
@@ -782,7 +766,7 @@
             jax.ShapeDtypeStruct((2,) + la.shape, BF16),
             jax.ShapeDtypeStruct((dps, plan.tens) + grads.shape[1:], BF16),
         ],
-        scratch_shapes=[pltpu.VMEM((2, 2 * rows, 128), BF16)] * 3
+        scratch_shapes=[pltpu.VMEM((2 * rows, 256), BF16)] * 4
         + [pltpu.VMEM((rows, 128), F32), pltpu.VMEM((2, 2, rows, 128), BF16), dma(heads), dma(heads),
            *Route.semaphores()]
         + Pool.scratch(plan, grads.shape[1:]),
@@ -793,25 +777,15 @@
     )(q, kv, kv, kv2, kv2, g, ctx, lse, la, lb, grads)
 
 
-def qkv_back_kernel(
-    info, xa_ref, xb_ref, gain_ref, dq_ref, dkv_ref, dkv2_ref, gm_ref, low_ref, w_ref, down_ref, up_ref,
-    ya_ref, yb_ref, g_down, g_up, gn_s, back_s,
-):
-    half, depth = xa_ref.shape
-    parts, width = w_ref.shape[1], w_ref.shape[4]
+def low_back_kernel(info, x_ref, gain_ref, dq_ref, dkv_ref, dkv2_ref, low_ref, up_ref, gkv_ref, back_ref, grads_ref):
+    half = x_ref.shape[1]
     step, last = pl.program_id(0), pl.num_programs(0) - 1
+    cuts = grads_ref.shape[1]
 
     def go(g, first):
         back = mm_nt(g, up_ref[0, 0])
-        total = back if first else back_s[...] + back
-        back_s[...] = total
-        acc = None if first else gn_s[...]
-        for part in range(parts):
-            cols = slice(part * width, (part + 1) * width)
-            term = mm_nt(g[:, cols], w_ref[:, part, 0].reshape(depth, width))
-            acc = term if acc is None else acc + term
-        gn_s[...] = acc
-        g_up[0] = mm_tn(low_ref[...].astype(BF16), g)
+        back_ref[...] = back if first else back_ref[...] + back
+        grads_ref[(step + 1) // cuts, lax.rem(step + 1, cuts)] = mm_tn(low_ref[...].astype(BF16), g).astype(BF16)
 
     @pl.when(step == 0)
     def _():
@@ -819,57 +793,124 @@
 
     @pl.when(step > 0)
     def _():
-        go((dkv_ref[0].astype(F32) + dkv2_ref[0].astype(F32)).astype(BF16), False)
+        g = (dkv_ref[0].astype(F32) + dkv2_ref[0].astype(F32)).astype(BF16)
+        gkv_ref[0] = g
+        go(g, False)
 
     @pl.when(step == last)
     def _():
-        back = back_s[...].astype(BF16)
-        gn_s[...] += mm(back, down_ref[0])
-        total = jnp.zeros(g_down.shape, F32)
-        for part, (x_ref, y_ref) in enumerate(((xa_ref, ya_ref), (xb_ref, yb_ref))):
-            s = slice(part * half, (part + 1) * half)
-            normed, scale = norm_parts(x_ref[...].astype(F32))
-            total = total + mm_tn(back_s[s, :].astype(BF16), (normed * gain_ref[...]).astype(BF16))
-            y_ref[...] = (gm_ref[s, :] + norm_back(normed, scale, gain_ref[...], gn_s[s, :])).astype(BF16)
-        g_down[...] = total
-
-
-def project_back(info, xa, xb, gain, dq, dkv, dkv2, gm, low, w, down, up):
-    half, depth = xa.shape
-    rows = 2 * half
-    rank = down.shape[1]
-    dp, tens, _, wr, wc = w.shape
-    whole = lambda *shape: pl.BlockSpec(shape, lambda j, info: (0,) * len(shape))
+        total = None
+        for part in range(2):
+            normed, _ = norm_parts(x_ref[part].astype(F32))
+            back = back_ref[part * half : (part + 1) * half, :].astype(BF16)
+            term = mm_tn(back, (normed * gain_ref[...]).astype(BF16))
+            total = term if total is None else total + term
+        grads_ref[0, 0] = total.astype(BF16)
+
+
+def low_back(info, x, gain, dq, dkv, dkv2, low, up):
+    _, half, depth = x.shape
+    rows, rank = 2 * half, low.shape[1]
     once = lambda *shape: pl.BlockSpec(shape, lambda j, info: (0,) * len(shape), pipeline_mode=pl.Buffered(1))
     pair = pl.BlockSpec((1, rows, depth), lambda j, info: (jnp.maximum(j - 1, 0), 0, 0))
     return pl.pallas_call(
-        qkv_back_kernel,
+        low_back_kernel,
         grid_spec=pltpu.PrefetchScalarGridSpec(
             num_scalar_prefetch=1,
             grid=(3,),
             in_specs=[
-                once(half, depth), once(half, depth), whole(1, depth),
-                once(rows, depth), pair, pair,
-                once(rows, depth), once(rows, rank),
-                pl.BlockSpec((dp, tens, 1, wr, wc), lambda j, info: (0, 0, j, 0, 0)),
-                pl.BlockSpec((1, rank, depth), lambda j, info: (info[0], 0, 0)),
+                once(2, half, depth), once(1, depth), once(rows, depth), pair, pair, once(rows, rank),
                 pl.BlockSpec((1, 1, rank, depth), lambda j, info: (info[0], j, 0, 0)),
             ],
             out_specs=[
-                whole(half, depth), whole(half, depth), whole(rank, depth),
-                pl.BlockSpec((1, rank, depth), lambda j, info: (j, 0, 0)),
+                pair, pl.BlockSpec((rows, rank), lambda j, info: (0, 0)),
+                pl.BlockSpec((2, 2, rank, depth), lambda j, info: (0, 0, 0, 0)),
             ],
-            scratch_shapes=[pltpu.VMEM((rows, depth), F32), pltpu.VMEM((rows, rank), F32)],
         ),
+        out_shape=[
+            jax.ShapeDtypeStruct((2, rows, depth), BF16),
+            jax.ShapeDtypeStruct((rows, rank), F32),
+            jax.ShapeDtypeStruct((2, 2, rank, depth), BF16),
+        ],
+        compiler_params=params(),
+        name="low_back",
+    )(info, x, gain, dq, dkv, dkv2, low, up)
+
+
+def outro_kernel(
+    plan, info, x_ref, gain_ref, dq_ref, gkv_ref, back_ref, gm_ref, w_ref, down_ref, grads_ref,
+    ya_ref, yb_ref, late_ref, gn_s, *pool,
+):
+    half, depth = x_ref.shape[1:]
+    parts, width = w_ref.shape[1], w_ref.shape[4]
+    step, last = pl.program_id(0), pl.num_programs(0) - 1
+    late = Pool(plan, grads_ref, late_ref, *pool).steps
+
+    @pl.when(step == 0)
+    def _():
+        plan.greet()
+        late[0]()
+
+    def go(g, first):
+        acc = mm(back_ref[...].astype(BF16), down_ref[info[0]]) if first else gn_s[...]
+        for part in range(parts):
+            cols = slice(part * width, (part + 1) * width)
+            acc = acc + mm_nt(g[:, cols], w_ref[:, part, 0].reshape(depth, width))
+        gn_s[...] = acc
+
+    @pl.when(step == 0)
+    def _():
+        go(dq_ref[...], True)
+        late[1]()
+
+    @pl.when(step > 0)
+    def _():
+        go(gkv_ref[0], False)
+
+    @pl.when(step == 1)
+    def _():
+        late[2]()
+
+    @pl.when(step == last)
+    def _():
+        late[3]()
+        for part, y_ref in enumerate((ya_ref, yb_ref)):
+            s = slice(part * half, (part + 1) * half)
+            normed, scale = norm_parts(x_ref[part].astype(F32))
+            y_ref[...] = (gm_ref[s, :] + norm_back(normed, scale, gain_ref[...], gn_s[s, :])).astype(BF16)
+        for one in late[4:]:
+            one()
+
+
+def outro(plan, dps, info, x, gain, dq, gkv, back, gm, w, down, grads, number):
+    _, half, depth = x.shape
+    rows = 2 * half
+    dp, tens, _, wr, wc = w.shape
+    whole = lambda *shape: pl.BlockSpec(shape, lambda j: (0,) * len(shape))
+    once = lambda *shape: pl.BlockSpec(shape, lambda j: (0,) * len(shape), pipeline_mode=pl.Buffered(1))
+    return pl.pallas_call(
+        functools.partial(outro_kernel, plan),
+        grid=(3,),
+        in_specs=[
+            pl.BlockSpec(memory_space=pltpu.SMEM),
+            once(2, half, depth), once(1, depth), once(rows, depth),
+            pl.BlockSpec((1, rows, depth), lambda j: (jnp.maximum(j - 1, 0), 0, 0)),
+            once(*back.shape), once(rows, depth),
+            pl.BlockSpec((dp, tens, 1, wr, wc), lambda j: (0, 0, j, 0, 0)),
+            once(*down.shape), once(*grads.shape),
+        ],
+        out_specs=[whole(half, depth), whole(half, depth), pl.BlockSpec(memory_space=pl.ANY)],
         out_shape=[
             jax.ShapeDtypeStruct((half, depth), BF16),
             jax.ShapeDtypeStruct((half, depth), BF16),
-            jax.ShapeDtypeStruct((rank, depth), F32),
-            jax.ShapeDtypeStruct((3, rank, depth), F32),
+            jax.ShapeDtypeStruct((dps, plan.tens) + grads.shape[1:], BF16),
         ],
-        compiler_params=params(),
-        name="project_back",
-    )(info, xa, xb, gain, dq, dkv, dkv2, gm, low, w, down, up)
+        scratch_shapes=[pltpu.VMEM((rows, depth), F32)] + Pool.scratch(plan, grads.shape[1:]),
+        compiler_params=pltpu.CompilerParams(
+            vmem_limit_bytes=VMEM_BYTES, collective_id=number, has_side_effects=True
+        ),
+        name="outro",
+    )(info, x, gain, dq, gkv, back, gm, w, down, grads)
 
 
 def table_kernel(places, unit, owner, g_ref, *outs):
@@ -965,10 +1006,10 @@
     parts_o = weight_out.reshape(2, -1, weight_out.shape[1])
     late, fine = [], 2
     if dps <= 8:
-        fine, n = 8, parts_1.shape[0] // 2
+        fine, n = 8, parts_1.shape[0] * EARLY // 8
         late = [parts_1[n:], parts_2[n:]]
         parts_1, parts_2 = parts_1[:n], parts_2[:n]
-    x, q, kv, kv2, low, codes, w_qkv, w_out, w_fc1, w_fc2 = intro(
+    x, q, kv, kv2, low, reach, codes, w_qkv, w_out, w_fc1, w_fc2 = intro(
         plan, dps, info, tokens, codes, g1, parts_q, parts_o, parts_1, parts_2, qkv_down, qkv_up, fine, 0
     )
     owner = codes[:, 0, 0, :2, 0].reshape(-1)
@@ -976,7 +1017,7 @@
     w_qkv = fold(w_qkv.reshape((dps, tens) + weight_qkv.shape), 3)
     cotangent, q = lax.optimization_barrier((cotangent, q))
     ca, cb = spread(cotangent)
-    ctx, lse = attend(q, kv, kv2)
+    ctx, lse = attend(reach, q, kv, kv2)
     w_out, w_fc1, w_fc2 = fold(w_out, 4), fold(w_fc1, 3), fold(w_fc2, 4)
     la, lb, gm, gctx, grads = feed_forward(
         plan, info, xa, xb, ca, cb, ctx, g2, w_out, w_fc1, w_fc2, late,
@@ -984,14 +1025,14 @@
     )
     dq, dkv, dkv2, layer_out, early = attend_back(plan, dps, q, kv, kv2, gctx, ctx, lse, la, lb, grads, 3)
     depth, ff = out_down.shape[2], fc1_up.shape[2]
+    gkv, back, grads = low_back(info, x, g1, dq, dkv, dkv2, low, qkv_up)
+    ya, yb, late_grads = outro(plan, dps, info, x, g1, dq, gkv, back, gm, w_qkv, qkv_down, grads, 4)
+    grad_tokens = unspread([ya, yb])
+    late_grads, early, owner, ya = lax.optimization_barrier((late_grads, early, owner, ya))
     t_od, t_ou, t_d1, t_u2, t_u1, t_d2 = tables(
         owner, early, [a.shape for a in (out_down, out_up, fc1_down, fc2_up, fc1_up, fc2_down)],
         [(n, None, 0) for n in range(4)] + [(n, None, c) for n in (4, 5) for c in range(0, ff, depth)], depth,
     )
-    ya, yb, g_qd, g_qu = project_back(info, xa, xb, g1, dq, dkv, dkv2, gm, low, w_qkv, qkv_down, qkv_up)
-    grads = jnp.concatenate([g_qd[None], g_qu]).astype(BF16)
-    late_grads = share(plan, dps, grads.reshape((2, 2) + grads.shape[1:]), 4)
-    grad_tokens = unspread([ya, yb])
     t_qd, t_qu = tables(
         owner, late_grads, [qkv_down.shape, qkv_up.shape], [(0, None, 0)] + [(1, j, 0) for j in range(3)], depth
     )

time: 450 us -> 433 us (0.962)
  Pallas kernels: 415 us -> 377 us
  waiting for transfers between devices: 0.01 us -> 20.4 us
    pallas_call x4, Pallas kernels: 180 us -> 153 us  [the longest x1 81.9 us: feed_forward(): pl.pallas_call(functools.partial(feed_kernel, plan), grid=(ff // wide,),...]
    ppermute x2, waiting for transfers between devices: 0.01 us -> 20.4 us  [unspread(): got = [lax.ppermute(part, axes, r) for part, r in zip(parts, back_routes)]]
    pallas_call x1, Pallas kernels: 96.8 us -> 81.8 us  [attend_back(): pl.pallas_call(functools.partial(attend_back_kernel, plan), grid=(heads,)...]
  transfers between devices with their start and end apart: 5 -> 5, of which waited for: 0 -> 2; matrix products, arithmetic and copies ran while one was open for 2% -> 2% of each run, Pallas kernels for 22% -> 10%
where the time goes in v3:
time: 433 us; the launch traced here: 425 us
  Pallas kernels  377 us (87%)
  waiting for transfers between devices  20.4 us (5%)
  starting transfers between devices  13.1 us (3%)
  local copies, waits for them, and re-layouts  11.2 us (3%)
    pallas_call x1, Pallas kernels, intro(): pl.pallas_call(functools.partial(intro_kernel, plan), in_specs=[pl.BlockS...  130 us
    pallas_call x1, Pallas kernels, feed_forward(): pl.pallas_call(functools.partial(feed_kernel, plan), grid=(ff // wide,),...  81.9 us
    pallas_call x1, Pallas kernels, attend_back(): pl.pallas_call(functools.partial(attend_back_kernel, plan), grid=(heads,)...  81.8 us
    pallas_call x1, Pallas kernels, attend(): pl.pallas_call(attend_kernel, grid_spec=pltpu.PrefetchScalarGridSpec(num_...  31.8 us
    pallas_call x1, Pallas kernels, outro(): pl.pallas_call(functools.partial(outro_kernel, plan), grid=(3,), in_specs...  29.6 us
    ppermute x2, waiting for transfers between devices, unspread(): got = [lax.ppermute(part, axes, r) for part, r in zip(parts, back_routes)]  20.4 us
    pallas_call x2, Pallas kernels, tables(): pl.pallas_call(functools.partial(table_kernel, places, unit), grid_spec=p...  12 us
    pallas_call x1, Pallas kernels, low_back(): pl.pallas_call(low_back_kernel, grid_spec=pltpu.PrefetchScalarGridSpec(nu...  9.91 us
  transfers between devices with their start and end apart: 5, of which 2 were waited for; matrix products, arithmetic and copies ran while one was open for 2% of the time, Pallas kernels for 10%

profile of v3, /device:TPU:1, one launch (start us, length us, event | category | flops | bytes accessed | tf_op | source)
XLA Modules:
  0.0 425.0 jit_solution(10101225957556642792)
XLA Ops:
  0.7 0.7 pad_add_fusion
  1.5 0.7 broadcast_in_dim.9
  2.2 1.1 copy.28
  3.3 0.2 copy.29
  3.5 0.7 fusion.1
  4.2 0.7 fusion
  5.0 0.7 dynamic-slice_reduce_fusion.info
  5.7 0.7 broadcast_in_dim.11.codes_ref
  6.3 129.5 %intro.1 = (bf16[2,392,1024]{2,1,0:T(8,128)(2,1)}, bf16[784,1024]{1,0:T(8,128)(2,1)}, bf16[2,784,1024]{2,1,0:T(8,128)(2,1)}, bf16[2,784,1024]{2,1,0:T(8,128)(2,1...) custom-call(s32[2]{0:T(128)} %dynamic-slice_reduce_fusion.info, ...), custom_call_target="tpu_custom_call" | custom-call | tf_op jit(solution)/shard_map/intro/pallas_call | solution.py:355
  135.9 1.0 dynamic-slice_bitcast_fusion
  136.9 6.0 %collective-permute-start.2 = (bf16[392,1024]{1,0:T(8,128)(2,1)}, bf16[392,1024]{1,0:T(8,128)(2,1)}, u32[]{:S(2)}, u32[]{:S(2)}) collective-permute-start(bf16[392,1024]{1,0:T(8,128)(2,1)} %get-tuple-element.94), channel_id=1, source_target_pairs={{0,1},{1,0},{2,5},{3,4},{4,3},{5,2},{6,7},{7,6},{8,9},{9,8},{10,13... | collective-permute-start | bytes 2408456 | tf_op jit(solution)/shard_map/ppermute | solution.py:980
  142.9 2.1 collective-permute-start.1
  145.0 0.7 slice_reduce_fusion.1
  145.7 0.1 reduce_max.9
  145.8 0.5 compare_convert_fusion.safe
  146.4 31.8 %attend.1 = (bf16[784,1024]{1,0:T(8,128)(2,1)}, f32[784,1024]{1,0:T(8,128)}) custom-call(s32[8]{0:T(128)} %compare_convert_fusion.safe, bf16[784,1024]{1,0:T(8,128)(2,1)} %get-tuple-element.53.q_ref, bf16[2,784,1024]{2,1,0:T(8,128)(2,1)} %get-tuple-element.54.k_ref.v_ref, bf16[2,784,1024]{2,1,0:T(8,128)(2,1)} %get-tuple-element.54.k_ref.v_ref, ...), custom_call_target="tpu_custom_call" | custom-call | tf_op jit(solution)/shard_map/attend/pallas_call | solution.py:434
  178.2 1.3 slice_bitcast_fusion
  179.5 81.9 %feed_forward.1 = (bf16[392,1024]{1,0:T(8,128)(2,1)}, bf16[392,1024]{1,0:T(8,128)(2,1)}, f32[784,1024]{1,0:T(8,128)}, bf16[784,1024]{1,0:T(8,128)(2,1)}, bf16[2,2,16,3072]{3,2,1,0:T(8,128)(2,1)}) custom-call(s32[2]{0:T(128)} %dynamic-slice_reduce_fusion.info, bf16[392,1024]{1,0:T(8,128)(2,1)} %get-tuple-element.97.xa_ref, ...), custom_call_target="tpu_custom_call" | custom-call | tf_op jit(solution)/shard_map/feed_forward/pallas_call | solution.py:622
  261.4 81.8 %attend_back.1 = (bf16[784,1024]{1,0:T(8,128)(2,1)}, bf16[2,784,1024]{2,1,0:T(8,128)(2,1)}, bf16[2,784,1024]{2,1,0:T(8,128)(2,1)}, bf16[2,392,1024]{2,1,0:T(8,128)(2,1)}, bf16[8,4,2,16,3072]{4,3,2,1,0:T(8,128)(2,1)}) custom-call(bf16[784,1024]{1,0:T(8,128)(2,1)} %get-tuple-element.53.q_ref, bf16[2,784,1024]{2,1,0:T(8,128)(2,1)} %get-tuple-element.54.k_ref.v_ref, ...), custom_call_target="tpu_custom_call" | custom-call | tf_op jit(solution)/shard_map/attend_back/pallas_call | solution.py:756
  343.2 9.9 %low_back.1 = (bf16[2,784,1024]{2,1,0:T(8,128)(2,1)}, f32[784,16]{1,0:T(8,128)}, bf16[2,2,16,1024]{3,2,1,0:T(8,128)(2,1)}) custom-call(s32[2]{0:T(128)} %dynamic-slice_reduce_fusion.info, bf16[2,392,1024]{2,1,0:T(8,128)(2,1)} %get-tuple-element.56.x_ref, f32[1,1024]{1,0:T(1,128)} %bitcast.35, bf16[784,1024]{1,0:T(8,128)(2,1)} %get-tuple-element.69.dq_ref, ...), custom_call_target="tpu_custom_call" | custom-call | tf_op jit(solution)/shard_map/low_back/pallas_call | solution.py:816
  353.1 29.6 %outro.1 = (bf16[392,1024]{1,0:T(8,128)(2,1)}, bf16[392,1024]{1,0:T(8,128)(2,1)}, bf16[8,4,2,16,1024]{4,3,2,1,0:T(8,128)(2,1)}) custom-call(s32[2]{0:T(128)} %dynamic-slice_reduce_fusion.info, bf16[2,392,1024]{2,1,0:T(8,128)(2,1)} %get-tuple-element.56.x_ref, f32[1,1024]{1,0:T(1,128)} %bitcast.36, bf16[784,1024]{1,0:T(8,128)(2,1)} %get-tuple-element.69.dq_ref, ...), custom_call_target="tpu_custom_call" | custom-call | tf_op jit(solution)/shard_map/outro/pallas_call | solution.py:891
  382.7 2.5 collective-permute-start.4
  385.2 2.5 collective-permute-start.3
  387.7 1.0 slice_reduce_fusion
  388.7 0.6 reshape_squeeze.7.owner
  389.3 7.5 %tables.3 = (f32[8,16,1024]{2,1,0:T(8,128)}, f32[8,16,1024]{2,1,0:T(8,128)}, f32[8,16,1024]{2,1,0:T(8,128)}, f32[8,16,1024]{2,1,0:T(8,128)}, f32[8,16,4096]{2,1,0:T(8,128)}, /*index=5*/f32[8,16,4096]{2,1,0:T(8,128)}) custom-call(s32[16]{0:T(128)} %reshape_squeeze.7.owner, bf16[4,2,4,2,16,3072]{5,4,3,2,1,0:T(8,128)(2,1)} %bitcast.24), custom_call_target="tpu_custom_call" | custom-call | tf_op jit(solution)/shard_map/tables/pallas_call | solution.py:940
  396.7 4.6 %tables.2 = (f32[8,16,1024]{2,1,0:T(8,128)}, f32[8,3,16,1024]{3,2,1,0:T(8,128)}) custom-call(s32[16]{0:T(128)} %reshape_squeeze.7.owner, bf16[4,2,4,2,16,1024]{5,4,3,2,1,0:T(8,128)(2,1)} %bitcast.25), custom_call_target="tpu_custom_call" | custom-call | tf_op jit(solution)/shard_map/tables/pallas_call | solution.py:940
  401.3 2.4 collective-permute-done.4
  403.7 18.0 %collective-permute-done.3 = bf16[392,1024]{1,0:T(8,128)(2,1)S(1)} collective-permute-done((bf16[392,1024]{1,0:T(8,128)(2,1)}, bf16[392,1024]{1,0:T(8,128)(2,1)S(1)}, u32[]{:S(2)}, u32[]{:S(2)}) %collective-permute-start.3) | collective-permute-done | bytes 802848 | tf_op jit(solution)/shard_map/ppermute | solution.py:984
  421.7 1.4 maximum_select_fusion
  423.1 0.6 copy-done.2
  423.6 1.2 copy.31
  (18 shorter events, 0.3 us)
Async XLA Ops:
  0.6 4.3 %copy-start.4 = (s32[2]{0:T(128)S(1)}, s32[2]{0:T(128)}, u32[]{:S(2)}) copy-start(s32[2]{0:T(128)} %param.21) | copy-start | bytes 28
  0.7 4.3 %copy-start.5 = (s32[2]{0:T(128)S(1)}, s32[2]{0:T(128)}, u32[]{:S(2)}) copy-start(s32[2]{0:T(128)} %param.20) | copy-start | bytes 28
  0.7 3.6 copy-start.3
  1.4 3.6 collective-permute-start
  5.0 130.9 %copy-start.1 = (bf16[2,392,1024]{2,1,0:T(8,128)(2,1)S(1)}, bf16[2,392,1024]{2,1,0:T(8,128)(2,1)}, u32[]{:S(2)}) copy-start(bf16[2,392,1024]{2,1,0:T(8,128)(2,1)} %param.19) | copy-start | bytes 4816900
  136.9 42.6 %collective-permute-start.2 = (bf16[392,1024]{1,0:T(8,128)(2,1)}, bf16[392,1024]{1,0:T(8,128)(2,1)}, u32[]{:S(2)}, u32[]{:S(2)}) collective-permute-start(bf16[392,1024]{1,0:T(8,128)(2,1)} %get-tuple-element.94), channel_id=1, source_target_pairs={{0,1},{1,0},{2,5},{3,4},{4,3},{5,2},{6,7},{7,6},{8,9},{9,8},{10,13... | collective-permute-start | bytes 2408456 | tf_op jit(solution)/shard_map/ppermute | solution.py:980
  142.9 36.6 %collective-permute-start.1 = (bf16[392,1024]{1,0:T(8,128)(2,1)S(1)}, bf16[392,1024]{1,0:T(8,128)(2,1)}, u32[]{:S(2)}, u32[]{:S(2)}) collective-permute-start(bf16[392,1024]{1,0:T(8,128)(2,1)S(1)} %get-tuple-element.95), channel_id=1, source_target_pairs={{0,0},{1,1},{2,4},{3,5},{4,2},{5,3},{6,6},{7,7},{8,8},{9,9},{10,12... | collective-permute-start | bytes 2408456 | tf_op jit(solution)/shard_map/ppermute | solution.py:980
  146.4 31.8 %copy-start = (bf16[2,392,1024]{2,1,0:T(8,128)(2,1)S(1)}, bf16[2,392,1024]{2,1,0:T(8,128)(2,1)}, u32[]{:S(2)}) copy-start(bf16[2,392,1024]{2,1,0:T(8,128)(2,1)} %get-tuple-element.56.x_ref) | copy-start | bytes 4816900
  382.7 21.0 %collective-permute-start.4 = (bf16[392,1024]{1,0:T(8,128)(2,1)}, bf16[392,1024]{1,0:T(8,128)(2,1)S(1)}, u32[]{:S(2)}, u32[]{:S(2)}) collective-permute-start(bf16[392,1024]{1,0:T(8,128)(2,1)} %get-tuple-element.79), channel_id=1, source_target_pairs={{1,0},{0,1},{5,2},{4,3},{3,4},{2,5},{7,6},{6,7},{9,8},{8,9},{13,10... | collective-permute-start | bytes 2408456 | tf_op jit(solution)/shard_map/ppermute | solution.py:984
  385.2 36.4 %collective-permute-start.3 = (bf16[392,1024]{1,0:T(8,128)(2,1)}, bf16[392,1024]{1,0:T(8,128)(2,1)S(1)}, u32[]{:S(2)}, u32[]{:S(2)}) collective-permute-start(bf16[392,1024]{1,0:T(8,128)(2,1)} %get-tuple-element.78), channel_id=1, source_target_pairs={{0,0},{1,1},{4,2},{5,3},{2,4},{3,5},{6,6},{7,7},{8,8},{9,9},{12,10... | collective-permute-start | bytes 2408456 | tf_op jit(solution)/shard_map/ppermute | solution.py:984
  421.7 2.0 copy-start.2

commit v4 on v3

--- a/solution.py
+++ b/solution.py
@@ -92,7 +92,9 @@
         self.local, self.zs, self.zr, self.ss, self.rs = [s.at[number] for s in sems]
         self.order, self.blocks, self.tops, self.sends, self.ids = plan.ways[order]
         self.me, self.t = lax.axis_index("dp"), lax.axis_index("tensor")
-        self.stages = [r for r in self.blocks if len(self.sends[r])]
+        passed = [r for r in self.blocks if len(self.sends[r])]
+        far = sorted({bin(r).count("1") for r in passed})
+        self.stages = [[r for r in passed if bin(r).count("1") == n] for n in far]
 
     def keep(self):
         return pltpu.make_async_copy(self.src, self.spot(self.me, self.t), self.local)
@@ -135,10 +137,10 @@
             self.across(r ^ self.order[j], j, True).wait_recv()
 
     def advance(self, stage):
-        r = self.stages[stage]
-        self.arrived(r)
-        for j in self.sends[r]:
-            self.across(r, j).start()
+        for r in self.stages[stage]:
+            self.arrived(r)
+            for j in self.sends[r]:
+                self.across(r, j).start()
 
     def finish(self):
         for r in self.blocks:
@@ -490,8 +492,9 @@
     if late:
         pl.when(step == 0)(plan.greet)
         pl.when(step == 0)(steps[0])
-        for n in range(3, len(steps) - 1):
-            pl.when(step == n - 2)(steps[n])
+        delay = known - len(items[0].stages) - 1
+        for n in range(1 if delay else 2, len(steps) - 1):
+            pl.when(step == n + delay)(steps[n])
         for n in range(parts - known):
             @pl.when(step == known + n)
             def _():
@@ -512,8 +515,6 @@
         for part, ref in enumerate((xa_ref, xb_ref)):
             s = slice(part * half, (part + 1) * half)
             mid_s[s, :] = ref[...].astype(F32) + attention[s, :]
-        if late:
-            steps[1]()
         for part, ref in enumerate((ca_ref, cb_ref)):
             s = slice(part * half, (part + 1) * half)
             gm_ref[s, :] = ref[...].astype(F32) * live
@@ -552,8 +553,8 @@
     low1, b2 = low1_s[...].astype(BF16), b2_s[...].astype(BF16)
     preact = mm(n, w1) + mm(low1, u1)
     ghid = mm_nt(gf, w2) + mm(b2, d2)
-    if late:
-        pl.when(step == 0)(steps[2])
+    if late and not delay:
+        pl.when(step == 0)(steps[1])
     hid, slope = gelu_both(preact)
     hid = hid.astype(BF16)
     gpre = (ghid * slope).astype(BF16)
@@ -673,7 +674,7 @@
     def _():
         plan.greet(route.peers)
 
-    for n, one in zip((0, 1, 3, 5, 6, 7), early[:-1]):
+    for n, one in zip((0, 1, 3, 5, 7), early[:-1]):
         @pl.when(step == n)
         def _():
             one()

time: 433 us -> 426 us (0.984)
  Pallas kernels: 377 us -> 369 us
    pallas_call x1, Pallas kernels: 81.9 us -> 77 us  [feed_forward(): pl.pallas_call(functools.partial(feed_kernel, plan), grid=(ff // wide,),...]
where the time goes in v4:
time: 426 us; the launch traced here: 418 us
  Pallas kernels  369 us (87%)
  waiting for transfers between devices  20.4 us (5%)
  starting transfers between devices  13.7 us (3%)
  local copies, waits for them, and re-layouts  11.2 us (3%)
    pallas_call x1, Pallas kernels, intro(): pl.pallas_call(functools.partial(intro_kernel, plan), in_specs=[pl.BlockS...  129 us
    pallas_call x1, Pallas kernels, attend_back(): pl.pallas_call(functools.partial(attend_back_kernel, plan), grid=(heads,)...  80 us
    pallas_call x1, Pallas kernels, feed_forward(): pl.pallas_call(functools.partial(feed_kernel, plan), grid=(ff // wide,),...  77 us
    pallas_call x1, Pallas kernels, attend(): pl.pallas_call(attend_kernel, grid_spec=pltpu.PrefetchScalarGridSpec(num_...  31.8 us
    pallas_call x1, Pallas kernels, outro(): pl.pallas_call(functools.partial(outro_kernel, plan), grid=(3,), in_specs...  28.9 us
    ppermute x2, waiting for transfers between devices, unspread(): got = [lax.ppermute(part, axes, r) for part, r in zip(parts, back_routes)]  20.4 us
    pallas_call x2, Pallas kernels, tables(): pl.pallas_call(functools.partial(table_kernel, places, unit), grid_spec=p...  12 us
    pallas_call x1, Pallas kernels, low_back(): pl.pallas_call(low_back_kernel, grid_spec=pltpu.PrefetchScalarGridSpec(nu...  9.91 us
  transfers between devices with their start and end apart: 5, of which 2 were waited for; matrix products, arithmetic and copies ran while one was open for 2% of the time, Pallas kernels for 10%

profile of v4, /device:TPU:1, one launch (start us, length us, event | category | flops | bytes accessed | tf_op | source)
XLA Modules:
  0.0 417.5 jit_solution(6302375423273288334)
XLA Ops:
  0.7 0.7 pad_add_fusion
  1.5 0.7 broadcast_in_dim.9
  2.2 1.1 copy.28
  3.3 0.2 copy.29
  3.5 0.7 fusion.1
  4.2 0.7 fusion
  5.0 0.7 dynamic-slice_reduce_fusion.info
  5.7 0.7 broadcast_in_dim.11.codes_ref
  6.3 129.0 %intro.1 = (bf16[2,392,1024]{2,1,0:T(8,128)(2,1)}, bf16[784,1024]{1,0:T(8,128)(2,1)}, bf16[2,784,1024]{2,1,0:T(8,128)(2,1)}, bf16[2,784,1024]{2,1,0:T(8,128)(2,1...) custom-call(s32[2]{0:T(128)} %dynamic-slice_reduce_fusion.info, ...), custom_call_target="tpu_custom_call" | custom-call | tf_op jit(solution)/shard_map/intro/pallas_call | solution.py:357
  135.3 1.0 dynamic-slice_bitcast_fusion
  136.4 6.7 %collective-permute-start.2 = (bf16[392,1024]{1,0:T(8,128)(2,1)}, bf16[392,1024]{1,0:T(8,128)(2,1)}, u32[]{:S(2)}, u32[]{:S(2)}) collective-permute-start(bf16[392,1024]{1,0:T(8,128)(2,1)} %get-tuple-element.94), channel_id=1, source_target_pairs={{0,1},{1,0},{2,5},{3,4},{4,3},{5,2},{6,7},{7,6},{8,9},{9,8},{10,13... | collective-permute-start | bytes 2408456 | tf_op jit(solution)/shard_map/ppermute | solution.py:981
  143.1 2.1 collective-permute-start.1
  145.2 0.7 slice_reduce_fusion.1
  146.0 0.1 reduce_max.9
  146.1 0.5 compare_convert_fusion.safe
  146.6 31.8 %attend.1 = (bf16[784,1024]{1,0:T(8,128)(2,1)}, f32[784,1024]{1,0:T(8,128)}) custom-call(s32[8]{0:T(128)} %compare_convert_fusion.safe, bf16[784,1024]{1,0:T(8,128)(2,1)} %get-tuple-element.53.q_ref, bf16[2,784,1024]{2,1,0:T(8,128)(2,1)} %get-tuple-element.54.k_ref.v_ref, bf16[2,784,1024]{2,1,0:T(8,128)(2,1)} %get-tuple-element.54.k_ref.v_ref, ...), custom_call_target="tpu_custom_call" | custom-call | tf_op jit(solution)/shard_map/attend/pallas_call | solution.py:436
  178.4 1.3 slice_bitcast_fusion
  179.7 77.0 %feed_forward.1 = (bf16[392,1024]{1,0:T(8,128)(2,1)}, bf16[392,1024]{1,0:T(8,128)(2,1)}, f32[784,1024]{1,0:T(8,128)}, bf16[784,1024]{1,0:T(8,128)(2,1)}, bf16[2,2,16,3072]{3,2,1,0:T(8,128)(2,1)}) custom-call(s32[2]{0:T(128)} %dynamic-slice_reduce_fusion.info, bf16[392,1024]{1,0:T(8,128)(2,1)} %get-tuple-element.97.xa_ref, ...), custom_call_target="tpu_custom_call" | custom-call | tf_op jit(solution)/shard_map/feed_forward/pallas_call | solution.py:623
  256.6 80.0 %attend_back.1 = (bf16[784,1024]{1,0:T(8,128)(2,1)}, bf16[2,784,1024]{2,1,0:T(8,128)(2,1)}, bf16[2,784,1024]{2,1,0:T(8,128)(2,1)}, bf16[2,392,1024]{2,1,0:T(8,128)(2,1)}, bf16[8,4,2,16,3072]{4,3,2,1,0:T(8,128)(2,1)}) custom-call(bf16[784,1024]{1,0:T(8,128)(2,1)} %get-tuple-element.53.q_ref, bf16[2,784,1024]{2,1,0:T(8,128)(2,1)} %get-tuple-element.54.k_ref.v_ref, ...), custom_call_target="tpu_custom_call" | custom-call | tf_op jit(solution)/shard_map/attend_back/pallas_call | solution.py:757
  336.6 9.9 %low_back.1 = (bf16[2,784,1024]{2,1,0:T(8,128)(2,1)}, f32[784,16]{1,0:T(8,128)}, bf16[2,2,16,1024]{3,2,1,0:T(8,128)(2,1)}) custom-call(s32[2]{0:T(128)} %dynamic-slice_reduce_fusion.info, bf16[2,392,1024]{2,1,0:T(8,128)(2,1)} %get-tuple-element.56.x_ref, f32[1,1024]{1,0:T(1,128)} %bitcast.35, bf16[784,1024]{1,0:T(8,128)(2,1)} %get-tuple-element.69.dq_ref, ...), custom_call_target="tpu_custom_call" | custom-call | tf_op jit(solution)/shard_map/low_back/pallas_call | solution.py:817
  346.5 28.9 %outro.1 = (bf16[392,1024]{1,0:T(8,128)(2,1)}, bf16[392,1024]{1,0:T(8,128)(2,1)}, bf16[8,4,2,16,1024]{4,3,2,1,0:T(8,128)(2,1)}) custom-call(s32[2]{0:T(128)} %dynamic-slice_reduce_fusion.info, bf16[2,392,1024]{2,1,0:T(8,128)(2,1)} %get-tuple-element.56.x_ref, f32[1,1024]{1,0:T(1,128)} %bitcast.36, bf16[784,1024]{1,0:T(8,128)(2,1)} %get-tuple-element.69.dq_ref, ...), custom_call_target="tpu_custom_call" | custom-call | tf_op jit(solution)/shard_map/outro/pallas_call | solution.py:892
  375.4 1.6 collective-permute-start.4
  377.1 3.2 collective-permute-start.3
  380.2 1.0 slice_reduce_fusion
  381.2 0.6 reshape_squeeze.7.owner
  381.8 7.5 %tables.3 = (f32[8,16,1024]{2,1,0:T(8,128)}, f32[8,16,1024]{2,1,0:T(8,128)}, f32[8,16,1024]{2,1,0:T(8,128)}, f32[8,16,1024]{2,1,0:T(8,128)}, f32[8,16,4096]{2,1,0:T(8,128)}, /*index=5*/f32[8,16,4096]{2,1,0:T(8,128)}) custom-call(s32[16]{0:T(128)} %reshape_squeeze.7.owner, bf16[4,2,4,2,16,3072]{5,4,3,2,1,0:T(8,128)(2,1)} %bitcast.24), custom_call_target="tpu_custom_call" | custom-call | tf_op jit(solution)/shard_map/tables/pallas_call | solution.py:941
  389.2 4.6 %tables.2 = (f32[8,16,1024]{2,1,0:T(8,128)}, f32[8,3,16,1024]{3,2,1,0:T(8,128)}) custom-call(s32[16]{0:T(128)} %reshape_squeeze.7.owner, bf16[4,2,4,2,16,1024]{5,4,3,2,1,0:T(8,128)(2,1)} %bitcast.25), custom_call_target="tpu_custom_call" | custom-call | tf_op jit(solution)/shard_map/tables/pallas_call | solution.py:941
  393.8 2.3 collective-permute-done.4
  396.1 18.1 %collective-permute-done.3 = bf16[392,1024]{1,0:T(8,128)(2,1)S(1)} collective-permute-done((bf16[392,1024]{1,0:T(8,128)(2,1)}, bf16[392,1024]{1,0:T(8,128)(2,1)S(1)}, u32[]{:S(2)}, u32[]{:S(2)}) %collective-permute-start.3) | collective-permute-done | bytes 802848 | tf_op jit(solution)/shard_map/ppermute | solution.py:985
  414.2 1.4 maximum_select_fusion
  415.6 0.6 copy-done.2
  416.1 1.2 copy.31
  (18 shorter events, 0.3 us)
Async XLA Ops:
  0.6 4.3 %copy-start.4 = (s32[2]{0:T(128)S(1)}, s32[2]{0:T(128)}, u32[]{:S(2)}) copy-start(s32[2]{0:T(128)} %param.21) | copy-start | bytes 28
  0.7 4.3 %copy-start.5 = (s32[2]{0:T(128)S(1)}, s32[2]{0:T(128)}, u32[]{:S(2)}) copy-start(s32[2]{0:T(128)} %param.20) | copy-start | bytes 28
  0.7 3.6 copy-start.3
  1.4 3.6 collective-permute-start
  5.0 130.4 %copy-start.1 = (bf16[2,392,1024]{2,1,0:T(8,128)(2,1)S(1)}, bf16[2,392,1024]{2,1,0:T(8,128)(2,1)}, u32[]{:S(2)}) copy-start(bf16[2,392,1024]{2,1,0:T(8,128)(2,1)} %param.19) | copy-start | bytes 4816900
  136.4 43.3 %collective-permute-start.2 = (bf16[392,1024]{1,0:T(8,128)(2,1)}, bf16[392,1024]{1,0:T(8,128)(2,1)}, u32[]{:S(2)}, u32[]{:S(2)}) collective-permute-start(bf16[392,1024]{1,0:T(8,128)(2,1)} %get-tuple-element.94), channel_id=1, source_target_pairs={{0,1},{1,0},{2,5},{3,4},{4,3},{5,2},{6,7},{7,6},{8,9},{9,8},{10,13... | collective-permute-start | bytes 2408456 | tf_op jit(solution)/shard_map/ppermute | solution.py:981
  143.1 36.6 %collective-permute-start.1 = (bf16[392,1024]{1,0:T(8,128)(2,1)S(1)}, bf16[392,1024]{1,0:T(8,128)(2,1)}, u32[]{:S(2)}, u32[]{:S(2)}) collective-permute-start(bf16[392,1024]{1,0:T(8,128)(2,1)S(1)} %get-tuple-element.95), channel_id=1, source_target_pairs={{0,0},{1,1},{2,4},{3,5},{4,2},{5,3},{6,6},{7,7},{8,8},{9,9},{10,12... | collective-permute-start | bytes 2408456 | tf_op jit(solution)/shard_map/ppermute | solution.py:981
  146.6 31.8 %copy-start = (bf16[2,392,1024]{2,1,0:T(8,128)(2,1)S(1)}, bf16[2,392,1024]{2,1,0:T(8,128)(2,1)}, u32[]{:S(2)}) copy-start(bf16[2,392,1024]{2,1,0:T(8,128)(2,1)} %get-tuple-element.56.x_ref) | copy-start | bytes 4816900
  375.4 20.7 %collective-permute-start.4 = (bf16[392,1024]{1,0:T(8,128)(2,1)}, bf16[392,1024]{1,0:T(8,128)(2,1)S(1)}, u32[]{:S(2)}, u32[]{:S(2)}) collective-permute-start(bf16[392,1024]{1,0:T(8,128)(2,1)} %get-tuple-element.79), channel_id=1, source_target_pairs={{1,0},{0,1},{5,2},{4,3},{3,4},{2,5},{7,6},{6,7},{9,8},{8,9},{13,10... | collective-permute-start | bytes 2408456 | tf_op jit(solution)/shard_map/ppermute | solution.py:985
  377.1 37.1 %collective-permute-start.3 = (bf16[392,1024]{1,0:T(8,128)(2,1)}, bf16[392,1024]{1,0:T(8,128)(2,1)S(1)}, u32[]{:S(2)}, u32[]{:S(2)}) collective-permute-start(bf16[392,1024]{1,0:T(8,128)(2,1)} %get-tuple-element.78), channel_id=1, source_target_pairs={{0,0},{1,1},{4,2},{5,3},{2,4},{3,5},{6,6},{7,7},{8,8},{9,9},{12,10... | collective-permute-start | bytes 2408456 | tf_op jit(solution)/shard_map/ppermute | solution.py:985
  414.2 2.0 copy-start.2

commit v5 on v4

--- a/solution.py
+++ b/solution.py
@@ -294,6 +294,8 @@
             route.start(tok_ref, x_s)
     later[1]()
     later[2]()
+    later[3]()
+    later[4]()
     route.wait(tok_ref, x_s)
     x_ref[...] = x_s[...]
     for part in range(2):
@@ -317,7 +319,8 @@
     )
     blocks = w_ref.shape[0] // 3
     for turn, j in enumerate((1, 2, 0)):
-        later[turn + 3]()
+        if turn == 1:
+            later[5]()
         for c in range(tens):
             cols = slice(c * width, (c + 1) * width)
             w = w_s[:, c, j * blocks : (j + 1) * blocks].reshape(depth, width)

time: 426 us -> 419 us (0.984)
  transfers between devices with their start and end apart: 5 -> 5, of which waited for: 2 -> 2; matrix products, arithmetic and copies ran while one was open for 2% -> 2% of each run, Pallas kernels for 10% -> 11%
where the time goes in v5:
time: 419 us; the launch traced here: 410 us
  Pallas kernels  365 us (87%)
  waiting for transfers between devices  20.4 us (5%)
  local copies, waits for them, and re-layouts  11.2 us (3%)
  starting transfers between devices  9.96 us (2%)
    pallas_call x1, Pallas kernels, intro(): pl.pallas_call(functools.partial(intro_kernel, plan), in_specs=[pl.BlockS...  126 us
    pallas_call x1, Pallas kernels, attend_back(): pl.pallas_call(functools.partial(attend_back_kernel, plan), grid=(heads,)...  80.6 us
    pallas_call x1, Pallas kernels, feed_forward(): pl.pallas_call(functools.partial(feed_kernel, plan), grid=(ff // wide,),...  76 us
    pallas_call x1, Pallas kernels, attend(): pl.pallas_call(attend_kernel, grid_spec=pltpu.PrefetchScalarGridSpec(num_...  31.8 us
    pallas_call x1, Pallas kernels, outro(): pl.pallas_call(functools.partial(outro_kernel, plan), grid=(3,), in_specs...  28.8 us
    ppermute x2, waiting for transfers between devices, unspread(): got = [lax.ppermute(part, axes, r) for part, r in zip(parts, back_routes)]  20.4 us
    pallas_call x2, Pallas kernels, tables(): pl.pallas_call(functools.partial(table_kernel, places, unit), grid_spec=p...  12 us
    pallas_call x1, Pallas kernels, low_back(): pl.pallas_call(low_back_kernel, grid_spec=pltpu.PrefetchScalarGridSpec(nu...  9.91 us
  transfers between devices with their start and end apart: 5, of which 2 were waited for; matrix products, arithmetic and copies ran while one was open for 2% of the time, Pallas kernels for 11%

profile of v5, /device:TPU:1, one launch (start us, length us, event | category | flops | bytes accessed | tf_op | source)
XLA Modules:
  0.0 410.4 jit_solution(14602439228888159667)
XLA Ops:
  0.7 0.7 pad_add_fusion
  1.5 0.7 broadcast_in_dim.9
  2.2 1.1 copy.28
  3.3 0.2 copy.29
  3.5 0.7 fusion.1
  4.2 0.7 fusion
  5.0 0.7 dynamic-slice_reduce_fusion.info
  5.7 0.7 broadcast_in_dim.11.codes_ref
  6.3 126.0 %intro.1 = (bf16[2,392,1024]{2,1,0:T(8,128)(2,1)}, bf16[784,1024]{1,0:T(8,128)(2,1)}, bf16[2,784,1024]{2,1,0:T(8,128)(2,1)}, bf16[2,784,1024]{2,1,0:T(8,128)(2,1...) custom-call(s32[2]{0:T(128)} %dynamic-slice_reduce_fusion.info, ...), custom_call_target="tpu_custom_call" | custom-call | tf_op jit(solution)/shard_map/intro/pallas_call | solution.py:360
  132.4 1.0 dynamic-slice_bitcast_fusion
  133.4 1.9 collective-permute-start.2
  135.3 3.2 collective-permute-start.1
  138.5 0.7 slice_reduce_fusion.1
  139.3 0.1 reduce_max.9
  139.4 0.5 compare_convert_fusion.safe
  139.9 31.8 %attend.1 = (bf16[784,1024]{1,0:T(8,128)(2,1)}, f32[784,1024]{1,0:T(8,128)}) custom-call(s32[8]{0:T(128)} %compare_convert_fusion.safe, bf16[784,1024]{1,0:T(8,128)(2,1)} %get-tuple-element.53.q_ref, bf16[2,784,1024]{2,1,0:T(8,128)(2,1)} %get-tuple-element.54.k_ref.v_ref, bf16[2,784,1024]{2,1,0:T(8,128)(2,1)} %get-tuple-element.54.k_ref.v_ref, ...), custom_call_target="tpu_custom_call" | custom-call | tf_op jit(solution)/shard_map/attend/pallas_call | solution.py:439
  171.7 1.3 slice_bitcast_fusion
  173.0 76.0 %feed_forward.1 = (bf16[392,1024]{1,0:T(8,128)(2,1)}, bf16[392,1024]{1,0:T(8,128)(2,1)}, f32[784,1024]{1,0:T(8,128)}, bf16[784,1024]{1,0:T(8,128)(2,1)}, bf16[2,2,16,3072]{3,2,1,0:T(8,128)(2,1)}) custom-call(s32[2]{0:T(128)} %dynamic-slice_reduce_fusion.info, bf16[392,1024]{1,0:T(8,128)(2,1)} %get-tuple-element.97.xa_ref, ...), custom_call_target="tpu_custom_call" | custom-call | tf_op jit(solution)/shard_map/feed_forward/pallas_call | solution.py:626
  249.0 80.6 %attend_back.1 = (bf16[784,1024]{1,0:T(8,128)(2,1)}, bf16[2,784,1024]{2,1,0:T(8,128)(2,1)}, bf16[2,784,1024]{2,1,0:T(8,128)(2,1)}, bf16[2,392,1024]{2,1,0:T(8,128)(2,1)}, bf16[8,4,2,16,3072]{4,3,2,1,0:T(8,128)(2,1)}) custom-call(bf16[784,1024]{1,0:T(8,128)(2,1)} %get-tuple-element.53.q_ref, bf16[2,784,1024]{2,1,0:T(8,128)(2,1)} %get-tuple-element.54.k_ref.v_ref, ...), custom_call_target="tpu_custom_call" | custom-call | tf_op jit(solution)/shard_map/attend_back/pallas_call | solution.py:760
  329.6 9.9 %low_back.1 = (bf16[2,784,1024]{2,1,0:T(8,128)(2,1)}, f32[784,16]{1,0:T(8,128)}, bf16[2,2,16,1024]{3,2,1,0:T(8,128)(2,1)}) custom-call(s32[2]{0:T(128)} %dynamic-slice_reduce_fusion.info, bf16[2,392,1024]{2,1,0:T(8,128)(2,1)} %get-tuple-element.56.x_ref, f32[1,1024]{1,0:T(1,128)} %bitcast.35, bf16[784,1024]{1,0:T(8,128)(2,1)} %get-tuple-element.69.dq_ref, ...), custom_call_target="tpu_custom_call" | custom-call | tf_op jit(solution)/shard_map/low_back/pallas_call | solution.py:820
  339.5 28.8 %outro.1 = (bf16[392,1024]{1,0:T(8,128)(2,1)}, bf16[392,1024]{1,0:T(8,128)(2,1)}, bf16[8,4,2,16,1024]{4,3,2,1,0:T(8,128)(2,1)}) custom-call(s32[2]{0:T(128)} %dynamic-slice_reduce_fusion.info, bf16[2,392,1024]{2,1,0:T(8,128)(2,1)} %get-tuple-element.56.x_ref, f32[1,1024]{1,0:T(1,128)} %bitcast.36, bf16[784,1024]{1,0:T(8,128)(2,1)} %get-tuple-element.69.dq_ref, ...), custom_call_target="tpu_custom_call" | custom-call | tf_op jit(solution)/shard_map/outro/pallas_call | solution.py:895
  368.3 1.7 collective-permute-start.4
  369.9 3.2 collective-permute-start.3
  373.1 1.0 slice_reduce_fusion
  374.1 0.6 reshape_squeeze.7.owner
  374.7 7.5 %tables.3 = (f32[8,16,1024]{2,1,0:T(8,128)}, f32[8,16,1024]{2,1,0:T(8,128)}, f32[8,16,1024]{2,1,0:T(8,128)}, f32[8,16,1024]{2,1,0:T(8,128)}, f32[8,16,4096]{2,1,0:T(8,128)}, /*index=5*/f32[8,16,4096]{2,1,0:T(8,128)}) custom-call(s32[16]{0:T(128)} %reshape_squeeze.7.owner, bf16[4,2,4,2,16,3072]{5,4,3,2,1,0:T(8,128)(2,1)} %bitcast.24), custom_call_target="tpu_custom_call" | custom-call | tf_op jit(solution)/shard_map/tables/pallas_call | solution.py:944
  382.1 4.6 %tables.2 = (f32[8,16,1024]{2,1,0:T(8,128)}, f32[8,3,16,1024]{3,2,1,0:T(8,128)}) custom-call(s32[16]{0:T(128)} %reshape_squeeze.7.owner, bf16[4,2,4,2,16,1024]{5,4,3,2,1,0:T(8,128)(2,1)} %bitcast.25), custom_call_target="tpu_custom_call" | custom-call | tf_op jit(solution)/shard_map/tables/pallas_call | solution.py:944
  386.7 2.3 collective-permute-done.4
  389.0 18.1 %collective-permute-done.3 = bf16[392,1024]{1,0:T(8,128)(2,1)S(1)} collective-permute-done((bf16[392,1024]{1,0:T(8,128)(2,1)}, bf16[392,1024]{1,0:T(8,128)(2,1)S(1)}, u32[]{:S(2)}, u32[]{:S(2)}) %collective-permute-start.3) | collective-permute-done | bytes 802848 | tf_op jit(solution)/shard_map/ppermute | solution.py:988
  407.1 1.4 maximum_select_fusion
  408.5 0.6 copy-done.2
  409.0 1.2 copy.31
  (18 shorter events, 0.3 us)
Async XLA Ops:
  0.6 4.3 %copy-start.4 = (s32[2]{0:T(128)S(1)}, s32[2]{0:T(128)}, u32[]{:S(2)}) copy-start(s32[2]{0:T(128)} %param.21) | copy-start | bytes 28
  0.7 4.3 %copy-start.5 = (s32[2]{0:T(128)S(1)}, s32[2]{0:T(128)}, u32[]{:S(2)}) copy-start(s32[2]{0:T(128)} %param.20) | copy-start | bytes 28
  0.7 3.6 copy-start.3
  1.4 3.6 collective-permute-start
  5.0 127.4 %copy-start.1 = (bf16[2,392,1024]{2,1,0:T(8,128)(2,1)S(1)}, bf16[2,392,1024]{2,1,0:T(8,128)(2,1)}, u32[]{:S(2)}) copy-start(bf16[2,392,1024]{2,1,0:T(8,128)(2,1)} %param.19) | copy-start | bytes 4816900
  133.4 39.6 %collective-permute-start.2 = (bf16[392,1024]{1,0:T(8,128)(2,1)}, bf16[392,1024]{1,0:T(8,128)(2,1)}, u32[]{:S(2)}, u32[]{:S(2)}) collective-permute-start(bf16[392,1024]{1,0:T(8,128)(2,1)} %get-tuple-element.94), channel_id=1, source_target_pairs={{0,1},{1,0},{2,5},{3,4},{4,3},{5,2},{6,7},{7,6},{8,9},{9,8},{10,13... | collective-permute-start | bytes 2408456 | tf_op jit(solution)/shard_map/ppermute | solution.py:984
  135.3 37.7 %collective-permute-start.1 = (bf16[392,1024]{1,0:T(8,128)(2,1)S(1)}, bf16[392,1024]{1,0:T(8,128)(2,1)}, u32[]{:S(2)}, u32[]{:S(2)}) collective-permute-start(bf16[392,1024]{1,0:T(8,128)(2,1)S(1)} %get-tuple-element.95), channel_id=1, source_target_pairs={{0,0},{1,1},{2,4},{3,5},{4,2},{5,3},{6,6},{7,7},{8,8},{9,9},{10,12... | collective-permute-start | bytes 2408456 | tf_op jit(solution)/shard_map/ppermute | solution.py:984
  139.9 31.8 %copy-start = (bf16[2,392,1024]{2,1,0:T(8,128)(2,1)S(1)}, bf16[2,392,1024]{2,1,0:T(8,128)(2,1)}, u32[]{:S(2)}) copy-start(bf16[2,392,1024]{2,1,0:T(8,128)(2,1)} %get-tuple-element.56.x_ref) | copy-start | bytes 4816900
  368.3 20.7 %collective-permute-start.4 = (bf16[392,1024]{1,0:T(8,128)(2,1)}, bf16[392,1024]{1,0:T(8,128)(2,1)S(1)}, u32[]{:S(2)}, u32[]{:S(2)}) collective-permute-start(bf16[392,1024]{1,0:T(8,128)(2,1)} %get-tuple-element.79), channel_id=1, source_target_pairs={{1,0},{0,1},{5,2},{4,3},{3,4},{2,5},{7,6},{6,7},{9,8},{8,9},{13,10... | collective-permute-start | bytes 2408456 | tf_op jit(solution)/shard_map/ppermute | solution.py:988
  369.9 37.1 %collective-permute-start.3 = (bf16[392,1024]{1,0:T(8,128)(2,1)}, bf16[392,1024]{1,0:T(8,128)(2,1)S(1)}, u32[]{:S(2)}, u32[]{:S(2)}) collective-permute-start(bf16[392,1024]{1,0:T(8,128)(2,1)} %get-tuple-element.78), channel_id=1, source_target_pairs={{0,0},{1,1},{4,2},{5,3},{2,4},{3,5},{6,6},{7,7},{8,8},{9,9},{12,10... | collective-permute-start | bytes 2408456 | tf_op jit(solution)/shard_map/ppermute | solution.py:988
  407.1 2.0 copy-start.2
